TPU v7x, 32 devices: a whole 2x2x4 slice. The times are simulated.
32 devices in a mesh: row: 8 (over z, core), col: 4 (over y, x).
Axes of the slice: x: 2, y: 2, z: 4, core: 2. Of those that a mesh axis runs over, the one named last changes fastest.
Arguments:
- panels: bfloat16 [256, 32, 256], P(('row', 'col')), may hold values from -21 to 21
- tiles: bfloat16 [1536, 256, 512], P(('row', 'col')), may hold values from -0.109375 to 0.109375
- tile_dst: int32 [1536], P(('row', 'col')), may hold values from 0 to 7
- tile_src: int32 [1536], P(('row', 'col')), may hold values from 0 to 63
- geometry: float32 [256, 6, 256], P(('row', 'col')), may hold values from -5 to 5
- areas: float32 [256, 256], P(('row', 'col')), may hold values from 0.25 to 2
- block_owner: int32 [256, 1], P(('row', 'col')), may hold values from 0 to 3; in each aligned block of 8 rows (0 to 7, 8 to 15, ...) at most 2 rows name the same one
- block_slot: int32 [256], P(('row', 'col')), may hold values from 0 to 3
Outputs:
- field: float32 [256, 32, 256], P(('row', 'col'))
- shape_gradient: float32 [256, 256], P(('row', 'col'))
Inputs may be any that keep to these rules, and one draw needn't show every extreme that they name: Among the blocks of one device at most 2 have the same block_owner, and some device reaches 2.
All inputs are finite; a program needn't handle non-finite values.
Results may differ from a plain program's by a relative error of at most 0.0003.
Values may be sent and summed in bfloat16 or wider, within the bound.
No kernel may reach another device: no remote copies, remote signals or barrier semaphores. Data moves between devices by JAX's collectives and lax.ppermute only.
A program may use at most 64 MiB of HBM per device.

v0:
```python
import jax
import jax.numpy as jnp
from jax import lax
from jax.sharding import PartitionSpec as P

PD = 4


EPSILON = 1e-05


def make_basis(geometry, areas):
    normal = geometry[:, 0:3]
    place = geometry[:, 3:6]
    twist = jnp.stack(
        [
            place[:, 1] * normal[:, 2] - place[:, 2] * normal[:, 1],
            place[:, 2] * normal[:, 0] - place[:, 0] * normal[:, 2],
            place[:, 0] * normal[:, 1] - place[:, 1] * normal[:, 0],
        ],
        axis=1,
    )
    weight = areas[:, None, :]
    return jnp.concatenate([weight * normal, weight * twist, weight, weight], axis=1)


def split_complex(images, freq_count, node_count):
    real_part = images[:, :freq_count, :node_count] - images[:, freq_count:, node_count:]
    imag_part = images[:, :freq_count, node_count:] + images[:, freq_count:, :node_count]
    return jnp.concatenate([real_part, imag_part], axis=1)


def normalize(totals):
    return totals * lax.rsqrt(jnp.mean(totals * totals, axis=1, keepdims=True) + EPSILON)


def shards(panels, tiles, tile_dst, tile_src, geometry, areas, block_owner, block_slot):
    precise = lax.Precision.HIGHEST
    block_count, rows_twice, node_count = panels.shape
    freq_count = rows_twice // 2
    tile_count = tiles.shape[0]
    flat_panels = panels.reshape(block_count, rows_twice * node_count)
    gathered = lax.all_gather(flat_panels, "row", axis=0, tiled=True)
    count = gathered.shape[0]
    picking = (tile_src[:, None] == jnp.arange(count, dtype=jnp.int32)[None, :]).astype(
        jnp.bfloat16
    )
    picked = jnp.dot(picking, gathered, preferred_element_type=jnp.float32)
    chosen = picked.astype(jnp.bfloat16).reshape(tile_count, rows_twice, node_count)
    images = jnp.einsum("tjn,tnm->tjm", chosen, tiles, preferred_element_type=jnp.float32)
    tile_terms = split_complex(images, freq_count, node_count)
    target = (tile_dst[None, :] == jnp.arange(block_count, dtype=jnp.int32)[:, None]).astype(
        jnp.float32
    )
    near = jnp.einsum("dt,tjn->djn", target, tile_terms, precision=precise)
    incident = panels.astype(jnp.float32)
    field = 0.5 * incident + near
    power = field[:, :freq_count] ** 2 + field[:, freq_count:] ** 2
    cross_power = (
        incident[:, :freq_count] * field[:, :freq_count]
        + incident[:, freq_count:] * field[:, freq_count:]
    )
    basis = make_basis(geometry, areas)
    first_moments = jnp.einsum("bkn,bfn->bkf", basis[:, :7], power, precision=precise)
    last_moment = jnp.einsum("bn,bfn->bf", basis[:, 7], cross_power, precision=precise)
    moments = jnp.concatenate([first_moments, last_moment[:, None, :]], axis=1).reshape(
        block_count, -1
    )
    group_count = lax.axis_size("col")
    owner = block_owner[:, 0]
    local_particle = owner * PD + block_slot
    particle_index = jnp.arange(group_count * PD, dtype=jnp.int32)
    table_map = (particle_index[:, None] == local_particle[None, :]).astype(jnp.float32)
    table = jnp.dot(table_map, moments, precision=precise)
    totals = lax.psum(table, "col")
    adjoint = normalize(totals)
    block_adjoint = jnp.dot(table_map.T, adjoint, precision=precise)
    shaped = block_adjoint.reshape(block_count, 8, freq_count)
    first_terms = jnp.einsum("bkf,bfn->bkn", shaped[:, :7], power, precision=precise)
    last_term = jnp.einsum("bf,bfn->bn", shaped[:, 7], cross_power, precision=precise)
    shape_gradient = (
        jnp.sum(basis[:, :7] * first_terms, axis=1) + basis[:, 7] * last_term
    ) / freq_count
    return (field, shape_gradient)


def solution(mesh):
    in_specs = (
        P(("row", "col"), None, None),
        P(("row", "col"), None, None),
        P(("row", "col")),
        P(("row", "col")),
        P(("row", "col"), None, None),
        P(("row", "col"), None),
        P(("row", "col"), None),
        P(("row", "col")),
    )
    out_specs = (P(("row", "col"), None, None), P(("row", "col"), None))
    return jax.shard_map(shards, mesh=mesh, in_specs=in_specs, out_specs=out_specs, check_vma=False)
```

profile of v0, /device:TPU:0, one launch (start us, length us, event | category | flops | bytes accessed | tf_op | source)
XLA Modules:
  0.0 66.3 jit_solution(11579135535735351693)
XLA Ops:
  7.2 0.0 all-gather.2.cloned.1.call-start
  7.2 1.6 %copy.35 = bf16[1,8,32,256]{3,1,2,0:T(8,128)(2,1)} copy(bf16[1,8,32,256]{3,2,1,0:T(8,128)(2,1)} %bitcast.33) | data formatting | bytes 262144
  8.8 0.0 all-gather.2.cloned.1.call-update
  8.9 0.7 %broadcast_in_dim.4 = f32[8,1,256]{2,1,0:T(1,128)S(1)} reshape(f32[8,256]{1,0:T(8,128)} %param.13) | data formatting | bytes 16384 | tf_op jit(solution)/shard_map/broadcast_in_dim | solution.py:23
  9.6 0.7 %slice.73 = f32[8,3,256]{2,0,1:T(8,128)S(1)} slice(f32[8,6,256]{2,0,1:T(8,128)} %param.12), slice={[0:8], [0:3], [0:256]} | slice | bytes 49152 | tf_op jit(solution)/shard_map/slice | solution.py:13
  10.3 0.7 %bitcast_add_fusion = s32[8]{0:T(128)S(1)} fusion(s32[8]{0:T(128)} %param.15, s32[8,1]{0,1:T(1,128)} %param.14), kind=kLoop, calls=%fused_computation.47 | loop fusion | flops 16 | bytes 96 | tf_op jit(solution)/shard_map/add | solution.py:71
  11.0 0.8 %fusion.29 = (f32[8,1,256]{2,0,1:T(8,128)S(1)}, f32[8,1,256]{2,0,1:T(8,128)S(1)}, f32[8,1,256]{2,0,1:T(8,128)S(1)}, f32[8,1,256]{2,0,1:T(8,128)S(1)}, f32[8,1,256]{2,0,1:T(8,128)S(1)}, /*index=5*/f32[8,1,256]{2,0,1:T(8,128)S(1)}) fusion(f32[8,6,256]{2,0,1:T(8,128)} %param.12), kind=kLoop, calls=%fused_computation.50 | loop fusion | bytes 98304 | tf_op jit(solution)/shard_map/slice | solution.py:17
  11.8 0.7 %copy_multiply_fusion = (f32[8,3,256]{2,1,0:T(4,128)S(1)}, f32[8,3,256]{2,1,0:T(4,128)S(1)}) fusion(f32[8,3,256]{2,0,1:T(8,128)S(1)} %slice.73, f32[8,256]{1,0:T(8,128)} %param.13, f32[8,1,256]{2,1,0:T(1,128)S(1)} %get-tuple-element.16, f32[8,1,256]{2,1,0:T(1,128)S(1)} %get-tuple-element.15, f32[8,1,256]{2,1,0:T(1,128)S(1)} %get-tuple-element.14), kind=kLoop, calls=%fused_computation.25 | loop fusion | flops 24576 | bytes 106496 | tf_op jit(solution)/shard_map/mul | solution.py:24
  12.6 1.0 %copy_convert_fusion = f32[8,32,256]{2,0,1:T(8,128)S(1)} fusion(bf16[8,32,256]{2,1,0:T(8,128)(2,1)} %param.8), kind=kLoop, calls=%fused_computation.12 | loop fusion | flops 65536 | bytes 393216 | tf_op jit(solution)/shard_map/convert_element_type | solution.py:56
  13.6 21.4 %all-gather.2.cloned.1.call-done = bf16[64,8192]{1,0:T(8,128)(2,1)} async-done(((bf16[8,8192]{1,0:T(8,128)(2,1)}), bf16[64,8192]{1,0:T(8,128)(2,1)}) %all-gather.2.cloned.1.call-update) | async-done | bytes 1048592 | tf_op jit(solution)/shard_map/all_gather | solution.py:43
  35.0 1.6 %convolution_convert_fusion = bf16[48,8192]{1,0:T(8,128)(2,1)S(1)} fusion(bf16[64,8192]{1,0:T(8,128)(2,1)} %all-gather.2.cloned.1.call-done, s32[48]{0:T(128)} %param.11), kind=kOutput, calls=%fused_computation | convolution fusion | flops 50727936 | bytes 1835200 | tf_op jit(solution)/shard_map/dot_general | solution.py:48
  36.7 0.2 copy.36
  36.8 6.8 %fusion.30 = f32[48,32,512]{2,1,0:T(8,128)S(1)} fusion(bf16[48,32,256]{2,1,0:T(8,128)(2,1)S(1)} %bitcast.31, bf16[48,256,512]{2,1,0:T(8,128)(2,1)} %param.9), kind=kOutput, calls=%fused_computation.51 | convolution fusion | flops 402653184 | bytes 16515072 | tf_op jit(solution)/shard_map/tjn,tnm->tjm/dot_general | solution.py:50
  43.7 0.3 slice_subtract_fusion
  44.0 0.0 copy-start
  44.0 0.0 copy-start.2
  44.0 0.1 pad_maximum_fusion
  44.1 0.7 %copy-done = bf16[8,32,256]{2,1,0:T(8,128)(2,1)S(1)} copy-done((bf16[8,32,256]{2,1,0:T(8,128)(2,1)S(1)}, bf16[8,32,256]{2,1,0:T(8,128)(2,1)}, u32[]{:S(2)}) %copy-start) | copy-done | bytes 131096
  44.9 1.5 %fusion.2 = f32[8,32,256]{2,0,1:T(8,128)S(1)} fusion(f32[48,32,256]{2,1,0:T(8,128)S(1)} %pad_maximum_fusion, bf16[8,32,256]{2,1,0:T(8,128)(2,1)S(1)} %copy-done, s32[48]{0:T(128)S(1)} %copy-done.2), kind=kOutput, calls=%fused_computation.4 | convolution fusion | flops 37945728 | bytes 1966272 | tf_op jit(solution)/shard_map/dt,tjn->djn/dot_general | solution.py:55
  46.4 0.8 %copy.22 = f32[8,32,256]{2,1,0:T(8,128)} copy(f32[8,32,256]{2,0,1:T(8,128)S(1)} %fusion.2) | data formatting | bytes 524288
  47.2 0.0 copy-done.1
  47.2 0.3 fusion.9
  47.5 0.3 fusion.12
  47.8 0.1 reshape.32
  47.9 0.1 fusion.21
  48.0 10.0 %psum.7 = f32[16,128]{1,0:T(8,128)S(1)} all-reduce(f32[16,128]{1,0:T(8,128)S(1)} %fusion.21), channel_id=1, replica_groups=mesh['row'=8,'col'=4] {'col'}, use_global_device_ids=true, to_apply=%region_0.0 | all-reduce | flops 2048 | bytes 16384 | tf_op jit(solution)/shard_map/psum | solution.py:75
  58.0 0.1 multiply_reduce_fusion
  58.1 0.2 fusion.19
  58.3 0.1 reshape.33
  58.4 0.3 fusion.5
  58.6 0.2 fusion.7
  58.9 0.6 fusion.17
  (6 shorter events, 0.1 us)
Async XLA Ops:
  7.2 27.8 %all-gather.2.cloned.1.call-start = ((), (), s32[]{:S(2)}) async-start(), calls=%async_computation | async-start | bytes 1179648 | tf_op jit(solution)/shard_map/all_gather | solution.py:43
  44.0 0.9 %copy-start = (bf16[8,32,256]{2,1,0:T(8,128)(2,1)S(1)}, bf16[8,32,256]{2,1,0:T(8,128)(2,1)}, u32[]{:S(2)}) copy-start(bf16[8,32,256]{2,1,0:T(8,128)(2,1)} %param.8) | copy-start | bytes 393220
  44.0 0.9 %copy-start.2 = (s32[48]{0:T(128)S(1)}, s32[48]{0:T(128)}, u32[]{:S(2)}) copy-start(s32[48]{0:T(128)} %param.10) | copy-start | bytes 580
  44.9 2.3 %copy-start.1 = (f32[8,256]{1,0:T(8,128)S(1)}, f32[8,256]{1,0:T(8,128)}, u32[]{:S(2)}) copy-start(f32[8,256]{1,0:T(8,128)} %param.13) | copy-start | bytes 24580
Sparse Core Ops, SparseCore 0:
  10.2 24.7 all-gather.1
where the time goes:
time: 66.8 us; the launch traced here: 66.3 us
  waiting for transfers between devices  21.5 us (32%)
  between operations  14.1 us (21%)
  matrix products  11.3 us (17%)
  blocking collectives  9.96 us (15%)
  local copies, waits for them, and re-layouts  5.73 us (9%)
  other arithmetic  3.65 us (5%)
    all_gather x1, waiting for transfers between devices, shards(): gathered = lax.all_gather(flat_panels, 'row', axis=0, tiled=True)  21.4 us
    psum x1, blocking collectives, shards(): totals = lax.psum(table, 'col')  9.96 us
    dot_general x1, matrix products, shards(): jnp.einsum('tjn,tnm->tjm', chosen, tiles, preferred_element_type=jnp.floa...  6.83 us
    unnamed x9, local copies, waits for them, and re-layouts  3.35 us
    dot_general x1, matrix products, shards(): picked = jnp.dot(picking, gathered, preferred_element_type=jnp.float32)  1.64 us
    dot_general x1, matrix products, shards(): near = jnp.einsum('dt,tjn->djn', target, tile_terms, precision=precise)  1.51 us
  transfers between devices with their start and end apart: 1, of which 1 were waited for; matrix products, arithmetic and copies ran while one was open for 7% of the time, Pallas kernels for 0%

commit v1 on v0

v1 whole, which is shorter than its diff:
```python
import functools

import jax
import jax.numpy as jnp
from jax import lax
from jax.experimental import pallas as pl
from jax.experimental.pallas import tpu as pltpu
from jax.sharding import PartitionSpec as P

PD = 4
EPSILON = 1e-05
UNROLL = 4
COPIES = 8
MOMENTS = 8
F32 = jnp.float32
BF16 = jnp.bfloat16
VMEM_LIMIT = 28 << 20

VMEM_SPEC = pl.BlockSpec(memory_space=pltpu.VMEM)
SMEM_SPEC = pl.BlockSpec(memory_space=pltpu.SMEM)
ANY_SPEC = pl.BlockSpec(memory_space=pl.ANY)


def params():
    return pltpu.CompilerParams(vmem_limit_bytes=VMEM_LIMIT)


def parts_of(values, count):
    parts = []
    for _ in range(count - 1):
        part = values.astype(BF16)
        parts.append(part)
        values = values - part.astype(F32)
    parts.append(values.astype(BF16))
    return parts


def dot(left, right, transposed=False):
    axes = (((1,), (1 if transposed else 0,)), ((), ()))
    return lax.dot_general(left, right, axes, preferred_element_type=F32)


def dot_near_exact(left, right, transposed=False):
    left_high, left_low = parts_of(left, 2)
    right_high, right_low = parts_of(right, 2)
    return dot(left_high, right_high, transposed) + (
        dot(left_high, right_low, transposed) + dot(left_low, right_high, transposed)
    )


def block_mask(block_count, freq_count):
    shape = (block_count, block_count * freq_count)
    rows = lax.broadcasted_iota(jnp.int32, shape, 0)
    columns = lax.broadcasted_iota(jnp.int32, shape, 1)
    return (columns // freq_count == rows).astype(F32)


def fill_panels(sources, held):
    depth = sources[0].shape[0]
    for index, source in enumerate(sources):
        held[index * depth : (index + 1) * depth] = source[...]
    held[len(sources) * depth] = jnp.zeros(held.shape[1:], held.dtype)


def add_stage(stage, width, plan, held, tiles, total):
    def body(step, carry):
        base = step * UNROLL
        images = [
            dot(held[plan[width + base + lane]], tiles[plan[base + lane]])
            for lane in range(UNROLL)
        ]
        for lane in range(UNROLL):
            target = plan[2 * width + base + lane]
            total[target] += images[lane]
        return carry

    lax.fori_loop(plan[3 * width + stage], plan[3 * width + stage + 1], body, 0)


def first_kernel(bounds, width, src, dst, panels, tiles, held_tiles, total, plan, held, sems):
    tile_count = tiles.shape[0]
    depth = panels.shape[0]
    per_copy = tile_count // COPIES
    copies = [
        pltpu.make_async_copy(
            tiles.at[pl.ds(i * per_copy, per_copy)],
            held_tiles.at[pl.ds(i * per_copy, per_copy)],
            sems.at[i],
        )
        for i in range(COPIES)
    ]
    for copy in copies:
        copy.start()
    me = lax.axis_index("row")
    position = jnp.int32(0)
    for stage in range(len(bounds) - 1):
        low, high = bounds[stage], bounds[stage + 1]
        plan[3 * width + stage] = position // UNROLL

        def place(t, position, low=low, high=high):
            source = src[t]
            hop = (source // depth) ^ me
            plan[position] = t
            plan[width + position] = (hop - low) * depth + source % depth
            plan[2 * width + position] = dst[t]
            return position + ((hop >= low) & (hop < high)).astype(jnp.int32)

        position = lax.fori_loop(0, tile_count, place, position)
        for lane in range(UNROLL):
            plan[position + lane] = 0
            plan[width + position + lane] = (high - low) * depth
            plan[2 * width + position + lane] = 0
        position = (position + UNROLL - 1) // UNROLL * UNROLL
    plan[3 * width + len(bounds) - 1] = position // UNROLL
    total[...] = jnp.zeros_like(total)
    fill_panels([panels], held)
    for copy in copies:
        copy.wait()
    add_stage(0, width, plan, held, held_tiles, total)


def middle_kernel(width, count, plan, owner, slot, *refs):
    sources = refs[:count]
    tiles, start, place, areas, total, basis, spread, held = refs[count:]
    block_count = areas.shape[0]
    fill_panels(sources, held)
    total[...] = start[...]
    nx, ny, nz, px, py, pz = [place[i] for i in range(6)]
    weight = areas[...]
    rows = [nx, ny, nz, py * nz - pz * ny, pz * nx - px * nz, px * ny - py * nx]
    for index, row in enumerate(rows):
        basis[index * block_count : (index + 1) * block_count] = weight * row
    for index in range(len(rows), MOMENTS):
        basis[index * block_count : (index + 1) * block_count] = weight
    freq_count = spread.shape[0] // block_count
    shape = (freq_count, spread.shape[1])
    lanes = lax.broadcasted_iota(jnp.int32, shape, 1)
    same = lanes % freq_count == lax.broadcasted_iota(jnp.int32, shape, 0)
    for block in range(block_count):
        particle = owner[block] * PD + slot[block]
        chosen = same & (lanes // freq_count == particle)
        spread[block * freq_count : (block + 1) * freq_count] = jnp.where(
            chosen, 1.0, 0.0
        ).astype(BF16)
    add_stage(1, width, plan, held, tiles, total)


def field_kernel(width, count, plan, *refs):
    sources = refs[:count]
    panels, tiles, start, basis, spread = refs[count : count + 5]
    field, table, powers, crosses, held, total = refs[count + 5 :]
    block_count, rows_twice, node_count = panels.shape
    freq_count = rows_twice // 2
    fill_panels(sources, held)
    total[...] = start[...]
    add_stage(2, width, plan, held, tiles, total)
    for block in range(block_count):
        image = total[block]
        incident = panels[block].astype(F32)
        real_in, imag_in = incident[:freq_count], incident[freq_count:]
        real = 0.5 * real_in + (
            image[:freq_count, :node_count] - image[freq_count:, node_count:]
        )
        imag = 0.5 * imag_in + (
            image[:freq_count, node_count:] + image[freq_count:, :node_count]
        )
        field[block, :freq_count] = real
        field[block, freq_count:] = imag
        span = slice(block * freq_count, (block + 1) * freq_count)
        powers[span] = real * real + imag * imag
        crosses[span] = real_in * real + imag_in * imag
    last = (MOMENTS - 1) * block_count
    first_moments = dot_near_exact(basis[:last], powers[...], True)
    last_moment = dot_near_exact(basis[last:], crosses[...], True)
    mask = block_mask(block_count, freq_count)
    pieces = [
        jnp.sum(mask * first_moments[k * block_count : (k + 1) * block_count], axis=0, keepdims=True)
        for k in range(MOMENTS - 1)
    ]
    pieces.append(jnp.sum(mask * last_moment, axis=0, keepdims=True))
    moments = jnp.concatenate(pieces, axis=0)
    joined = dot(jnp.concatenate(parts_of(moments, 3), axis=0), spread[...])
    table[...] = joined[:MOMENTS] + (joined[MOMENTS : 2 * MOMENTS] + joined[2 * MOMENTS :])


def gradient_kernel(count, *refs):
    tables = refs[:count]
    basis, spread, powers, crosses, gradient = refs[count:]
    block_count = gradient.shape[0]
    freq_count = powers.shape[0] // block_count
    summed = tables[0][...]
    for table in tables[1:]:
        summed = summed + table[...]
    joined = dot(jnp.concatenate(parts_of(summed, 3), axis=0), spread[...], True)
    totals = joined[:MOMENTS] + (joined[MOMENTS : 2 * MOMENTS] + joined[2 * MOMENTS :])
    mask = block_mask(block_count, freq_count)
    squares = jnp.sum(totals * totals, axis=0, keepdims=True)
    mean = jnp.sum(mask * squares, axis=1, keepdims=True) / (MOMENTS * freq_count)
    scale = lax.rsqrt(mean + EPSILON) / freq_count
    spots = [mask * totals[k : k + 1] for k in range(MOMENTS)]
    first_terms = dot_near_exact(jnp.concatenate(spots[:-1], axis=0), powers[...])
    last_term = dot_near_exact(spots[-1], crosses[...])
    result = basis[(MOMENTS - 1) * block_count :] * last_term
    for k in range(MOMENTS - 1):
        span = slice(k * block_count, (k + 1) * block_count)
        result = result + basis[span] * first_terms[span]
    gradient[...] = result * scale


def exchange(values, axis, hop):
    pairs = [(i, i ^ hop) for i in range(lax.axis_size(axis))]
    return lax.ppermute(values, axis, pairs)


def shards(panels, tiles, tile_dst, tile_src, geometry, areas, block_owner, block_slot):
    block_count, rows_twice, node_count = panels.shape
    freq_count = rows_twice // 2
    tile_count = tiles.shape[0]
    row_count = lax.axis_size("row")
    group_count = lax.axis_size("col")
    particle_count = group_count * PD
    bounds = (0, 1, row_count - 2, row_count)
    width = -(-(tile_count + 4 * UNROLL) // 128) * 128
    image_shape = (block_count, rows_twice, 2 * node_count)

    def held(count):
        return pltpu.VMEM((count * block_count + 1, rows_twice, node_count), BF16)

    hops = {0: panels}
    for hop in [row_count - 2, *range(row_count - 4, 0, -2)]:
        hops[hop] = exchange(panels, "row", hop)
    hops[1] = exchange(panels, "row", 1)
    for hop in range(2, row_count, 2):
        hops[hop + 1] = exchange(hops[hop], "row", 1)

    held_tiles, early, plan = pl.pallas_call(
        functools.partial(first_kernel, bounds, width),
        out_shape=(
            pltpu.VMEM(tiles.shape, tiles.dtype),
            pltpu.VMEM(image_shape, F32),
            jax.ShapeDtypeStruct((3 * width + 128,), jnp.int32),
        ),
        in_specs=[SMEM_SPEC, SMEM_SPEC, VMEM_SPEC, ANY_SPEC],
        out_specs=(VMEM_SPEC, VMEM_SPEC, SMEM_SPEC),
        scratch_shapes=[held(1), pltpu.SemaphoreType.DMA((COPIES,))],
        compiler_params=params(),
        cost_estimate=pl.CostEstimate(
            flops=0, bytes_accessed=2 * tiles.size * 2, transcendentals=0
        ),
        name="first_stage",
    )(tile_src, tile_dst, panels, tiles)

    middle = [hops[j] for j in range(bounds[1], bounds[2])]
    basis_shape = (MOMENTS * block_count, node_count)
    spread_shape = (block_count * freq_count, particle_count * freq_count)
    power_shape = (block_count * freq_count, node_count)
    table_shape = (MOMENTS, particle_count * freq_count)
    partial_field, basis, spread = pl.pallas_call(
        functools.partial(middle_kernel, width, len(middle)),
        out_shape=(
            pltpu.VMEM(image_shape, F32),
            pltpu.VMEM(basis_shape, F32),
            pltpu.VMEM(spread_shape, BF16),
        ),
        in_specs=[SMEM_SPEC] * 3 + [VMEM_SPEC] * (len(middle) + 4),
        out_specs=(VMEM_SPEC,) * 3,
        scratch_shapes=[held(len(middle))],
        compiler_params=params(),
        name="middle_stage",
    )(
        plan,
        block_owner[:, 0],
        block_slot,
        *middle,
        held_tiles,
        early,
        jnp.transpose(geometry, (1, 0, 2)),
        areas,
    )

    late = [hops[j] for j in range(bounds[2], bounds[3])]
    field, table, powers, crosses = pl.pallas_call(
        functools.partial(field_kernel, width, len(late)),
        out_shape=(
            jax.ShapeDtypeStruct(panels.shape, F32),
            pltpu.VMEM(table_shape, F32),
            pltpu.VMEM(power_shape, F32),
            pltpu.VMEM(power_shape, F32),
        ),
        in_specs=[SMEM_SPEC] + [VMEM_SPEC] * (len(late) + 5),
        out_specs=(VMEM_SPEC,) * 4,
        scratch_shapes=[held(len(late)), pltpu.VMEM(image_shape, F32)],
        compiler_params=params(),
        name="field_stage",
    )(plan, *late, panels, held_tiles, partial_field, basis, spread)

    tables = [table]
    for hop in range(1, group_count):
        tables.append(exchange(table, "col", hop))

    gradient = pl.pallas_call(
        functools.partial(gradient_kernel, len(tables)),
        out_shape=jax.ShapeDtypeStruct((block_count, node_count), F32),
        in_specs=[VMEM_SPEC] * (len(tables) + 4),
        out_specs=VMEM_SPEC,
        compiler_params=params(),
        name="gradient_stage",
    )(*tables, basis, spread, powers, crosses)
    return (field, gradient)


def solution(mesh):
    in_specs = (
        P(("row", "col"), None, None),
        P(("row", "col"), None, None),
        P(("row", "col")),
        P(("row", "col")),
        P(("row", "col"), None, None),
        P(("row", "col"), None),
        P(("row", "col"), None),
        P(("row", "col")),
    )
    out_specs = (P(("row", "col"), None, None), P(("row", "col"), None))
    return jax.shard_map(shards, mesh=mesh, in_specs=in_specs, out_specs=out_specs, check_vma=False)
```

time: 66.8 us -> 54.2 us (0.81)
  between operations: 14.1 us -> 0.74 us
  local copies, waits for them, and re-layouts: 5.73 us -> 17.2 us
  matrix products: 11.3 us -> 0 us
  Pallas kernels: 0 us -> 11.2 us
  starting transfers between devices: 0.04 us -> 10.1 us
  blocking collectives: 9.96 us -> 0 us
  waiting for transfers between devices: 21.5 us -> 15.1 us
  other arithmetic: 3.65 us -> 0 us
    all_gather x1 -> x0, waiting for transfers between devices: 21.4 us -> none  [shards(): gathered = lax.all_gather(flat_panels, 'row', axis=0, tiled=True)]
    ppermute x0 -> x10, waiting for transfers between devices: none -> 15.1 us  [exchange(): return lax.ppermute(values, axis, pairs)]
    unnamed x9 -> x24, local copies, waits for them, and re-layouts: 3.35 us -> 17.2 us
    dot_general x9 -> x0, matrix products: 11.3 us -> none  [the longest x1 6.83 us: shards(): jnp.einsum('tjn,tnm->tjm', chosen, tiles, preferred_element_type=jnp.floa...]
    pallas_call x0 -> x4, Pallas kernels: none -> 11.2 us  [the longest x1 4.97 us: shards(): pl.pallas_call(functools.partial(first_kernel, bounds, width), out_shape=...]
    ppermute x0 -> x10, starting transfers between devices: none -> 10.1 us  [exchange(): return lax.ppermute(values, axis, pairs)]
    psum x1 -> x0, blocking collectives: 9.96 us -> none  [shards(): totals = lax.psum(table, 'col')]
    slice x2 -> x0, local copies, waits for them, and re-layouts: 1.52 us -> none  [the longest x1 0.78 us: make_basis(): normal[:, 2]]
  transfers between devices with their start and end apart: 1 -> 10, of which waited for: 1 -> 5; matrix products, arithmetic and copies ran while one was open for 7% -> 0% of each run, Pallas kernels for 0% -> 15%
where the time goes in v1:
time: 54.2 us; the launch traced here: 54.3 us
  local copies, waits for them, and re-layouts  17.2 us (32%)
  waiting for transfers between devices  15.1 us (28%)
  Pallas kernels  11.2 us (21%)
  starting transfers between devices  10.1 us (19%)
  between operations  0.74 us (1%)
    unnamed x24, local copies, waits for them, and re-layouts  17.2 us
    ppermute x10, waiting for transfers between devices, exchange(): return lax.ppermute(values, axis, pairs)  15.1 us
    ppermute x10, starting transfers between devices, exchange(): return lax.ppermute(values, axis, pairs)  10.1 us
    pallas_call x1, Pallas kernels, shards(): pl.pallas_call(functools.partial(first_kernel, bounds, width), out_shape=...  4.97 us
    pallas_call x1, Pallas kernels, shards(): pl.pallas_call(functools.partial(middle_kernel, width, len(middle)), out_...  3.25 us
    pallas_call x1, Pallas kernels, shards(): pl.pallas_call(functools.partial(field_kernel, width, len(late)), out_sha...  2.05 us
  transfers between devices with their start and end apart: 10, of which 5 were waited for; matrix products, arithmetic and copies ran while one was open for 0% of the time, Pallas kernels for 15%

profile of v1, /device:TPU:0, one launch (start us, length us, event | category | flops | bytes accessed | tf_op | source)
XLA Modules:
  0.0 54.3 jit_solution(15979655620517522821)
XLA Ops:
  0.6 3.1 %collective-permute-start.3 = (bf16[8,32,256]{2,1,0:T(8,128)(2,1)}, bf16[8,32,256]{2,1,0:T(8,128)(2,1)S(1)}, u32[]{:S(2)}, u32[]{:S(2)}) collective-permute-start(bf16[8,32,256]{2,1,0:T(8,128)(2,1)} %refs_2_.1), channel_id=1, source_target_pairs={{0,8},{4,12},{8,0},{12,4},{16,24},{20,28},{24,16},{28,20},{1,9},{5... | collective-permute-start | bytes 393224 | tf_op jit(solution)/shard_map/ppermute | solution.py:212
  3.7 2.6 %collective-permute-start.5 = (bf16[8,32,256]{2,1,0:T(8,128)(2,1)}, bf16[8,32,256]{2,1,0:T(8,128)(2,1)S(1)}, u32[]{:S(2)}, u32[]{:S(2)}) collective-permute-start(bf16[8,32,256]{2,1,0:T(8,128)(2,1)} %refs_2_.1), channel_id=1, source_target_pairs={{0,16},{4,20},{8,24},{12,28},{16,0},{20,4},{24,8},{28,12},{1,17},{... | collective-permute-start | bytes 393224 | tf_op jit(solution)/shard_map/ppermute | solution.py:212
  6.3 0.0 collective-permute-start
  6.3 0.0 collective-permute-start.2
  6.3 2.6 %collective-permute-done.3.refs_1_ = bf16[8,32,256]{2,1,0:T(8,128)(2,1)S(1)} collective-permute-done((bf16[8,32,256]{2,1,0:T(8,128)(2,1)}, bf16[8,32,256]{2,1,0:T(8,128)(2,1)S(1)}, u32[]{:S(2)}, u32[]{:S(2)}) %collective-permute-start.3) | collective-permute-done | bytes 131104 | tf_op jit(solution)/shard_map/ppermute | solution.py:212
  9.0 0.0 collective-permute-start.4
  9.0 7.9 %collective-permute-done.5.refs_3_ = bf16[8,32,256]{2,1,0:T(8,128)(2,1)S(1)} collective-permute-done((bf16[8,32,256]{2,1,0:T(8,128)(2,1)}, bf16[8,32,256]{2,1,0:T(8,128)(2,1)S(1)}, u32[]{:S(2)}, u32[]{:S(2)}) %collective-permute-start.5) | collective-permute-done | bytes 131104 | tf_op jit(solution)/shard_map/ppermute | solution.py:212
  16.9 0.0 collective-permute-start.6
  16.9 0.0 collective-permute-done.refs_0_
  16.9 0.5 collective-permute-start.1
  17.4 4.6 %copy-done.3 = bf16[48,256,512]{2,1,0:T(8,128)(2,1)S(1)} copy-done((bf16[48,256,512]{2,1,0:T(8,128)(2,1)S(1)}, bf16[48,256,512]{2,1,0:T(8,128)(2,1)}, u32[]{:S(2)}) %copy-start.3) | copy-done | bytes 12582936
  22.0 0.9 %copy-done.4 = bf16[8,32,256]{2,1,0:T(8,128)(2,1)S(1)} copy-done((bf16[8,32,256]{2,1,0:T(8,128)(2,1)S(1)}, bf16[8,32,256]{2,1,0:T(8,128)(2,1)}, u32[]{:S(2)}) %copy-start.4) | copy-done | bytes 131096
  22.9 0.7 %copy-done.8 = s32[48]{0:T(128)S(1)} copy-done((s32[48]{0:T(128)S(1)}, s32[48]{0:T(128)}, u32[]{:S(2)}) %copy-start.8) | copy-done | bytes 216
  23.5 0.7 %copy-done.9 = s32[48]{0:T(128)S(1)} copy-done((s32[48]{0:T(128)S(1)}, s32[48]{0:T(128)}, u32[]{:S(2)}) %copy-start.9) | copy-done | bytes 216
  24.2 5.0 %first_stage.1 = (bf16[48,256,512]{2,1,0:T(8,128)(2,1)S(1)}, f32[8,32,512]{2,1,0:T(8,128)S(1)}, s32[512]{0:T(512)S(1)}) custom-call(s32[48]{0:T(128)S(1)} %copy-done.8, s32[48]{0:T(128)S(1)} %copy-done.9, bf16[8,32,256]{2,1,0:T(8,128)(2,1)S(1)} %copy-done.4, bf16[48,256,512]{2,1,0:T(8,128)(2,1)S(1)} %copy-done.3), custom_call_target="tpu_custom_call" | custom-call | bytes 25165824 | tf_op jit(solution)/shard_map/first_stage/pallas_call | solution.py:236
  29.2 0.0 copy-start
  29.2 4.5 %copy-done = bf16[48,256,512]{2,1,0:T(8,128)(2,1)} copy-done((bf16[48,256,512]{2,1,0:T(8,128)(2,1)}, bf16[48,256,512]{2,1,0:T(8,128)(2,1)S(1)}, u32[]{:S(2)}) %copy-start) | copy-done | bytes 12582936
  33.7 0.0 collective-permute-done.2.refs_0_
  33.7 0.0 collective-permute-done.4.refs_2_
  33.7 0.0 collective-permute-done.6.refs_4_
  33.8 4.6 %copy-done.1 = bf16[48,256,512]{2,1,0:T(8,128)(2,1)S(1)} copy-done((bf16[48,256,512]{2,1,0:T(8,128)(2,1)S(1)}, bf16[48,256,512]{2,1,0:T(8,128)(2,1)}, u32[]{:S(2)}) %copy-start.1) | copy-done | bytes 12582936
  38.3 3.3 %middle_stage.1 = (f32[8,32,512]{2,1,0:T(8,128)S(1)}, f32[64,256]{1,0:T(8,128)S(1)}, bf16[128,256]{1,0:T(8,128)(2,1)S(1)}) custom-call(s32[512]{0:T(512)S(1)} %get-tuple-element.12.plan, s32[8]{0:T(128)S(1)} %bitcast.3, s32[8]{0:T(128)S(1)} %copy-done.11, bf16[8,32,256]{2,1,0:T(8,128)(2,1)S(1)} %collective-permute-done.2.refs_0_, ...), custom_call_target="tpu_custom_call" | custom-call | tf_op jit(solution)/shard_map/middle_stage/pallas_call | solution.py:258
  41.6 0.0 collective-permute-done.1.refs_1_
  41.6 1.3 %copy-done.2 = bf16[48,256,512]{2,1,0:T(8,128)(2,1)S(1)} copy-done((bf16[48,256,512]{2,1,0:T(8,128)(2,1)S(1)}, bf16[48,256,512]{2,1,0:T(8,128)(2,1)}, u32[]{:S(2)}) %copy-start.2) | copy-done | bytes 12582936
  42.9 2.1 %field_stage.1 = (f32[8,32,256]{2,1,0:T(8,128)}, f32[8,256]{1,0:T(8,128)S(1)}, f32[128,256]{1,0:T(8,128)S(1)}, f32[128,256]{1,0:T(8,128)S(1)}) custom-call(s32[512]{0:T(512)S(1)} %get-tuple-element.12.plan, bf16[8,32,256]{2,1,0:T(8,128)(2,1)S(1)} %collective-permute-done.refs_0_, bf16[8,32,256]{2,1,0:T(8,128)(2,1)S(1)} %collective-permute-done.1.refs_1_, ...), custom_call_target="tpu_custom_call" | custom-call | tf_op jit(solution)/shard_map/field_stage/pallas_call | solution.py:282
  45.0 2.4 %collective-permute-start.7 = (f32[8,256]{1,0:T(8,128)S(1)}, f32[8,256]{1,0:T(8,128)S(1)}, u32[]{:S(2)}, u32[]{:S(2)}) collective-permute-start(f32[8,256]{1,0:T(8,128)S(1)} %get-tuple-element.19.refs_0_), channel_id=1, source_target_pairs={{0,1},{1,0},{2,3},{3,2},{4,5},{5,4},{6,7},{7,6},{8,9},{9,8},{10,11... | collective-permute-start | bytes 24584 | tf_op jit(solution)/shard_map/ppermute | solution.py:212
  47.3 1.5 %collective-permute-start.8 = (f32[8,256]{1,0:T(8,128)S(1)}, f32[8,256]{1,0:T(8,128)S(1)}, u32[]{:S(2)}, u32[]{:S(2)}) collective-permute-start(f32[8,256]{1,0:T(8,128)S(1)} %get-tuple-element.19.refs_0_), channel_id=1, source_target_pairs={{0,2},{1,3},{2,0},{3,1},{4,6},{5,7},{6,4},{7,5},{8,10},{9,11},{10,... | collective-permute-start | bytes 24584 | tf_op jit(solution)/shard_map/ppermute | solution.py:212
  48.8 0.0 collective-permute-start.9
  48.8 0.1 collective-permute-done.7.refs_1_
  48.9 2.0 %collective-permute-done.8.refs_2_ = f32[8,256]{1,0:T(8,128)S(1)} collective-permute-done((f32[8,256]{1,0:T(8,128)S(1)}, f32[8,256]{1,0:T(8,128)S(1)}, u32[]{:S(2)}, u32[]{:S(2)}) %collective-permute-start.8) | collective-permute-done | bytes 8224 | tf_op jit(solution)/shard_map/ppermute | solution.py:212
  51.0 2.4 %collective-permute-done.9.refs_3_ = f32[8,256]{1,0:T(8,128)S(1)} collective-permute-done((f32[8,256]{1,0:T(8,128)S(1)}, f32[8,256]{1,0:T(8,128)S(1)}, u32[]{:S(2)}, u32[]{:S(2)}) %collective-permute-start.9) | collective-permute-done | bytes 8224 | tf_op jit(solution)/shard_map/ppermute | solution.py:212
  53.4 0.9 %gradient_stage.1 = f32[8,256]{1,0:T(8,128)} custom-call(f32[8,256]{1,0:T(8,128)S(1)} %get-tuple-element.19.refs_0_, f32[8,256]{1,0:T(8,128)S(1)} %collective-permute-done.7.refs_1_, f32[8,256]{1,0:T(8,128)S(1)} %collective-permute-done.8.refs_2_, f32[8,256]{1,0:T(8,128)S(1)} %collective-permute-done.9.refs_3_, ...), custom_call_target="tpu_custom_call" | custom-call | tf_op jit(solution)/shard_map/gradient_stage/pallas_call | solution.py:301
  (16 shorter events, 0.0 us)
Async XLA Ops:
  0.6 8.3 %collective-permute-start.3 = (bf16[8,32,256]{2,1,0:T(8,128)(2,1)}, bf16[8,32,256]{2,1,0:T(8,128)(2,1)S(1)}, u32[]{:S(2)}, u32[]{:S(2)}) collective-permute-start(bf16[8,32,256]{2,1,0:T(8,128)(2,1)} %refs_2_.1), channel_id=1, source_target_pairs={{0,8},{4,12},{8,0},{12,4},{16,24},{20,28},{24,16},{28,20},{1,9},{5... | collective-permute-start | bytes 393224 | tf_op jit(solution)/shard_map/ppermute | solution.py:212
  3.7 13.2 %collective-permute-start.5 = (bf16[8,32,256]{2,1,0:T(8,128)(2,1)}, bf16[8,32,256]{2,1,0:T(8,128)(2,1)S(1)}, u32[]{:S(2)}, u32[]{:S(2)}) collective-permute-start(bf16[8,32,256]{2,1,0:T(8,128)(2,1)} %refs_2_.1), channel_id=1, source_target_pairs={{0,16},{4,20},{8,24},{12,28},{16,0},{20,4},{24,8},{28,12},{1,17},{... | collective-permute-start | bytes 393224 | tf_op jit(solution)/shard_map/ppermute | solution.py:212
  6.3 10.6 %collective-permute-start = (bf16[8,32,256]{2,1,0:T(8,128)(2,1)}, bf16[8,32,256]{2,1,0:T(8,128)(2,1)S(1)}, u32[]{:S(2)}, u32[]{:S(2)}) collective-permute-start(bf16[8,32,256]{2,1,0:T(8,128)(2,1)} %refs_2_.1), channel_id=1, source_target_pairs={{0,24},{4,28},{8,16},{12,20},{16,8},{20,12},{24,0},{28,4},{1,25},{... | collective-permute-start | bytes 393224 | tf_op jit(solution)/shard_map/ppermute | solution.py:212
  6.3 27.4 %collective-permute-start.2 = (bf16[8,32,256]{2,1,0:T(8,128)(2,1)}, bf16[8,32,256]{2,1,0:T(8,128)(2,1)S(1)}, u32[]{:S(2)}, u32[]{:S(2)}) collective-permute-start(bf16[8,32,256]{2,1,0:T(8,128)(2,1)} %refs_2_.1), channel_id=1, source_target_pairs={{0,4},{4,0},{8,12},{12,8},{16,20},{20,16},{24,28},{28,24},{1,5},{5... | collective-permute-start | bytes 393224 | tf_op jit(solution)/shard_map/ppermute | solution.py:212
  9.0 24.7 %collective-permute-start.4 = (bf16[8,32,256]{2,1,0:T(8,128)(2,1)S(1)}, bf16[8,32,256]{2,1,0:T(8,128)(2,1)S(1)}, u32[]{:S(2)}, u32[]{:S(2)}) collective-permute-start(bf16[8,32,256]{2,1,0:T(8,128)(2,1)S(1)} %collective-permute-done.3.refs_1_), channel_id=1, source_target_pairs={{0,4},{4,0},{8,12},{12,8},{16,20},{20,16},{24,28},{28,24},{1,5},{5... | collective-permute-start | bytes 393224 | tf_op jit(solution)/shard_map/ppermute | solution.py:212
  16.9 16.8 %collective-permute-start.6 = (bf16[8,32,256]{2,1,0:T(8,128)(2,1)S(1)}, bf16[8,32,256]{2,1,0:T(8,128)(2,1)S(1)}, u32[]{:S(2)}, u32[]{:S(2)}) collective-permute-start(bf16[8,32,256]{2,1,0:T(8,128)(2,1)S(1)} %collective-permute-done.5.refs_3_), channel_id=1, source_target_pairs={{0,4},{4,0},{8,12},{12,8},{16,20},{20,16},{24,28},{28,24},{1,5},{5... | collective-permute-start | bytes 393224 | tf_op jit(solution)/shard_map/ppermute | solution.py:212
  16.9 24.7 %collective-permute-start.1 = (bf16[8,32,256]{2,1,0:T(8,128)(2,1)S(1)}, bf16[8,32,256]{2,1,0:T(8,128)(2,1)S(1)}, u32[]{:S(2)}, u32[]{:S(2)}) collective-permute-start(bf16[8,32,256]{2,1,0:T(8,128)(2,1)S(1)} %collective-permute-done.refs_0_), channel_id=1, source_target_pairs={{0,4},{4,0},{8,12},{12,8},{16,20},{20,16},{24,28},{28,24},{1,5},{5... | collective-permute-start | bytes 393224 | tf_op jit(solution)/shard_map/ppermute | solution.py:212
  17.4 4.6 %copy-start.3 = (bf16[48,256,512]{2,1,0:T(8,128)(2,1)S(1)}, bf16[48,256,512]{2,1,0:T(8,128)(2,1)}, u32[]{:S(2)}) copy-start(bf16[48,256,512]{2,1,0:T(8,128)(2,1)} %tiles.1) | copy-start | bytes 37748740
  22.0 0.9 %copy-start.4 = (bf16[8,32,256]{2,1,0:T(8,128)(2,1)S(1)}, bf16[8,32,256]{2,1,0:T(8,128)(2,1)}, u32[]{:S(2)}) copy-start(bf16[8,32,256]{2,1,0:T(8,128)(2,1)} %refs_2_.1) | copy-start | bytes 393220
  22.9 0.7 %copy-start.8 = (s32[48]{0:T(128)S(1)}, s32[48]{0:T(128)}, u32[]{:S(2)}) copy-start(s32[48]{0:T(128)} %src.1) | copy-start | bytes 580
  23.5 0.7 %copy-start.9 = (s32[48]{0:T(128)S(1)}, s32[48]{0:T(128)}, u32[]{:S(2)}) copy-start(s32[48]{0:T(128)} %dst.1) | copy-start | bytes 580
  24.2 9.5 %copy-start.6 = (f32[8,6,256]{2,0,1:T(8,128)S(1)}, f32[8,6,256]{2,0,1:T(8,128)}, u32[]{:S(2)}) copy-start(f32[8,6,256]{2,0,1:T(8,128)} %param.12) | copy-start | bytes 147460
  24.2 9.5 %copy-start.7 = (f32[8,256]{1,0:T(8,128)S(1)}, f32[8,256]{1,0:T(8,128)}, u32[]{:S(2)}) copy-start(f32[8,256]{1,0:T(8,128)} %refs_8_.1) | copy-start | bytes 24580
  24.2 9.6 %copy-start.10 = (s32[8,1]{0,1:T(1,128)S(1)}, s32[8,1]{0,1:T(1,128)}, u32[]{:S(2)}) copy-start(s32[8,1]{0,1:T(1,128)} %param.14) | copy-start | bytes 100
  24.2 9.6 %copy-start.11 = (s32[8]{0:T(128)S(1)}, s32[8]{0:T(128)}, u32[]{:S(2)}) copy-start(s32[8]{0:T(128)} %slot.1) | copy-start | bytes 100
  24.2 17.4 %copy-start.5 = (bf16[8,32,256]{2,1,0:T(8,128)(2,1)S(1)}, bf16[8,32,256]{2,1,0:T(8,128)(2,1)}, u32[]{:S(2)}) copy-start(bf16[8,32,256]{2,1,0:T(8,128)(2,1)} %refs_2_.1) | copy-start | bytes 393220
  29.2 4.5 %copy-start = (bf16[48,256,512]{2,1,0:T(8,128)(2,1)}, bf16[48,256,512]{2,1,0:T(8,128)(2,1)S(1)}, u32[]{:S(2)}) copy-start(bf16[48,256,512]{2,1,0:T(8,128)(2,1)S(1)} %get-tuple-element.13.refs_5_.refs_3_) | copy-start | bytes 37748740
  33.8 4.6 %copy-start.1 = (bf16[48,256,512]{2,1,0:T(8,128)(2,1)S(1)}, bf16[48,256,512]{2,1,0:T(8,128)(2,1)}, u32[]{:S(2)}) copy-start(bf16[48,256,512]{2,1,0:T(8,128)(2,1)} %copy-done) | copy-start | bytes 37748740
  38.3 4.6 %copy-start.2 = (bf16[48,256,512]{2,1,0:T(8,128)(2,1)S(1)}, bf16[48,256,512]{2,1,0:T(8,128)(2,1)}, u32[]{:S(2)}) copy-start(bf16[48,256,512]{2,1,0:T(8,128)(2,1)} %copy-done) | copy-start | bytes 37748740
  45.0 4.0 %collective-permute-start.7 = (f32[8,256]{1,0:T(8,128)S(1)}, f32[8,256]{1,0:T(8,128)S(1)}, u32[]{:S(2)}, u32[]{:S(2)}) collective-permute-start(f32[8,256]{1,0:T(8,128)S(1)} %get-tuple-element.19.refs_0_), channel_id=1, source_target_pairs={{0,1},{1,0},{2,3},{3,2},{4,5},{5,4},{6,7},{7,6},{8,9},{9,8},{10,11... | collective-permute-start | bytes 24584 | tf_op jit(solution)/shard_map/ppermute | solution.py:212
  47.3 3.7 %collective-permute-start.8 = (f32[8,256]{1,0:T(8,128)S(1)}, f32[8,256]{1,0:T(8,128)S(1)}, u32[]{:S(2)}, u32[]{:S(2)}) collective-permute-start(f32[8,256]{1,0:T(8,128)S(1)} %get-tuple-element.19.refs_0_), channel_id=1, source_target_pairs={{0,2},{1,3},{2,0},{3,1},{4,6},{5,7},{6,4},{7,5},{8,10},{9,11},{10,... | collective-permute-start | bytes 24584 | tf_op jit(solution)/shard_map/ppermute | solution.py:212
  48.8 4.5 %collective-permute-start.9 = (f32[8,256]{1,0:T(8,128)S(1)}, f32[8,256]{1,0:T(8,128)S(1)}, u32[]{:S(2)}, u32[]{:S(2)}) collective-permute-start(f32[8,256]{1,0:T(8,128)S(1)} %get-tuple-element.19.refs_0_), channel_id=1, source_target_pairs={{0,3},{1,2},{2,1},{3,0},{4,7},{5,6},{6,5},{7,4},{8,11},{9,10},{10,... | collective-permute-start | bytes 24584 | tf_op jit(solution)/shard_map/ppermute | solution.py:212

commit v2 on v1

--- a/solution.py
+++ b/solution.py
@@ -14,15 +14,16 @@
 MOMENTS = 8
 F32 = jnp.float32
 BF16 = jnp.bfloat16
-VMEM_LIMIT = 28 << 20
+VMEM_LIMIT = 8 << 20
+FIRST_LIMIT = 44 << 20
 
 VMEM_SPEC = pl.BlockSpec(memory_space=pltpu.VMEM)
 SMEM_SPEC = pl.BlockSpec(memory_space=pltpu.SMEM)
-ANY_SPEC = pl.BlockSpec(memory_space=pl.ANY)
-
-
-def params():
-    return pltpu.CompilerParams(vmem_limit_bytes=VMEM_LIMIT)
+HBM_SPEC = pl.BlockSpec(memory_space=pltpu.HBM)
+
+
+def params(limit=VMEM_LIMIT):
+    return pltpu.CompilerParams(vmem_limit_bytes=limit)
 
 
 def parts_of(values, count):
@@ -230,9 +231,6 @@
     for hop in [row_count - 2, *range(row_count - 4, 0, -2)]:
         hops[hop] = exchange(panels, "row", hop)
     hops[1] = exchange(panels, "row", 1)
-    for hop in range(2, row_count, 2):
-        hops[hop + 1] = exchange(hops[hop], "row", 1)
-
     held_tiles, early, plan = pl.pallas_call(
         functools.partial(first_kernel, bounds, width),
         out_shape=(
@@ -240,15 +238,19 @@
             pltpu.VMEM(image_shape, F32),
             jax.ShapeDtypeStruct((3 * width + 128,), jnp.int32),
         ),
-        in_specs=[SMEM_SPEC, SMEM_SPEC, VMEM_SPEC, ANY_SPEC],
+        in_specs=[SMEM_SPEC, SMEM_SPEC, VMEM_SPEC, HBM_SPEC],
         out_specs=(VMEM_SPEC, VMEM_SPEC, SMEM_SPEC),
         scratch_shapes=[held(1), pltpu.SemaphoreType.DMA((COPIES,))],
-        compiler_params=params(),
+        compiler_params=params(FIRST_LIMIT),
         cost_estimate=pl.CostEstimate(
             flops=0, bytes_accessed=2 * tiles.size * 2, transcendentals=0
         ),
         name="first_stage",
     )(tile_src, tile_dst, panels, tiles)
+
+    for hop in range(2, row_count, 2):
+        hops[hop], plan = lax.optimization_barrier((hops[hop], plan))
+        hops[hop + 1] = exchange(hops[hop], "row", 1)
 
     middle = [hops[j] for j in range(bounds[1], bounds[2])]
     basis_shape = (MOMENTS * block_count, node_count)

time: 54.2 us -> 33.2 us (0.61)
  local copies, waits for them, and re-layouts: 17.2 us -> 0.7 us
  waiting for transfers between devices: 15.1 us -> 8.8 us
  Pallas kernels: 11.2 us -> 13.1 us
    unnamed x24 -> x12, local copies, waits for them, and re-layouts: 17.2 us -> 0.7 us
    ppermute x10, waiting for transfers between devices: 15.1 us -> 8.8 us  [exchange(): return lax.ppermute(values, axis, pairs)]
    pallas_call x1, Pallas kernels: 4.97 us -> 6.83 us  [shards(): pl.pallas_call(functools.partial(first_kernel, bounds, width), out_shape=...]
  transfers between devices with their start and end apart: 10 -> 10, of which waited for: 5 -> 6; matrix products, arithmetic and copies ran while one was open for 0% -> 0% of each run, Pallas kernels for 15% -> 30%
where the time goes in v2:
time: 33.2 us; the launch traced here: 33 us
  Pallas kernels  13.1 us (39%)
  starting transfers between devices  9.68 us (29%)
  waiting for transfers between devices  8.8 us (27%)
  between operations  0.74 us (2%)
  local copies, waits for them, and re-layouts  0.7 us (2%)
    ppermute x10, starting transfers between devices, exchange(): return lax.ppermute(values, axis, pairs)  9.68 us
    ppermute x10, waiting for transfers between devices, exchange(): return lax.ppermute(values, axis, pairs)  8.8 us
    pallas_call x1, Pallas kernels, shards(): pl.pallas_call(functools.partial(first_kernel, bounds, width), out_shape=...  6.83 us
    pallas_call x1, Pallas kernels, shards(): pl.pallas_call(functools.partial(middle_kernel, width, len(middle)), out_...  2.97 us
    pallas_call x1, Pallas kernels, shards(): pl.pallas_call(functools.partial(field_kernel, width, len(late)), out_sha...  2.34 us
    pallas_call x1, Pallas kernels, shards(): pl.pallas_call(functools.partial(gradient_kernel, len(tables)), out_shape...  0.94 us
    unnamed x12, local copies, waits for them, and re-layouts  0.7 us
  transfers between devices with their start and end apart: 10, of which 6 were waited for; matrix products, arithmetic and copies ran while one was open for 0% of the time, Pallas kernels for 30%

profile of v2, /device:TPU:0, one launch (start us, length us, event | category | flops | bytes accessed | tf_op | source)
XLA Modules:
  0.0 33.0 jit_solution(1569186544399239217)
XLA Ops:
  0.6 0.0 copy-start
  0.6 0.0 copy-start.4
  0.7 0.0 copy-start.1
  0.7 0.0 copy-start.2
  0.7 0.0 copy-start.5
  0.7 3.1 %collective-permute-start.2 = (bf16[8,32,256]{2,1,0:T(8,128)(2,1)}, bf16[8,32,256]{2,1,0:T(8,128)(2,1)S(1)}, u32[]{:S(2)}, u32[]{:S(2)}) collective-permute-start(bf16[8,32,256]{2,1,0:T(8,128)(2,1)} %refs_2_.1), channel_id=1, source_target_pairs={{0,8},{4,12},{8,0},{12,4},{16,24},{20,28},{24,16},{28,20},{1,9},{5... | collective-permute-start | bytes 393224 | tf_op jit(solution)/shard_map/ppermute | solution.py:213
  3.8 2.6 %collective-permute-start.1 = (bf16[8,32,256]{2,1,0:T(8,128)(2,1)}, bf16[8,32,256]{2,1,0:T(8,128)(2,1)S(1)}, u32[]{:S(2)}, u32[]{:S(2)}) collective-permute-start(bf16[8,32,256]{2,1,0:T(8,128)(2,1)} %refs_2_.1), channel_id=1, source_target_pairs={{0,16},{4,20},{8,24},{12,28},{16,0},{20,4},{24,8},{28,12},{1,17},{... | collective-permute-start | bytes 393224 | tf_op jit(solution)/shard_map/ppermute | solution.py:213
  6.4 0.0 collective-permute-start
  6.4 0.0 collective-permute-start.4
  6.4 6.8 %first_stage.1 = (bf16[48,256,512]{2,1,0:T(8,128)(2,1)S(1)}, f32[8,32,512]{2,1,0:T(8,128)S(1)}, s32[512]{0:T(512)}) custom-call(s32[48]{0:T(128)} %src.1, s32[48]{0:T(128)} %dst.1, bf16[8,32,256]{2,1,0:T(8,128)(2,1)} %refs_2_.1, bf16[48,256,512]{2,1,0:T(8,128)(2,1)} %tiles.1), custom_call_target="tpu_custom_call" | custom-call | bytes 25165824 | tf_op jit(solution)/shard_map/first_stage/pallas_call | solution.py:234
  13.2 0.0 collective-permute-done.2.refs_1_
  13.2 3.7 %collective-permute-done.1.refs_3_ = bf16[8,32,256]{2,1,0:T(8,128)(2,1)S(1)} collective-permute-done((bf16[8,32,256]{2,1,0:T(8,128)(2,1)}, bf16[8,32,256]{2,1,0:T(8,128)(2,1)S(1)}, u32[]{:S(2)}, u32[]{:S(2)}) %collective-permute-start.1) | collective-permute-done | bytes 131104 | tf_op jit(solution)/shard_map/ppermute | solution.py:213
  16.9 0.0 collective-permute-start.6
  16.9 0.5 %collective-permute-start.5 = (bf16[8,32,256]{2,1,0:T(8,128)(2,1)S(1)}, bf16[8,32,256]{2,1,0:T(8,128)(2,1)S(1)}, u32[]{:S(2)}, u32[]{:S(2)}) collective-permute-start(bf16[8,32,256]{2,1,0:T(8,128)(2,1)S(1)} %collective-permute-done.2.refs_1_), channel_id=1, source_target_pairs={{0,4},{4,0},{8,12},{12,8},{16,20},{20,16},{24,28},{28,24},{1,5},{5... | collective-permute-start | bytes 393224 | tf_op jit(solution)/shard_map/ppermute | solution.py:213
  17.4 0.0 collective-permute-done.refs_0_
  17.4 0.0 collective-permute-start.3
  17.4 0.0 collective-permute-done.4.refs_0_
  17.4 0.8 %collective-permute-done.6.refs_4_ = bf16[8,32,256]{2,1,0:T(8,128)(2,1)S(1)} collective-permute-done((bf16[8,32,256]{2,1,0:T(8,128)(2,1)S(1)}, bf16[8,32,256]{2,1,0:T(8,128)(2,1)S(1)}, u32[]{:S(2)}, u32[]{:S(2)}) %collective-permute-start.6) | collective-permute-done | bytes 131104 | tf_op jit(solution)/shard_map/ppermute | solution.py:213
  18.3 0.2 collective-permute-done.5.refs_2_
  18.5 0.0 copy-done.5
  18.5 0.0 copy-start.3
  18.5 0.7 %copy-done.3 = s32[512]{0:T(512)S(1)} copy-done((s32[512]{0:T(512)S(1)}, s32[512]{0:T(512)}, u32[]{:S(2)}) %copy-start.3) | copy-done | bytes 2072
  19.2 3.0 %middle_stage.1 = (f32[8,32,512]{2,1,0:T(8,128)S(1)}, f32[64,256]{1,0:T(8,128)S(1)}, bf16[128,256]{1,0:T(8,128)(2,1)S(1)}) custom-call(s32[512]{0:T(512)S(1)} %copy-done.3, s32[8]{0:T(128)S(1)} %bitcast.3, s32[8]{0:T(128)S(1)} %copy-done.5, bf16[8,32,256]{2,1,0:T(8,128)(2,1)S(1)} %collective-permute-done.4.refs_0_, ...), custom_call_target="tpu_custom_call" | custom-call | tf_op jit(solution)/shard_map/middle_stage/pallas_call | solution.py:260
  22.1 0.0 collective-permute-done.3.refs_1_
  22.2 2.3 %field_stage.1 = (f32[8,32,256]{2,1,0:T(8,128)}, f32[8,256]{1,0:T(8,128)S(1)}, f32[128,256]{1,0:T(8,128)S(1)}, f32[128,256]{1,0:T(8,128)S(1)}) custom-call(s32[512]{0:T(512)S(1)} %copy-done.3, bf16[8,32,256]{2,1,0:T(8,128)(2,1)S(1)} %collective-permute-done.refs_0_, bf16[8,32,256]{2,1,0:T(8,128)(2,1)S(1)} %collective-permute-done.3.refs_1_, ...), custom_call_target="tpu_custom_call" | custom-call | tf_op jit(solution)/shard_map/field_stage/pallas_call | solution.py:284
  24.5 1.5 %collective-permute-start.7 = (f32[8,256]{1,0:T(8,128)S(1)}, f32[8,256]{1,0:T(8,128)S(1)}, u32[]{:S(2)}, u32[]{:S(2)}) collective-permute-start(f32[8,256]{1,0:T(8,128)S(1)} %get-tuple-element.31.refs_0_), channel_id=1, source_target_pairs={{0,1},{1,0},{2,3},{3,2},{4,5},{5,4},{6,7},{7,6},{8,9},{9,8},{10,11... | collective-permute-start | bytes 24584 | tf_op jit(solution)/shard_map/ppermute | solution.py:213
  26.0 1.5 %collective-permute-start.8 = (f32[8,256]{1,0:T(8,128)S(1)}, f32[8,256]{1,0:T(8,128)S(1)}, u32[]{:S(2)}, u32[]{:S(2)}) collective-permute-start(f32[8,256]{1,0:T(8,128)S(1)} %get-tuple-element.31.refs_0_), channel_id=1, source_target_pairs={{0,2},{1,3},{2,0},{3,1},{4,6},{5,7},{6,4},{7,5},{8,10},{9,11},{10,... | collective-permute-start | bytes 24584 | tf_op jit(solution)/shard_map/ppermute | solution.py:213
  27.5 0.5 %collective-permute-start.9 = (f32[8,256]{1,0:T(8,128)S(1)}, f32[8,256]{1,0:T(8,128)S(1)}, u32[]{:S(2)}, u32[]{:S(2)}) collective-permute-start(f32[8,256]{1,0:T(8,128)S(1)} %get-tuple-element.31.refs_0_), channel_id=1, source_target_pairs={{0,3},{1,2},{2,1},{3,0},{4,7},{5,6},{6,5},{7,4},{8,11},{9,10},{10,... | collective-permute-start | bytes 24584 | tf_op jit(solution)/shard_map/ppermute | solution.py:213
  28.0 0.2 collective-permute-done.7.refs_1_
  28.2 1.5 %collective-permute-done.8.refs_2_ = f32[8,256]{1,0:T(8,128)S(1)} collective-permute-done((f32[8,256]{1,0:T(8,128)S(1)}, f32[8,256]{1,0:T(8,128)S(1)}, u32[]{:S(2)}, u32[]{:S(2)}) %collective-permute-start.8) | collective-permute-done | bytes 8224 | tf_op jit(solution)/shard_map/ppermute | solution.py:213
  29.6 2.4 %collective-permute-done.9.refs_3_ = f32[8,256]{1,0:T(8,128)S(1)} collective-permute-done((f32[8,256]{1,0:T(8,128)S(1)}, f32[8,256]{1,0:T(8,128)S(1)}, u32[]{:S(2)}, u32[]{:S(2)}) %collective-permute-start.9) | collective-permute-done | bytes 8224 | tf_op jit(solution)/shard_map/ppermute | solution.py:213
  32.1 0.9 %gradient_stage.1 = f32[8,256]{1,0:T(8,128)} custom-call(f32[8,256]{1,0:T(8,128)S(1)} %get-tuple-element.31.refs_0_, f32[8,256]{1,0:T(8,128)S(1)} %collective-permute-done.7.refs_1_, f32[8,256]{1,0:T(8,128)S(1)} %collective-permute-done.8.refs_2_, f32[8,256]{1,0:T(8,128)S(1)} %collective-permute-done.9.refs_3_, ...), custom_call_target="tpu_custom_call" | custom-call | tf_op jit(solution)/shard_map/gradient_stage/pallas_call | solution.py:303
  (4 shorter events, 0.0 us)
Async XLA Ops:
  0.6 21.5 %copy-start = (bf16[8,32,256]{2,1,0:T(8,128)(2,1)S(1)}, bf16[8,32,256]{2,1,0:T(8,128)(2,1)}, u32[]{:S(2)}) copy-start(bf16[8,32,256]{2,1,0:T(8,128)(2,1)} %refs_2_.1) | copy-start | bytes 393220
  0.6 17.8 %copy-start.4 = (s32[8,1]{0,1:T(1,128)S(1)}, s32[8,1]{0,1:T(1,128)}, u32[]{:S(2)}) copy-start(s32[8,1]{0,1:T(1,128)} %param.14) | copy-start | bytes 100
  0.7 17.8 %copy-start.1 = (f32[8,6,256]{2,0,1:T(8,128)S(1)}, f32[8,6,256]{2,0,1:T(8,128)}, u32[]{:S(2)}) copy-start(f32[8,6,256]{2,0,1:T(8,128)} %param.12) | copy-start | bytes 147460
  0.7 17.8 %copy-start.2 = (f32[8,256]{1,0:T(8,128)S(1)}, f32[8,256]{1,0:T(8,128)}, u32[]{:S(2)}) copy-start(f32[8,256]{1,0:T(8,128)} %refs_8_.1) | copy-start | bytes 24580
  0.7 17.8 %copy-start.5 = (s32[8]{0:T(128)S(1)}, s32[8]{0:T(128)}, u32[]{:S(2)}) copy-start(s32[8]{0:T(128)} %slot.1) | copy-start | bytes 100
  0.7 12.5 %collective-permute-start.2 = (bf16[8,32,256]{2,1,0:T(8,128)(2,1)}, bf16[8,32,256]{2,1,0:T(8,128)(2,1)S(1)}, u32[]{:S(2)}, u32[]{:S(2)}) collective-permute-start(bf16[8,32,256]{2,1,0:T(8,128)(2,1)} %refs_2_.1), channel_id=1, source_target_pairs={{0,8},{4,12},{8,0},{12,4},{16,24},{20,28},{24,16},{28,20},{1,9},{5... | collective-permute-start | bytes 393224 | tf_op jit(solution)/shard_map/ppermute | solution.py:213
  3.8 13.2 %collective-permute-start.1 = (bf16[8,32,256]{2,1,0:T(8,128)(2,1)}, bf16[8,32,256]{2,1,0:T(8,128)(2,1)S(1)}, u32[]{:S(2)}, u32[]{:S(2)}) collective-permute-start(bf16[8,32,256]{2,1,0:T(8,128)(2,1)} %refs_2_.1), channel_id=1, source_target_pairs={{0,16},{4,20},{8,24},{12,28},{16,0},{20,4},{24,8},{28,12},{1,17},{... | collective-permute-start | bytes 393224 | tf_op jit(solution)/shard_map/ppermute | solution.py:213
  6.4 11.1 %collective-permute-start = (bf16[8,32,256]{2,1,0:T(8,128)(2,1)}, bf16[8,32,256]{2,1,0:T(8,128)(2,1)S(1)}, u32[]{:S(2)}, u32[]{:S(2)}) collective-permute-start(bf16[8,32,256]{2,1,0:T(8,128)(2,1)} %refs_2_.1), channel_id=1, source_target_pairs={{0,24},{4,28},{8,16},{12,20},{16,8},{20,12},{24,0},{28,4},{1,25},{... | collective-permute-start | bytes 393224 | tf_op jit(solution)/shard_map/ppermute | solution.py:213
  6.4 11.1 %collective-permute-start.4 = (bf16[8,32,256]{2,1,0:T(8,128)(2,1)}, bf16[8,32,256]{2,1,0:T(8,128)(2,1)S(1)}, u32[]{:S(2)}, u32[]{:S(2)}) collective-permute-start(bf16[8,32,256]{2,1,0:T(8,128)(2,1)} %refs_2_.1), channel_id=1, source_target_pairs={{0,4},{4,0},{8,12},{12,8},{16,20},{20,16},{24,28},{28,24},{1,5},{5... | collective-permute-start | bytes 393224 | tf_op jit(solution)/shard_map/ppermute | solution.py:213
  16.9 1.3 %collective-permute-start.6 = (bf16[8,32,256]{2,1,0:T(8,128)(2,1)S(1)}, bf16[8,32,256]{2,1,0:T(8,128)(2,1)S(1)}, u32[]{:S(2)}, u32[]{:S(2)}) collective-permute-start(bf16[8,32,256]{2,1,0:T(8,128)(2,1)S(1)} %collective-permute-done.1.refs_3_), channel_id=1, source_target_pairs={{0,4},{4,0},{8,12},{12,8},{16,20},{20,16},{24,28},{28,24},{1,5},{5... | collective-permute-start | bytes 393224 | tf_op jit(solution)/shard_map/ppermute | solution.py:213
  16.9 1.5 %collective-permute-start.5 = (bf16[8,32,256]{2,1,0:T(8,128)(2,1)S(1)}, bf16[8,32,256]{2,1,0:T(8,128)(2,1)S(1)}, u32[]{:S(2)}, u32[]{:S(2)}) collective-permute-start(bf16[8,32,256]{2,1,0:T(8,128)(2,1)S(1)} %collective-permute-done.2.refs_1_), channel_id=1, source_target_pairs={{0,4},{4,0},{8,12},{12,8},{16,20},{20,16},{24,28},{28,24},{1,5},{5... | collective-permute-start | bytes 393224 | tf_op jit(solution)/shard_map/ppermute | solution.py:213
  17.4 4.7 %collective-permute-start.3 = (bf16[8,32,256]{2,1,0:T(8,128)(2,1)S(1)}, bf16[8,32,256]{2,1,0:T(8,128)(2,1)S(1)}, u32[]{:S(2)}, u32[]{:S(2)}) collective-permute-start(bf16[8,32,256]{2,1,0:T(8,128)(2,1)S(1)} %collective-permute-done.refs_0_), channel_id=1, source_target_pairs={{0,4},{4,0},{8,12},{12,8},{16,20},{20,16},{24,28},{28,24},{1,5},{5... | collective-permute-start | bytes 393224 | tf_op jit(solution)/shard_map/ppermute | solution.py:213
  18.5 0.7 %copy-start.3 = (s32[512]{0:T(512)S(1)}, s32[512]{0:T(512)}, u32[]{:S(2)}) copy-start(s32[512]{0:T(512)} %get-tuple-element.21.plan) | copy-start | bytes 6148
  24.5 3.7 %collective-permute-start.7 = (f32[8,256]{1,0:T(8,128)S(1)}, f32[8,256]{1,0:T(8,128)S(1)}, u32[]{:S(2)}, u32[]{:S(2)}) collective-permute-start(f32[8,256]{1,0:T(8,128)S(1)} %get-tuple-element.31.refs_0_), channel_id=1, source_target_pairs={{0,1},{1,0},{2,3},{3,2},{4,5},{5,4},{6,7},{7,6},{8,9},{9,8},{10,11... | collective-permute-start | bytes 24584 | tf_op jit(solution)/shard_map/ppermute | solution.py:213
  26.0 3.7 %collective-permute-start.8 = (f32[8,256]{1,0:T(8,128)S(1)}, f32[8,256]{1,0:T(8,128)S(1)}, u32[]{:S(2)}, u32[]{:S(2)}) collective-permute-start(f32[8,256]{1,0:T(8,128)S(1)} %get-tuple-element.31.refs_0_), channel_id=1, source_target_pairs={{0,2},{1,3},{2,0},{3,1},{4,6},{5,7},{6,4},{7,5},{8,10},{9,11},{10,... | collective-permute-start | bytes 24584 | tf_op jit(solution)/shard_map/ppermute | solution.py:213
  27.5 4.5 %collective-permute-start.9 = (f32[8,256]{1,0:T(8,128)S(1)}, f32[8,256]{1,0:T(8,128)S(1)}, u32[]{:S(2)}, u32[]{:S(2)}) collective-permute-start(f32[8,256]{1,0:T(8,128)S(1)} %get-tuple-element.31.refs_0_), channel_id=1, source_target_pairs={{0,3},{1,2},{2,1},{3,0},{4,7},{5,6},{6,5},{7,4},{8,11},{9,10},{10,... | collective-permute-start | bytes 24584 | tf_op jit(solution)/shard_map/ppermute | solution.py:213

commit v3 on v2

--- a/solution.py
+++ b/solution.py
@@ -78,9 +78,12 @@
     lax.fori_loop(plan[3 * width + stage], plan[3 * width + stage + 1], body, 0)
 
 
-def first_kernel(bounds, width, src, dst, panels, tiles, held_tiles, total, plan, held, sems):
+def load_kernel(
+    bounds, width, freq_count, src, dst, owner, slot, place, areas, tiles,
+    held_tiles, basis, spread, plan, sems,
+):
     tile_count = tiles.shape[0]
-    depth = panels.shape[0]
+    block_count = areas.shape[0]
     per_copy = tile_count // COPIES
     copies = [
         pltpu.make_async_copy(
@@ -94,38 +97,17 @@
         copy.start()
     me = lax.axis_index("row")
     position = jnp.int32(0)
-    for stage in range(len(bounds) - 1):
-        low, high = bounds[stage], bounds[stage + 1]
+    for stage, hops in enumerate(bounds):
         plan[3 * width + stage] = position // UNROLL
-
-        def place(t, position, low=low, high=high):
-            source = src[t]
-            hop = (source // depth) ^ me
-            plan[position] = t
-            plan[width + position] = (hop - low) * depth + source % depth
-            plan[2 * width + position] = dst[t]
-            return position + ((hop >= low) & (hop < high)).astype(jnp.int32)
-
-        position = lax.fori_loop(0, tile_count, place, position)
+        position = lax.fori_loop(
+            0, tile_count, functools.partial(place_tile, width, hops, block_count, me, src, dst, plan), position
+        )
         for lane in range(UNROLL):
             plan[position + lane] = 0
-            plan[width + position + lane] = (high - low) * depth
+            plan[width + position + lane] = len(hops) * block_count
             plan[2 * width + position + lane] = 0
         position = (position + UNROLL - 1) // UNROLL * UNROLL
-    plan[3 * width + len(bounds) - 1] = position // UNROLL
-    total[...] = jnp.zeros_like(total)
-    fill_panels([panels], held)
-    for copy in copies:
-        copy.wait()
-    add_stage(0, width, plan, held, held_tiles, total)
-
-
-def middle_kernel(width, count, plan, owner, slot, *refs):
-    sources = refs[:count]
-    tiles, start, place, areas, total, basis, spread, held = refs[count:]
-    block_count = areas.shape[0]
-    fill_panels(sources, held)
-    total[...] = start[...]
+    plan[3 * width + len(bounds)] = position // UNROLL
     nx, ny, nz, px, py, pz = [place[i] for i in range(6)]
     weight = areas[...]
     rows = [nx, ny, nz, py * nz - pz * ny, pz * nx - px * nz, px * ny - py * nx]
@@ -133,7 +115,6 @@
         basis[index * block_count : (index + 1) * block_count] = weight * row
     for index in range(len(rows), MOMENTS):
         basis[index * block_count : (index + 1) * block_count] = weight
-    freq_count = spread.shape[0] // block_count
     shape = (freq_count, spread.shape[1])
     lanes = lax.broadcasted_iota(jnp.int32, shape, 1)
     same = lanes % freq_count == lax.broadcasted_iota(jnp.int32, shape, 0)
@@ -143,10 +124,38 @@
         spread[block * freq_count : (block + 1) * freq_count] = jnp.where(
             chosen, 1.0, 0.0
         ).astype(BF16)
-    add_stage(1, width, plan, held, tiles, total)
-
-
-def field_kernel(width, count, plan, *refs):
+    for copy in copies:
+        copy.wait()
+
+
+def place_tile(width, hops, depth, me, src, dst, plan, t, position):
+    source = src[t]
+    hop = (source // depth) ^ me
+    here = hop == hops[0]
+    row = jnp.int32(0)
+    for index, other in enumerate(hops[1:], 1):
+        here = here | (hop == other)
+        row = jnp.where(hop == other, index, row)
+    plan[position] = t
+    plan[width + position] = row * depth + source % depth
+    plan[2 * width + position] = dst[t]
+    return position + here.astype(jnp.int32)
+
+
+def near_kernel(stage, width, count, begin, plan, *refs):
+    sources, refs = refs[:count], refs[count:]
+    tiles, refs = refs[0], refs[1:]
+    if begin:
+        total, held = refs
+        total[...] = jnp.zeros_like(total)
+    else:
+        start, total, held = refs
+        total[...] = start[...]
+    fill_panels(sources, held)
+    add_stage(stage, width, plan, held, tiles, total)
+
+
+def field_kernel(stage, width, count, plan, *refs):
     sources = refs[:count]
     panels, tiles, start, basis, spread = refs[count : count + 5]
     field, table, powers, crosses, held, total = refs[count + 5 :]
@@ -154,7 +163,7 @@
     freq_count = rows_twice // 2
     fill_panels(sources, held)
     total[...] = start[...]
-    add_stage(2, width, plan, held, tiles, total)
+    add_stage(stage, width, plan, held, tiles, total)
     for block in range(block_count):
         image = total[block]
         incident = panels[block].astype(F32)
@@ -220,84 +229,81 @@
     row_count = lax.axis_size("row")
     group_count = lax.axis_size("col")
     particle_count = group_count * PD
-    bounds = (0, 1, row_count - 2, row_count)
-    width = -(-(tile_count + 4 * UNROLL) // 128) * 128
+    direct = list(range(2, row_count, 2))
+    soon, late = direct[:-1], direct[-1]
+    stages = ([0, 1], soon, [hop + 1 for hop in soon] + [late], [late + 1])
+    width = -(-(tile_count + (len(stages) + 1) * UNROLL) // 128) * 128
     image_shape = (block_count, rows_twice, 2 * node_count)
-
-    def held(count):
-        return pltpu.VMEM((count * block_count + 1, rows_twice, node_count), BF16)
+    basis_shape = (MOMENTS * block_count, node_count)
+    spread_shape = (block_count * freq_count, particle_count * freq_count)
+    power_shape = (block_count * freq_count, node_count)
+    table_shape = (MOMENTS, particle_count * freq_count)
+
+    def held(stage):
+        return pltpu.VMEM((len(stages[stage]) * block_count + 1, rows_twice, node_count), BF16)
 
     hops = {0: panels}
-    for hop in [row_count - 2, *range(row_count - 4, 0, -2)]:
+    for hop in direct:
         hops[hop] = exchange(panels, "row", hop)
     hops[1] = exchange(panels, "row", 1)
-    held_tiles, early, plan = pl.pallas_call(
-        functools.partial(first_kernel, bounds, width),
+
+    held_tiles, basis, spread, plan = pl.pallas_call(
+        functools.partial(load_kernel, stages, width, freq_count),
         out_shape=(
             pltpu.VMEM(tiles.shape, tiles.dtype),
-            pltpu.VMEM(image_shape, F32),
-            jax.ShapeDtypeStruct((3 * width + 128,), jnp.int32),
+            pltpu.VMEM(basis_shape, F32),
+            pltpu.VMEM(spread_shape, BF16),
+            pltpu.SMEM((3 * width + 128,), jnp.int32),
         ),
-        in_specs=[SMEM_SPEC, SMEM_SPEC, VMEM_SPEC, HBM_SPEC],
-        out_specs=(VMEM_SPEC, VMEM_SPEC, SMEM_SPEC),
-        scratch_shapes=[held(1), pltpu.SemaphoreType.DMA((COPIES,))],
+        in_specs=[SMEM_SPEC] * 4 + [VMEM_SPEC] * 2 + [HBM_SPEC],
+        out_specs=(VMEM_SPEC,) * 3 + (SMEM_SPEC,),
+        scratch_shapes=[pltpu.SemaphoreType.DMA((COPIES,))],
         compiler_params=params(FIRST_LIMIT),
         cost_estimate=pl.CostEstimate(
             flops=0, bytes_accessed=2 * tiles.size * 2, transcendentals=0
         ),
-        name="first_stage",
-    )(tile_src, tile_dst, panels, tiles)
-
-    for hop in range(2, row_count, 2):
-        hops[hop], plan = lax.optimization_barrier((hops[hop], plan))
+        name="load_stage",
+    )(tile_src, tile_dst, block_owner[:, 0], block_slot, jnp.transpose(geometry, (1, 0, 2)), areas, tiles)
+
+    def near(stage, total):
+        begin = total is None
+        sources = [hops[hop] for hop in stages[stage]]
+        return pl.pallas_call(
+            functools.partial(near_kernel, stage, width, len(sources), begin),
+            out_shape=pltpu.VMEM(image_shape, F32),
+            in_specs=[SMEM_SPEC] + [VMEM_SPEC] * (len(sources) + (1 if begin else 2)),
+            out_specs=VMEM_SPEC,
+            scratch_shapes=[held(stage)],
+            compiler_params=params(),
+            name="near_stage",
+        )(plan, *sources, held_tiles, *([] if begin else [total]))
+
+    total = near(0, None)
+    for hop in soon:
+        hops[hop], total = lax.optimization_barrier((hops[hop], total))
         hops[hop + 1] = exchange(hops[hop], "row", 1)
-
-    middle = [hops[j] for j in range(bounds[1], bounds[2])]
-    basis_shape = (MOMENTS * block_count, node_count)
-    spread_shape = (block_count * freq_count, particle_count * freq_count)
-    power_shape = (block_count * freq_count, node_count)
-    table_shape = (MOMENTS, particle_count * freq_count)
-    partial_field, basis, spread = pl.pallas_call(
-        functools.partial(middle_kernel, width, len(middle)),
+    total = near(1, total)
+    hops[late], total = lax.optimization_barrier((hops[late], total))
+    hops[late + 1] = exchange(hops[late], "row", 1)
+    total = near(2, total)
+
+    field, table, powers, crosses = pl.pallas_call(
+        functools.partial(field_kernel, 3, width, 1),
         out_shape=(
-            pltpu.VMEM(image_shape, F32),
-            pltpu.VMEM(basis_shape, F32),
-            pltpu.VMEM(spread_shape, BF16),
-        ),
-        in_specs=[SMEM_SPEC] * 3 + [VMEM_SPEC] * (len(middle) + 4),
-        out_specs=(VMEM_SPEC,) * 3,
-        scratch_shapes=[held(len(middle))],
-        compiler_params=params(),
-        name="middle_stage",
-    )(
-        plan,
-        block_owner[:, 0],
-        block_slot,
-        *middle,
-        held_tiles,
-        early,
-        jnp.transpose(geometry, (1, 0, 2)),
-        areas,
-    )
-
-    late = [hops[j] for j in range(bounds[2], bounds[3])]
-    field, table, powers, crosses = pl.pallas_call(
-        functools.partial(field_kernel, width, len(late)),
-        out_shape=(
-            jax.ShapeDtypeStruct(panels.shape, F32),
+            pltpu.VMEM(panels.shape, F32),
             pltpu.VMEM(table_shape, F32),
             pltpu.VMEM(power_shape, F32),
             pltpu.VMEM(power_shape, F32),
         ),
-        in_specs=[SMEM_SPEC] + [VMEM_SPEC] * (len(late) + 5),
+        in_specs=[SMEM_SPEC] + [VMEM_SPEC] * 6,
         out_specs=(VMEM_SPEC,) * 4,
-        scratch_shapes=[held(len(late)), pltpu.VMEM(image_shape, F32)],
+        scratch_shapes=[held(3), pltpu.VMEM(image_shape, F32)],
         compiler_params=params(),
         name="field_stage",
-    )(plan, *late, panels, held_tiles, partial_field, basis, spread)
+    )(plan, hops[late + 1], panels, held_tiles, total, basis, spread)
 
     tables = [table]
-    for hop in range(1, group_count):
+    for hop in range(group_count - 1, 0, -1):
         tables.append(exchange(table, "col", hop))
 
     gradient = pl.pallas_call(

time: 33.2 us -> 29 us (0.87)
  waiting for transfers between devices: 8.8 us -> 6.75 us
  Pallas kernels: 13.1 us -> 11.1 us
    ppermute x10, waiting for transfers between devices: 8.8 us -> 6.75 us  [exchange(): return lax.ppermute(values, axis, pairs)]
    pallas_call x3 -> x5, Pallas kernels: 12.1 us -> 10.1 us  [the longest x1 5.51 us: shards(): pl.pallas_call(functools.partial(load_kernel, stages, width, freq_count),...]
    unnamed x12 -> x3, local copies, waits for them, and re-layouts: 0.7 us -> 0.71 us
  transfers between devices with their start and end apart: 10 -> 10, of which waited for: 6 -> 5; matrix products, arithmetic and copies ran while one was open for 0% -> 2% of each run, Pallas kernels for 30% -> 31%
where the time goes in v3:
time: 29 us; the launch traced here: 29.1 us
  Pallas kernels  11.1 us (38%)
  starting transfers between devices  9.84 us (34%)
  waiting for transfers between devices  6.75 us (23%)
  local copies, waits for them, and re-layouts  0.71 us (2%)
  between operations  0.71 us (2%)
    ppermute x10, starting transfers between devices, exchange(): return lax.ppermute(values, axis, pairs)  9.84 us
    ppermute x10, waiting for transfers between devices, exchange(): return lax.ppermute(values, axis, pairs)  6.75 us
    pallas_call x1, Pallas kernels, shards(): pl.pallas_call(functools.partial(load_kernel, stages, width, freq_count),...  5.51 us
    pallas_call x3, Pallas kernels, near(): pl.pallas_call(functools.partial(near_kernel, stage, width, len(sources),...  3.62 us
    pallas_call x1, Pallas kernels, shards(): pl.pallas_call(functools.partial(field_kernel, 3, width, 1), out_shape=(p...  1.01 us
    pallas_call x1, Pallas kernels, shards(): pl.pallas_call(functools.partial(gradient_kernel, len(tables)), out_shape...  0.94 us
    unnamed x3, local copies, waits for them, and re-layouts  0.71 us
  transfers between devices with their start and end apart: 10, of which 5 were waited for; matrix products, arithmetic and copies ran while one was open for 2% of the time, Pallas kernels for 31%

profile of v3, /device:TPU:0, one launch (start us, length us, event | category | flops | bytes accessed | tf_op | source)
XLA Modules:
  0.0 29.1 jit_solution(7710153768921139393)
XLA Ops:
  0.6 0.0 copy-start
  0.6 0.5 %collective-permute-start.2 = (bf16[8,32,256]{2,1,0:T(8,128)(2,1)}, bf16[8,32,256]{2,1,0:T(8,128)(2,1)S(1)}, u32[]{:S(2)}, u32[]{:S(2)}) collective-permute-start(bf16[8,32,256]{2,1,0:T(8,128)(2,1)} %refs_1_.1), channel_id=1, source_target_pairs={{0,4},{4,0},{8,12},{12,8},{16,20},{20,16},{24,28},{28,24},{1,5},{5... | collective-permute-start | bytes 393224 | tf_op jit(solution)/shard_map/ppermute | solution.py:222
  1.2 2.6 %collective-permute-start.1 = (bf16[8,32,256]{2,1,0:T(8,128)(2,1)}, bf16[8,32,256]{2,1,0:T(8,128)(2,1)S(1)}, u32[]{:S(2)}, u32[]{:S(2)}) collective-permute-start(bf16[8,32,256]{2,1,0:T(8,128)(2,1)} %refs_1_.1), channel_id=1, source_target_pairs={{0,8},{4,12},{8,0},{12,4},{16,24},{20,28},{24,16},{28,20},{1,9},{5... | collective-permute-start | bytes 393224 | tf_op jit(solution)/shard_map/ppermute | solution.py:222
  3.8 2.6 %collective-permute-start.3 = (bf16[8,32,256]{2,1,0:T(8,128)(2,1)}, bf16[8,32,256]{2,1,0:T(8,128)(2,1)S(1)}, u32[]{:S(2)}, u32[]{:S(2)}) collective-permute-start(bf16[8,32,256]{2,1,0:T(8,128)(2,1)} %refs_1_.1), channel_id=1, source_target_pairs={{0,16},{4,20},{8,24},{12,28},{16,0},{20,4},{24,8},{28,12},{1,17},{... | collective-permute-start | bytes 393224 | tf_op jit(solution)/shard_map/ppermute | solution.py:222
  6.4 0.0 collective-permute-start
  6.4 5.5 %load_stage.1 = (bf16[48,256,512]{2,1,0:T(8,128)(2,1)S(1)}, f32[64,256]{1,0:T(8,128)S(1)}, bf16[128,256]{1,0:T(8,128)(2,1)S(1)}, s32[512]{0:T(512)S(4)}) custom-call(s32[48]{0:T(128)} %src.1, s32[48]{0:T(128)} %dst.1, s32[8]{0:T(128)} %bitcast.3, s32[8]{0:T(128)} %slot.1, f32[6,8,256]{2,1,0:T(8,128)} %bitcast.2, f32[8,256]{1,0:T(8,128)} %areas.1, ...), custom_call_target="tpu_custom_call" | custom-call | bytes 25165824 | tf_op jit(solution)/shard_map/load_stage/pallas_call | solution.py:250
  11.9 0.0 collective-permute-done.2.refs_1_
  11.9 0.0 copy-done
  11.9 1.2 %near_stage.3.refs_3_ = f32[8,32,512]{2,1,0:T(8,128)S(1)} custom-call(s32[512]{0:T(512)S(4)} %get-tuple-element.16.plan, bf16[8,32,256]{2,1,0:T(8,128)(2,1)S(1)} %copy-done, bf16[8,32,256]{2,1,0:T(8,128)(2,1)S(1)} %collective-permute-done.2.refs_1_, bf16[48,256,512]{2,1,0:T(8,128)(2,1)S(1)} %get-tuple-element.17.refs_2_.refs_3_), custom_call_target="tpu_custom_call" | custom-call | tf_op jit(solution)/shard_map/near_stage/pallas_call | solution.py:271
  13.1 0.0 collective-permute-done.1.refs_0_
  13.2 3.8 %collective-permute-done.3.refs_1_ = bf16[8,32,256]{2,1,0:T(8,128)(2,1)S(1)} collective-permute-done((bf16[8,32,256]{2,1,0:T(8,128)(2,1)}, bf16[8,32,256]{2,1,0:T(8,128)(2,1)S(1)}, u32[]{:S(2)}, u32[]{:S(2)}) %collective-permute-start.3) | collective-permute-done | bytes 131104 | tf_op jit(solution)/shard_map/ppermute | solution.py:222
  16.9 0.0 collective-permute-start.6
  16.9 0.5 %collective-permute-start.5 = (bf16[8,32,256]{2,1,0:T(8,128)(2,1)S(1)}, bf16[8,32,256]{2,1,0:T(8,128)(2,1)S(1)}, u32[]{:S(2)}, u32[]{:S(2)}) collective-permute-start(bf16[8,32,256]{2,1,0:T(8,128)(2,1)S(1)} %collective-permute-done.1.refs_0_), channel_id=1, source_target_pairs={{0,4},{4,0},{8,12},{12,8},{16,20},{20,16},{24,28},{28,24},{1,5},{5... | collective-permute-start | bytes 393224 | tf_op jit(solution)/shard_map/ppermute | solution.py:222
  17.4 1.2 %near_stage.4.refs_4_ = f32[8,32,512]{2,1,0:T(8,128)S(1)} custom-call(s32[512]{0:T(512)S(4)} %get-tuple-element.16.plan, bf16[8,32,256]{2,1,0:T(8,128)(2,1)S(1)} %collective-permute-done.1.refs_0_, bf16[8,32,256]{2,1,0:T(8,128)(2,1)S(1)} %collective-permute-done.3.refs_1_, bf16[48,256,512]{2,1,0:T(8,128)(2,1)S(1)} %get-tuple-element.17.refs_2_.refs_3_, ...), custom_call_target="tpu_custom_call" | custom-call | tf_op jit(solution)/shard_map/near_stage/pallas_call | solution.py:271
  18.6 0.0 collective-permute-done.refs_2_
  18.6 0.1 collective-permute-start.4
  18.7 0.0 collective-permute-done.6.refs_1_
  18.7 0.0 collective-permute-done.5.refs_0_
  18.7 1.2 %near_stage.5.refs_3_ = f32[8,32,512]{2,1,0:T(8,128)S(1)} custom-call(s32[512]{0:T(512)S(4)} %get-tuple-element.16.plan, bf16[8,32,256]{2,1,0:T(8,128)(2,1)S(1)} %collective-permute-done.5.refs_0_, bf16[8,32,256]{2,1,0:T(8,128)(2,1)S(1)} %collective-permute-done.6.refs_1_, bf16[8,32,256]{2,1,0:T(8,128)(2,1)S(1)} %collective-permute-done.refs_2_, ...), custom_call_target="tpu_custom_call" | custom-call | tf_op jit(solution)/shard_map/near_stage/pallas_call | solution.py:271
  20.0 0.1 collective-permute-done.4.refs_0_
  20.1 1.0 %field_stage.1 = (f32[8,32,256]{2,1,0:T(8,128)S(1)}, f32[8,256]{1,0:T(8,128)S(1)}, f32[128,256]{1,0:T(8,128)S(1)}, f32[128,256]{1,0:T(8,128)S(1)}) custom-call(s32[512]{0:T(512)S(4)} %get-tuple-element.16.plan, bf16[8,32,256]{2,1,0:T(8,128)(2,1)S(1)} %collective-permute-done.4.refs_0_, bf16[8,32,256]{2,1,0:T(8,128)(2,1)S(1)} %copy-done, ...), custom_call_target="tpu_custom_call" | custom-call | tf_op jit(solution)/shard_map/field_stage/pallas_call | solution.py:290
  21.1 2.2 %collective-permute-start.7 = (f32[8,256]{1,0:T(8,128)S(1)}, f32[8,256]{1,0:T(8,128)S(1)}, u32[]{:S(2)}, u32[]{:S(2)}) collective-permute-start(f32[8,256]{1,0:T(8,128)S(1)} %get-tuple-element.27.refs_0_), channel_id=1, source_target_pairs={{0,3},{1,2},{2,1},{3,0},{4,7},{5,6},{6,5},{7,4},{8,11},{9,10},{10,... | collective-permute-start | bytes 24584 | tf_op jit(solution)/shard_map/ppermute | solution.py:222
  23.2 1.3 %collective-permute-start.8 = (f32[8,256]{1,0:T(8,128)S(1)}, f32[8,256]{1,0:T(8,128)S(1)}, u32[]{:S(2)}, u32[]{:S(2)}) collective-permute-start(f32[8,256]{1,0:T(8,128)S(1)} %get-tuple-element.27.refs_0_), channel_id=1, source_target_pairs={{0,2},{1,3},{2,0},{3,1},{4,6},{5,7},{6,4},{7,5},{8,10},{9,11},{10,... | collective-permute-start | bytes 24584 | tf_op jit(solution)/shard_map/ppermute | solution.py:222
  24.5 0.1 collective-permute-start.9
  24.6 0.7 %copy.10 = f32[8,32,256]{2,1,0:T(8,128)} copy(f32[8,32,256]{2,1,0:T(8,128)S(1)} %get-tuple-element.30) | data formatting | bytes 524288
  25.3 0.4 %collective-permute-done.7.refs_1_ = f32[8,256]{1,0:T(8,128)S(1)} collective-permute-done((f32[8,256]{1,0:T(8,128)S(1)}, f32[8,256]{1,0:T(8,128)S(1)}, u32[]{:S(2)}, u32[]{:S(2)}) %collective-permute-start.7) | collective-permute-done | bytes 8224 | tf_op jit(solution)/shard_map/ppermute | solution.py:222
  25.7 1.2 %collective-permute-done.8.refs_2_ = f32[8,256]{1,0:T(8,128)S(1)} collective-permute-done((f32[8,256]{1,0:T(8,128)S(1)}, f32[8,256]{1,0:T(8,128)S(1)}, u32[]{:S(2)}, u32[]{:S(2)}) %collective-permute-start.8) | collective-permute-done | bytes 8224 | tf_op jit(solution)/shard_map/ppermute | solution.py:222
  26.9 1.3 %collective-permute-done.9.refs_3_ = f32[8,256]{1,0:T(8,128)S(1)} collective-permute-done((f32[8,256]{1,0:T(8,128)S(1)}, f32[8,256]{1,0:T(8,128)S(1)}, u32[]{:S(2)}, u32[]{:S(2)}) %collective-permute-start.9) | collective-permute-done | bytes 8224 | tf_op jit(solution)/shard_map/ppermute | solution.py:222
  28.2 0.9 %gradient_stage.1 = f32[8,256]{1,0:T(8,128)} custom-call(f32[8,256]{1,0:T(8,128)S(1)} %get-tuple-element.27.refs_0_, f32[8,256]{1,0:T(8,128)S(1)} %collective-permute-done.7.refs_1_, f32[8,256]{1,0:T(8,128)S(1)} %collective-permute-done.8.refs_2_, f32[8,256]{1,0:T(8,128)S(1)} %collective-permute-done.9.refs_3_, f32[64,256]{1,0:T(8,128)S(1)} %get-tuple-element.24.refs_4_, ...), custom_call_target="tpu_custom_call" | custom-call | tf_op jit(solution)/shard_map/gradient_stage/pallas_call | solution.py:309
Async XLA Ops:
  0.6 11.3 %copy-start = (bf16[8,32,256]{2,1,0:T(8,128)(2,1)S(1)}, bf16[8,32,256]{2,1,0:T(8,128)(2,1)}, u32[]{:S(2)}) copy-start(bf16[8,32,256]{2,1,0:T(8,128)(2,1)} %refs_1_.1) | copy-start | bytes 393220
  0.6 11.3 %collective-permute-start.2 = (bf16[8,32,256]{2,1,0:T(8,128)(2,1)}, bf16[8,32,256]{2,1,0:T(8,128)(2,1)S(1)}, u32[]{:S(2)}, u32[]{:S(2)}) collective-permute-start(bf16[8,32,256]{2,1,0:T(8,128)(2,1)} %refs_1_.1), channel_id=1, source_target_pairs={{0,4},{4,0},{8,12},{12,8},{16,20},{20,16},{24,28},{28,24},{1,5},{5... | collective-permute-start | bytes 393224 | tf_op jit(solution)/shard_map/ppermute | solution.py:222
  1.2 12.0 %collective-permute-start.1 = (bf16[8,32,256]{2,1,0:T(8,128)(2,1)}, bf16[8,32,256]{2,1,0:T(8,128)(2,1)S(1)}, u32[]{:S(2)}, u32[]{:S(2)}) collective-permute-start(bf16[8,32,256]{2,1,0:T(8,128)(2,1)} %refs_1_.1), channel_id=1, source_target_pairs={{0,8},{4,12},{8,0},{12,4},{16,24},{20,28},{24,16},{28,20},{1,9},{5... | collective-permute-start | bytes 393224 | tf_op jit(solution)/shard_map/ppermute | solution.py:222
  3.8 13.1 %collective-permute-start.3 = (bf16[8,32,256]{2,1,0:T(8,128)(2,1)}, bf16[8,32,256]{2,1,0:T(8,128)(2,1)S(1)}, u32[]{:S(2)}, u32[]{:S(2)}) collective-permute-start(bf16[8,32,256]{2,1,0:T(8,128)(2,1)} %refs_1_.1), channel_id=1, source_target_pairs={{0,16},{4,20},{8,24},{12,28},{16,0},{20,4},{24,8},{28,12},{1,17},{... | collective-permute-start | bytes 393224 | tf_op jit(solution)/shard_map/ppermute | solution.py:222
  6.4 12.2 %collective-permute-start = (bf16[8,32,256]{2,1,0:T(8,128)(2,1)}, bf16[8,32,256]{2,1,0:T(8,128)(2,1)S(1)}, u32[]{:S(2)}, u32[]{:S(2)}) collective-permute-start(bf16[8,32,256]{2,1,0:T(8,128)(2,1)} %refs_1_.1), channel_id=1, source_target_pairs={{0,24},{4,28},{8,16},{12,20},{16,8},{20,12},{24,0},{28,4},{1,25},{... | collective-permute-start | bytes 393224 | tf_op jit(solution)/shard_map/ppermute | solution.py:222
  16.9 1.8 %collective-permute-start.6 = (bf16[8,32,256]{2,1,0:T(8,128)(2,1)S(1)}, bf16[8,32,256]{2,1,0:T(8,128)(2,1)S(1)}, u32[]{:S(2)}, u32[]{:S(2)}) collective-permute-start(bf16[8,32,256]{2,1,0:T(8,128)(2,1)S(1)} %collective-permute-done.3.refs_1_), channel_id=1, source_target_pairs={{0,4},{4,0},{8,12},{12,8},{16,20},{20,16},{24,28},{28,24},{1,5},{5... | collective-permute-start | bytes 393224 | tf_op jit(solution)/shard_map/ppermute | solution.py:222
  16.9 1.8 %collective-permute-start.5 = (bf16[8,32,256]{2,1,0:T(8,128)(2,1)S(1)}, bf16[8,32,256]{2,1,0:T(8,128)(2,1)S(1)}, u32[]{:S(2)}, u32[]{:S(2)}) collective-permute-start(bf16[8,32,256]{2,1,0:T(8,128)(2,1)S(1)} %collective-permute-done.1.refs_0_), channel_id=1, source_target_pairs={{0,4},{4,0},{8,12},{12,8},{16,20},{20,16},{24,28},{28,24},{1,5},{5... | collective-permute-start | bytes 393224 | tf_op jit(solution)/shard_map/ppermute | solution.py:222
  18.6 1.4 %collective-permute-start.4 = (bf16[8,32,256]{2,1,0:T(8,128)(2,1)S(1)}, bf16[8,32,256]{2,1,0:T(8,128)(2,1)S(1)}, u32[]{:S(2)}, u32[]{:S(2)}) collective-permute-start(bf16[8,32,256]{2,1,0:T(8,128)(2,1)S(1)} %collective-permute-done.refs_2_), channel_id=1, source_target_pairs={{0,4},{4,0},{8,12},{12,8},{16,20},{20,16},{24,28},{28,24},{1,5},{5... | collective-permute-start | bytes 393224 | tf_op jit(solution)/shard_map/ppermute | solution.py:222
  21.1 4.6 %collective-permute-start.7 = (f32[8,256]{1,0:T(8,128)S(1)}, f32[8,256]{1,0:T(8,128)S(1)}, u32[]{:S(2)}, u32[]{:S(2)}) collective-permute-start(f32[8,256]{1,0:T(8,128)S(1)} %get-tuple-element.27.refs_0_), channel_id=1, source_target_pairs={{0,3},{1,2},{2,1},{3,0},{4,7},{5,6},{6,5},{7,4},{8,11},{9,10},{10,... | collective-permute-start | bytes 24584 | tf_op jit(solution)/shard_map/ppermute | solution.py:222
  23.2 3.7 %collective-permute-start.8 = (f32[8,256]{1,0:T(8,128)S(1)}, f32[8,256]{1,0:T(8,128)S(1)}, u32[]{:S(2)}, u32[]{:S(2)}) collective-permute-start(f32[8,256]{1,0:T(8,128)S(1)} %get-tuple-element.27.refs_0_), channel_id=1, source_target_pairs={{0,2},{1,3},{2,0},{3,1},{4,6},{5,7},{6,4},{7,5},{8,10},{9,11},{10,... | collective-permute-start | bytes 24584 | tf_op jit(solution)/shard_map/ppermute | solution.py:222
  24.5 3.7 %collective-permute-start.9 = (f32[8,256]{1,0:T(8,128)S(1)}, f32[8,256]{1,0:T(8,128)S(1)}, u32[]{:S(2)}, u32[]{:S(2)}) collective-permute-start(f32[8,256]{1,0:T(8,128)S(1)} %get-tuple-element.27.refs_0_), channel_id=1, source_target_pairs={{0,1},{1,0},{2,3},{3,2},{4,5},{5,4},{6,7},{7,6},{8,9},{9,8},{10,11... | collective-permute-start | bytes 24584 | tf_op jit(solution)/shard_map/ppermute | solution.py:222

commit v4 on v3

--- a/solution.py
+++ b/solution.py
@@ -10,12 +10,12 @@
 PD = 4
 EPSILON = 1e-05
 UNROLL = 4
-COPIES = 8
 MOMENTS = 8
 F32 = jnp.float32
 BF16 = jnp.bfloat16
 VMEM_LIMIT = 8 << 20
-FIRST_LIMIT = 44 << 20
+LOAD_LIMIT = 44 << 20
+COPIES = 8
 
 VMEM_SPEC = pl.BlockSpec(memory_space=pltpu.VMEM)
 SMEM_SPEC = pl.BlockSpec(memory_space=pltpu.SMEM)
@@ -63,9 +63,17 @@
     held[len(sources) * depth] = jnp.zeros(held.shape[1:], held.dtype)
 
 
-def add_stage(stage, width, plan, held, tiles, total):
+def add_stage(stage, region, plan, held, tiles, total):
+    count = plan[3 * (plan.shape[0] // 4) + stage]
+    add_groups(stage, region, 0, (count + UNROLL - 1) // UNROLL, plan, held, tiles, total)
+
+
+def add_groups(stage, region, begin, end, plan, held, tiles, total):
+    width = plan.shape[0] // 4
+    start = stage * region
+
     def body(step, carry):
-        base = step * UNROLL
+        base = start + step * UNROLL
         images = [
             dot(held[plan[width + base + lane]], tiles[plan[base + lane]])
             for lane in range(UNROLL)
@@ -75,39 +83,57 @@
             total[target] += images[lane]
         return carry
 
-    lax.fori_loop(plan[3 * width + stage], plan[3 * width + stage + 1], body, 0)
+    lax.fori_loop(begin, end, body, 0)
 
 
 def load_kernel(
-    bounds, width, freq_count, src, dst, owner, slot, place, areas, tiles,
-    held_tiles, basis, spread, plan, sems,
+    stages, region, freq_count, src, dst, owner, slot, panels, place, areas, tiles,
+    plan, held_tiles, total, basis, spread, held, sems,
 ):
     tile_count = tiles.shape[0]
-    block_count = areas.shape[0]
-    per_copy = tile_count // COPIES
-    copies = [
-        pltpu.make_async_copy(
-            tiles.at[pl.ds(i * per_copy, per_copy)],
-            held_tiles.at[pl.ds(i * per_copy, per_copy)],
-            sems.at[i],
-        )
-        for i in range(COPIES)
-    ]
+    edges = [tile_count * i // COPIES for i in range(COPIES + 1)]
+    copies = []
+    for i in range(COPIES):
+        span = pl.ds(edges[i], edges[i + 1] - edges[i])
+        copies.append(pltpu.make_async_copy(tiles.at[span], held_tiles.at[span], sems.at[i]))
     for copy in copies:
         copy.start()
+    block_count = areas.shape[0]
+    width = plan.shape[0] // 4
     me = lax.axis_index("row")
-    position = jnp.int32(0)
-    for stage, hops in enumerate(bounds):
-        plan[3 * width + stage] = position // UNROLL
-        position = lax.fori_loop(
-            0, tile_count, functools.partial(place_tile, width, hops, block_count, me, src, dst, plan), position
-        )
+
+    def place_tile(t, counts):
+        source = src[t]
+        hop = (source // block_count) ^ me
+        target, here, row = jnp.int32(0), [], jnp.int32(0)
+        for stage, hops in enumerate(stages):
+            inside = hop == hops[0]
+            for index, other in enumerate(hops[1:], 1):
+                inside = inside | (hop == other)
+                row = jnp.where(hop == other, index, row)
+            target = jnp.where(inside, stage * region + counts[stage], target)
+            here.append(inside)
+        plan[target] = t
+        plan[width + target] = row * block_count + source % block_count
+        plan[2 * width + target] = dst[t]
+        return tuple(count + inside.astype(jnp.int32) for count, inside in zip(counts, here))
+
+    counts = (jnp.int32(0),) * len(stages)
+    ready = []
+    for i in range(COPIES):
+        counts = lax.fori_loop(edges[i], edges[i + 1], place_tile, counts)
+        ready.append(counts[0] // UNROLL)
+    ready[-1] = (counts[0] + UNROLL - 1) // UNROLL
+    for stage, hops in enumerate(stages):
+        plan[3 * width + stage] = counts[stage]
+        loaded = plan[stage * region]
         for lane in range(UNROLL):
-            plan[position + lane] = 0
-            plan[width + position + lane] = len(hops) * block_count
-            plan[2 * width + position + lane] = 0
-        position = (position + UNROLL - 1) // UNROLL * UNROLL
-    plan[3 * width + len(bounds)] = position // UNROLL
+            position = stage * region + counts[stage] + lane
+            plan[position] = loaded
+            plan[width + position] = len(hops) * block_count
+            plan[2 * width + position] = 0
+    total[...] = jnp.zeros_like(total)
+    fill_panels([panels], held)
     nx, ny, nz, px, py, pz = [place[i] for i in range(6)]
     weight = areas[...]
     rows = [nx, ny, nz, py * nz - pz * ny, pz * nx - px * nz, px * ny - py * nx]
@@ -124,46 +150,28 @@
         spread[block * freq_count : (block + 1) * freq_count] = jnp.where(
             chosen, 1.0, 0.0
         ).astype(BF16)
-    for copy in copies:
+    begin = jnp.int32(0)
+    for copy, end in zip(copies, ready):
         copy.wait()
-
-
-def place_tile(width, hops, depth, me, src, dst, plan, t, position):
-    source = src[t]
-    hop = (source // depth) ^ me
-    here = hop == hops[0]
-    row = jnp.int32(0)
-    for index, other in enumerate(hops[1:], 1):
-        here = here | (hop == other)
-        row = jnp.where(hop == other, index, row)
-    plan[position] = t
-    plan[width + position] = row * depth + source % depth
-    plan[2 * width + position] = dst[t]
-    return position + here.astype(jnp.int32)
-
-
-def near_kernel(stage, width, count, begin, plan, *refs):
-    sources, refs = refs[:count], refs[count:]
-    tiles, refs = refs[0], refs[1:]
-    if begin:
-        total, held = refs
-        total[...] = jnp.zeros_like(total)
-    else:
-        start, total, held = refs
-        total[...] = start[...]
+        add_groups(0, region, begin, end, plan, held, held_tiles, total)
+        begin = end
+
+
+def near_kernel(stage, region, count, plan, *refs):
+    sources = refs[:count]
+    tiles, start, total, held = refs[count:]
     fill_panels(sources, held)
-    add_stage(stage, width, plan, held, tiles, total)
-
-
-def field_kernel(stage, width, count, plan, *refs):
+    add_stage(stage, region, plan, held, tiles, total)
+
+
+def field_kernel(stage, region, count, plan, *refs):
     sources = refs[:count]
     panels, tiles, start, basis, spread = refs[count : count + 5]
-    field, table, powers, crosses, held, total = refs[count + 5 :]
+    total, field, table, powers, crosses, held = refs[count + 5 :]
     block_count, rows_twice, node_count = panels.shape
     freq_count = rows_twice // 2
     fill_panels(sources, held)
-    total[...] = start[...]
-    add_stage(stage, width, plan, held, tiles, total)
+    add_stage(stage, region, plan, held, tiles, total)
     for block in range(block_count):
         image = total[block]
         incident = panels[block].astype(F32)
@@ -229,10 +237,16 @@
     row_count = lax.axis_size("row")
     group_count = lax.axis_size("col")
     particle_count = group_count * PD
-    direct = list(range(2, row_count, 2))
-    soon, late = direct[:-1], direct[-1]
-    stages = ([0, 1], soon, [hop + 1 for hop in soon] + [late], [late + 1])
-    width = -(-(tile_count + (len(stages) + 1) * UNROLL) // 128) * 128
+    first, late = row_count // 2, row_count - 2
+    others = [hop for hop in range(2, row_count, 2) if hop not in (first, late)]
+    stages = (
+        [0],
+        [first, *others],
+        [first + 1, *[hop + 1 for hop in others], late, 1],
+        [late + 1],
+    )
+    region = tile_count + UNROLL
+    width = -(-(len(stages) * region) // 128) * 128
     image_shape = (block_count, rows_twice, 2 * node_count)
     basis_shape = (MOMENTS * block_count, node_count)
     spread_shape = (block_count * freq_count, particle_count * freq_count)
@@ -243,43 +257,49 @@
         return pltpu.VMEM((len(stages[stage]) * block_count + 1, rows_twice, node_count), BF16)
 
     hops = {0: panels}
-    for hop in direct:
+    for hop in [first, *others, late, 1]:
         hops[hop] = exchange(panels, "row", hop)
-    hops[1] = exchange(panels, "row", 1)
-
-    held_tiles, basis, spread, plan = pl.pallas_call(
-        functools.partial(load_kernel, stages, width, freq_count),
+
+    plan, held_tiles, total, basis, spread = pl.pallas_call(
+        functools.partial(load_kernel, stages, region, freq_count),
         out_shape=(
+            pltpu.SMEM((4 * width,), jnp.int32),
             pltpu.VMEM(tiles.shape, tiles.dtype),
+            pltpu.VMEM(image_shape, F32),
             pltpu.VMEM(basis_shape, F32),
             pltpu.VMEM(spread_shape, BF16),
-            pltpu.SMEM((3 * width + 128,), jnp.int32),
         ),
-        in_specs=[SMEM_SPEC] * 4 + [VMEM_SPEC] * 2 + [HBM_SPEC],
-        out_specs=(VMEM_SPEC,) * 3 + (SMEM_SPEC,),
-        scratch_shapes=[pltpu.SemaphoreType.DMA((COPIES,))],
-        compiler_params=params(FIRST_LIMIT),
-        cost_estimate=pl.CostEstimate(
-            flops=0, bytes_accessed=2 * tiles.size * 2, transcendentals=0
-        ),
+        in_specs=[SMEM_SPEC] * 4 + [VMEM_SPEC] * 3 + [HBM_SPEC],
+        out_specs=(SMEM_SPEC,) + (VMEM_SPEC,) * 4,
+        scratch_shapes=[held(0), pltpu.SemaphoreType.DMA((COPIES,))],
+        compiler_params=params(LOAD_LIMIT),
+        cost_estimate=pl.CostEstimate(flops=0, bytes_accessed=tiles.size * 2, transcendentals=0),
         name="load_stage",
-    )(tile_src, tile_dst, block_owner[:, 0], block_slot, jnp.transpose(geometry, (1, 0, 2)), areas, tiles)
+    )(
+        tile_src,
+        tile_dst,
+        block_owner[:, 0],
+        block_slot,
+        panels,
+        jnp.transpose(geometry, (1, 0, 2)),
+        areas,
+        tiles,
+    )
 
     def near(stage, total):
-        begin = total is None
         sources = [hops[hop] for hop in stages[stage]]
         return pl.pallas_call(
-            functools.partial(near_kernel, stage, width, len(sources), begin),
+            functools.partial(near_kernel, stage, region, len(sources)),
             out_shape=pltpu.VMEM(image_shape, F32),
-            in_specs=[SMEM_SPEC] + [VMEM_SPEC] * (len(sources) + (1 if begin else 2)),
+            in_specs=[SMEM_SPEC] + [VMEM_SPEC] * (len(sources) + 2),
             out_specs=VMEM_SPEC,
             scratch_shapes=[held(stage)],
+            input_output_aliases={len(sources) + 2: 0},
             compiler_params=params(),
             name="near_stage",
-        )(plan, *sources, held_tiles, *([] if begin else [total]))
-
-    total = near(0, None)
-    for hop in soon:
+        )(plan, *sources, held_tiles, total)
+
+    for hop in [first, *others]:
         hops[hop], total = lax.optimization_barrier((hops[hop], total))
         hops[hop + 1] = exchange(hops[hop], "row", 1)
     total = near(1, total)
@@ -287,23 +307,25 @@
     hops[late + 1] = exchange(hops[late], "row", 1)
     total = near(2, total)
 
-    field, table, powers, crosses = pl.pallas_call(
-        functools.partial(field_kernel, 3, width, 1),
+    total, field, table, powers, crosses = pl.pallas_call(
+        functools.partial(field_kernel, 3, region, 1),
         out_shape=(
+            pltpu.VMEM(image_shape, F32),
             pltpu.VMEM(panels.shape, F32),
             pltpu.VMEM(table_shape, F32),
             pltpu.VMEM(power_shape, F32),
             pltpu.VMEM(power_shape, F32),
         ),
         in_specs=[SMEM_SPEC] + [VMEM_SPEC] * 6,
-        out_specs=(VMEM_SPEC,) * 4,
-        scratch_shapes=[held(3), pltpu.VMEM(image_shape, F32)],
+        out_specs=(VMEM_SPEC,) * 5,
+        scratch_shapes=[held(3)],
+        input_output_aliases={4: 0},
         compiler_params=params(),
         name="field_stage",
     )(plan, hops[late + 1], panels, held_tiles, total, basis, spread)
 
     tables = [table]
-    for hop in range(group_count - 1, 0, -1):
+    for hop in range(1, group_count):
         tables.append(exchange(table, "col", hop))
 
     gradient = pl.pallas_call(

time: 29 us -> 26.3 us (0.907)
  the two profiles are of different devices: /device:TPU:0 before, /device:TPU:20 now
where the time goes in v4:
time: 26.3 us; the launch traced here: 26.1 us
  Pallas kernels  10.5 us (40%)
  starting transfers between devices  7.65 us (29%)
  waiting for transfers between devices  6.57 us (25%)
  local copies, waits for them, and re-layouts  0.71 us (3%)
  between operations  0.69 us (3%)
    ppermute x10, starting transfers between devices, exchange(): return lax.ppermute(values, axis, pairs)  7.65 us
    ppermute x10, waiting for transfers between devices, exchange(): return lax.ppermute(values, axis, pairs)  6.57 us
    pallas_call x1, Pallas kernels, shards(): pl.pallas_call(functools.partial(load_kernel, stages, region, freq_count)...  5.94 us
    pallas_call x2, Pallas kernels, near(): pl.pallas_call(functools.partial(near_kernel, stage, region, len(sources)...  2.94 us
    pallas_call x1, Pallas kernels, shards(): pl.pallas_call(functools.partial(gradient_kernel, len(tables)), out_shape...  0.94 us
    unnamed x3, local copies, waits for them, and re-layouts  0.71 us
    pallas_call x1, Pallas kernels, shards(): pl.pallas_call(functools.partial(field_kernel, 3, region, 1), out_shape=(...  0.7 us
  transfers between devices with their start and end apart: 10, of which 4 were waited for; matrix products, arithmetic and copies ran while one was open for 3% of the time, Pallas kernels for 34%

profile of v4, /device:TPU:20, one launch (start us, length us, event | category | flops | bytes accessed | tf_op | source)
XLA Modules:
  0.0 26.1 jit_solution(12389943614991397650)
XLA Ops:
  0.6 0.4 %collective-permute-start.1 = (bf16[8,32,256]{2,1,0:T(8,128)(2,1)}, bf16[8,32,256]{2,1,0:T(8,128)(2,1)S(1)}, u32[]{:S(2)}, u32[]{:S(2)}) collective-permute-start(bf16[8,32,256]{2,1,0:T(8,128)(2,1)} %refs_1_.1), channel_id=1, source_target_pairs={{0,16},{4,20},{8,24},{12,28},{16,0},{20,4},{24,8},{28,12},{1,17},{... | collective-permute-start | bytes 393224 | tf_op jit(solution)/shard_map/ppermute | solution.py:230
  1.0 1.6 %collective-permute-start.2 = (bf16[8,32,256]{2,1,0:T(8,128)(2,1)}, bf16[8,32,256]{2,1,0:T(8,128)(2,1)S(1)}, u32[]{:S(2)}, u32[]{:S(2)}) collective-permute-start(bf16[8,32,256]{2,1,0:T(8,128)(2,1)} %refs_1_.1), channel_id=1, source_target_pairs={{0,8},{4,12},{8,0},{12,4},{16,24},{20,28},{24,16},{28,20},{1,9},{5... | collective-permute-start | bytes 393224 | tf_op jit(solution)/shard_map/ppermute | solution.py:230
  2.6 1.6 %collective-permute-start = (bf16[8,32,256]{2,1,0:T(8,128)(2,1)}, bf16[8,32,256]{2,1,0:T(8,128)(2,1)S(1)}, u32[]{:S(2)}, u32[]{:S(2)}) collective-permute-start(bf16[8,32,256]{2,1,0:T(8,128)(2,1)} %refs_1_.1), channel_id=1, source_target_pairs={{0,24},{4,28},{8,16},{12,20},{16,8},{20,12},{24,0},{28,4},{1,25},{... | collective-permute-start | bytes 393224 | tf_op jit(solution)/shard_map/ppermute | solution.py:230
  4.2 0.0 collective-permute-start.6
  4.2 5.9 %load_stage.1 = (s32[1024]{0:T(1024)S(4)}, bf16[48,256,512]{2,1,0:T(8,128)(2,1)S(1)}, f32[8,32,512]{2,1,0:T(8,128)S(1)}, f32[64,256]{1,0:T(8,128)S(1)}, bf16[128,256]{1,0:T(8,128)(2,1)S(1)}) custom-call(s32[48]{0:T(128)} %src.1, s32[48]{0:T(128)} %dst.1, s32[8]{0:T(128)} %bitcast.3, s32[8]{0:T(128)} %slot.1, bf16[8,32,256]{2,1,0:T(8,128)(2,1)} %refs_1_.1, ...), custom_call_target="tpu_custom_call" | custom-call | bytes 12582912 | tf_op jit(solution)/shard_map/load_stage/pallas_call | solution.py:263
  10.1 0.0 collective-permute-done.1.refs_0_
  10.1 0.0 collective-permute-done.2.refs_1_
  10.2 0.3 %collective-permute-start.5 = (bf16[8,32,256]{2,1,0:T(8,128)(2,1)S(1)}, bf16[8,32,256]{2,1,0:T(8,128)(2,1)S(1)}, u32[]{:S(2)}, u32[]{:S(2)}) collective-permute-start(bf16[8,32,256]{2,1,0:T(8,128)(2,1)S(1)} %collective-permute-done.2.refs_1_), channel_id=1, source_target_pairs={{0,4},{4,0},{8,12},{12,8},{16,20},{20,16},{24,28},{28,24},{1,5},{5... | collective-permute-start | bytes 393224 | tf_op jit(solution)/shard_map/ppermute | solution.py:230
  10.4 0.3 %collective-permute-start.4 = (bf16[8,32,256]{2,1,0:T(8,128)(2,1)S(1)}, bf16[8,32,256]{2,1,0:T(8,128)(2,1)S(1)}, u32[]{:S(2)}, u32[]{:S(2)}) collective-permute-start(bf16[8,32,256]{2,1,0:T(8,128)(2,1)S(1)} %collective-permute-done.1.refs_0_), channel_id=1, source_target_pairs={{0,4},{4,0},{8,12},{12,8},{16,20},{20,16},{24,28},{28,24},{1,5},{5... | collective-permute-start | bytes 393224 | tf_op jit(solution)/shard_map/ppermute | solution.py:230
  10.7 0.0 copy-start
  10.7 0.9 %near_stage.2.refs_5_ = f32[8,32,512]{2,1,0:T(8,128)S(1)} custom-call(s32[1024]{0:T(1024)S(4)} %get-tuple-element.17.plan, bf16[8,32,256]{2,1,0:T(8,128)(2,1)S(1)} %collective-permute-done.1.refs_0_, bf16[8,32,256]{2,1,0:T(8,128)(2,1)S(1)} %collective-permute-done.2.refs_1_, ...), custom_call_target="tpu_custom_call", output_to_operand_aliasing={{}: (4, {})} | custom-call | tf_op jit(solution)/shard_map/near_stage/pallas_call | solution.py:291
  11.6 3.9 %collective-permute-done.refs_2_ = bf16[8,32,256]{2,1,0:T(8,128)(2,1)S(1)} collective-permute-done((bf16[8,32,256]{2,1,0:T(8,128)(2,1)}, bf16[8,32,256]{2,1,0:T(8,128)(2,1)S(1)}, u32[]{:S(2)}, u32[]{:S(2)}) %collective-permute-start) | collective-permute-done | bytes 131104 | tf_op jit(solution)/shard_map/ppermute | solution.py:230
  15.5 0.0 collective-permute-start.3
  15.5 0.0 collective-permute-done.6.refs_3_
  15.5 0.0 collective-permute-done.5.refs_1_
  15.5 0.0 collective-permute-done.4.refs_0_
  15.5 2.1 %near_stage.3.refs_3_ = f32[8,32,512]{2,1,0:T(8,128)S(1)} custom-call(s32[1024]{0:T(1024)S(4)} %get-tuple-element.17.plan, bf16[8,32,256]{2,1,0:T(8,128)(2,1)S(1)} %collective-permute-done.4.refs_0_, bf16[8,32,256]{2,1,0:T(8,128)(2,1)S(1)} %collective-permute-done.5.refs_1_, ...), custom_call_target="tpu_custom_call", output_to_operand_aliasing={{}: (6, {})} | custom-call | tf_op jit(solution)/shard_map/near_stage/pallas_call | solution.py:291
  17.6 0.0 collective-permute-done.3.refs_0_
  17.6 0.0 copy-done
  17.6 0.7 %field_stage.1 = (f32[8,32,512]{2,1,0:T(8,128)S(1)}, f32[8,32,256]{2,1,0:T(8,128)S(1)}, f32[8,256]{1,0:T(8,128)S(1)}, f32[128,256]{1,0:T(8,128)S(1)}, f32[128,256]{1,0:T(8,128)S(1)}) custom-call(s32[1024]{0:T(1024)S(4)} %get-tuple-element.17.plan, bf16[8,32,256]{2,1,0:T(8,128)(2,1)S(1)} %collective-permute-done.3.refs_0_, ...), custom_call_target="tpu_custom_call", output_to_operand_aliasing={{0}: (4, {})} | custom-call | tf_op jit(solution)/shard_map/field_stage/pallas_call | solution.py:310
  18.3 1.4 %collective-permute-start.9 = (f32[8,256]{1,0:T(8,128)S(1)}, f32[8,256]{1,0:T(8,128)S(1)}, u32[]{:S(2)}, u32[]{:S(2)}) collective-permute-start(f32[8,256]{1,0:T(8,128)S(1)} %get-tuple-element.29.refs_0_), channel_id=1, source_target_pairs={{0,3},{1,2},{2,1},{3,0},{4,7},{5,6},{6,5},{7,4},{8,11},{9,10},{10,... | collective-permute-start | bytes 24584 | tf_op jit(solution)/shard_map/ppermute | solution.py:230
  19.7 1.8 %collective-permute-start.8 = (f32[8,256]{1,0:T(8,128)S(1)}, f32[8,256]{1,0:T(8,128)S(1)}, u32[]{:S(2)}, u32[]{:S(2)}) collective-permute-start(f32[8,256]{1,0:T(8,128)S(1)} %get-tuple-element.29.refs_0_), channel_id=1, source_target_pairs={{0,2},{1,3},{2,0},{3,1},{4,6},{5,7},{6,4},{7,5},{8,10},{9,11},{10,... | collective-permute-start | bytes 24584 | tf_op jit(solution)/shard_map/ppermute | solution.py:230
  21.5 0.2 collective-permute-start.7
  21.8 0.7 %copy.16 = f32[8,32,256]{2,1,0:T(8,128)} copy(f32[8,32,256]{2,1,0:T(8,128)S(1)} %get-tuple-element.32) | data formatting | bytes 524288
  22.5 0.4 %collective-permute-done.9.refs_3_ = f32[8,256]{1,0:T(8,128)S(1)} collective-permute-done((f32[8,256]{1,0:T(8,128)S(1)}, f32[8,256]{1,0:T(8,128)S(1)}, u32[]{:S(2)}, u32[]{:S(2)}) %collective-permute-start.9) | collective-permute-done | bytes 8224 | tf_op jit(solution)/shard_map/ppermute | solution.py:230
  22.8 0.5 %collective-permute-done.8.refs_2_ = f32[8,256]{1,0:T(8,128)S(1)} collective-permute-done((f32[8,256]{1,0:T(8,128)S(1)}, f32[8,256]{1,0:T(8,128)S(1)}, u32[]{:S(2)}, u32[]{:S(2)}) %collective-permute-start.8) | collective-permute-done | bytes 8224 | tf_op jit(solution)/shard_map/ppermute | solution.py:230
  23.4 1.8 %collective-permute-done.7.refs_1_ = f32[8,256]{1,0:T(8,128)S(1)} collective-permute-done((f32[8,256]{1,0:T(8,128)S(1)}, f32[8,256]{1,0:T(8,128)S(1)}, u32[]{:S(2)}, u32[]{:S(2)}) %collective-permute-start.7) | collective-permute-done | bytes 8224 | tf_op jit(solution)/shard_map/ppermute | solution.py:230
  25.2 0.9 %gradient_stage.1 = f32[8,256]{1,0:T(8,128)} custom-call(f32[8,256]{1,0:T(8,128)S(1)} %get-tuple-element.29.refs_0_, f32[8,256]{1,0:T(8,128)S(1)} %collective-permute-done.7.refs_1_, f32[8,256]{1,0:T(8,128)S(1)} %collective-permute-done.8.refs_2_, f32[8,256]{1,0:T(8,128)S(1)} %collective-permute-done.9.refs_3_, f32[64,256]{1,0:T(8,128)S(1)} %get-tuple-element.26.refs_4_, ...), custom_call_target="tpu_custom_call" | custom-call | tf_op jit(solution)/shard_map/gradient_stage/pallas_call | solution.py:331
Async XLA Ops:
  0.6 9.5 %collective-permute-start.1 = (bf16[8,32,256]{2,1,0:T(8,128)(2,1)}, bf16[8,32,256]{2,1,0:T(8,128)(2,1)S(1)}, u32[]{:S(2)}, u32[]{:S(2)}) collective-permute-start(bf16[8,32,256]{2,1,0:T(8,128)(2,1)} %refs_1_.1), channel_id=1, source_target_pairs={{0,16},{4,20},{8,24},{12,28},{16,0},{20,4},{24,8},{28,12},{1,17},{... | collective-permute-start | bytes 393224 | tf_op jit(solution)/shard_map/ppermute | solution.py:230
  1.0 9.1 %collective-permute-start.2 = (bf16[8,32,256]{2,1,0:T(8,128)(2,1)}, bf16[8,32,256]{2,1,0:T(8,128)(2,1)S(1)}, u32[]{:S(2)}, u32[]{:S(2)}) collective-permute-start(bf16[8,32,256]{2,1,0:T(8,128)(2,1)} %refs_1_.1), channel_id=1, source_target_pairs={{0,8},{4,12},{8,0},{12,4},{16,24},{20,28},{24,16},{28,20},{1,9},{5... | collective-permute-start | bytes 393224 | tf_op jit(solution)/shard_map/ppermute | solution.py:230
  2.6 12.9 %collective-permute-start = (bf16[8,32,256]{2,1,0:T(8,128)(2,1)}, bf16[8,32,256]{2,1,0:T(8,128)(2,1)S(1)}, u32[]{:S(2)}, u32[]{:S(2)}) collective-permute-start(bf16[8,32,256]{2,1,0:T(8,128)(2,1)} %refs_1_.1), channel_id=1, source_target_pairs={{0,24},{4,28},{8,16},{12,20},{16,8},{20,12},{24,0},{28,4},{1,25},{... | collective-permute-start | bytes 393224 | tf_op jit(solution)/shard_map/ppermute | solution.py:230
  4.2 11.3 %collective-permute-start.6 = (bf16[8,32,256]{2,1,0:T(8,128)(2,1)}, bf16[8,32,256]{2,1,0:T(8,128)(2,1)S(1)}, u32[]{:S(2)}, u32[]{:S(2)}) collective-permute-start(bf16[8,32,256]{2,1,0:T(8,128)(2,1)} %refs_1_.1), channel_id=1, source_target_pairs={{0,4},{4,0},{8,12},{12,8},{16,20},{20,16},{24,28},{28,24},{1,5},{5... | collective-permute-start | bytes 393224 | tf_op jit(solution)/shard_map/ppermute | solution.py:230
  10.2 5.3 %collective-permute-start.5 = (bf16[8,32,256]{2,1,0:T(8,128)(2,1)S(1)}, bf16[8,32,256]{2,1,0:T(8,128)(2,1)S(1)}, u32[]{:S(2)}, u32[]{:S(2)}) collective-permute-start(bf16[8,32,256]{2,1,0:T(8,128)(2,1)S(1)} %collective-permute-done.2.refs_1_), channel_id=1, source_target_pairs={{0,4},{4,0},{8,12},{12,8},{16,20},{20,16},{24,28},{28,24},{1,5},{5... | collective-permute-start | bytes 393224 | tf_op jit(solution)/shard_map/ppermute | solution.py:230
  10.4 5.1 %collective-permute-start.4 = (bf16[8,32,256]{2,1,0:T(8,128)(2,1)S(1)}, bf16[8,32,256]{2,1,0:T(8,128)(2,1)S(1)}, u32[]{:S(2)}, u32[]{:S(2)}) collective-permute-start(bf16[8,32,256]{2,1,0:T(8,128)(2,1)S(1)} %collective-permute-done.1.refs_0_), channel_id=1, source_target_pairs={{0,4},{4,0},{8,12},{12,8},{16,20},{20,16},{24,28},{28,24},{1,5},{5... | collective-permute-start | bytes 393224 | tf_op jit(solution)/shard_map/ppermute | solution.py:230
  10.7 6.8 %copy-start = (bf16[8,32,256]{2,1,0:T(8,128)(2,1)S(1)}, bf16[8,32,256]{2,1,0:T(8,128)(2,1)}, u32[]{:S(2)}) copy-start(bf16[8,32,256]{2,1,0:T(8,128)(2,1)} %refs_1_.1) | copy-start | bytes 393220
  15.5 2.1 %collective-permute-start.3 = (bf16[8,32,256]{2,1,0:T(8,128)(2,1)S(1)}, bf16[8,32,256]{2,1,0:T(8,128)(2,1)S(1)}, u32[]{:S(2)}, u32[]{:S(2)}) collective-permute-start(bf16[8,32,256]{2,1,0:T(8,128)(2,1)S(1)} %collective-permute-done.refs_2_), channel_id=1, source_target_pairs={{0,4},{4,0},{8,12},{12,8},{16,20},{20,16},{24,28},{28,24},{1,5},{5... | collective-permute-start | bytes 393224 | tf_op jit(solution)/shard_map/ppermute | solution.py:230
  18.3 4.6 %collective-permute-start.9 = (f32[8,256]{1,0:T(8,128)S(1)}, f32[8,256]{1,0:T(8,128)S(1)}, u32[]{:S(2)}, u32[]{:S(2)}) collective-permute-start(f32[8,256]{1,0:T(8,128)S(1)} %get-tuple-element.29.refs_0_), channel_id=1, source_target_pairs={{0,3},{1,2},{2,1},{3,0},{4,7},{5,6},{6,5},{7,4},{8,11},{9,10},{10,... | collective-permute-start | bytes 24584 | tf_op jit(solution)/shard_map/ppermute | solution.py:230
  19.7 3.7 %collective-permute-start.8 = (f32[8,256]{1,0:T(8,128)S(1)}, f32[8,256]{1,0:T(8,128)S(1)}, u32[]{:S(2)}, u32[]{:S(2)}) collective-permute-start(f32[8,256]{1,0:T(8,128)S(1)} %get-tuple-element.29.refs_0_), channel_id=1, source_target_pairs={{0,2},{1,3},{2,0},{3,1},{4,6},{5,7},{6,4},{7,5},{8,10},{9,11},{10,... | collective-permute-start | bytes 24584 | tf_op jit(solution)/shard_map/ppermute | solution.py:230
  21.5 3.7 %collective-permute-start.7 = (f32[8,256]{1,0:T(8,128)S(1)}, f32[8,256]{1,0:T(8,128)S(1)}, u32[]{:S(2)}, u32[]{:S(2)}) collective-permute-start(f32[8,256]{1,0:T(8,128)S(1)} %get-tuple-element.29.refs_0_), channel_id=1, source_target_pairs={{0,1},{1,0},{2,3},{3,2},{4,5},{5,4},{6,7},{7,6},{8,9},{9,8},{10,11... | collective-permute-start | bytes 24584 | tf_op jit(solution)/shard_map/ppermute | solution.py:230

commit v5 on v4

--- a/solution.py
+++ b/solution.py
@@ -11,15 +11,19 @@
 EPSILON = 1e-05
 UNROLL = 4
 MOMENTS = 8
+SMALL = 1 << 16
 F32 = jnp.float32
 BF16 = jnp.bfloat16
 VMEM_LIMIT = 8 << 20
-LOAD_LIMIT = 44 << 20
-COPIES = 8
+EARLY_LIMIT = 44 << 20
 
 VMEM_SPEC = pl.BlockSpec(memory_space=pltpu.VMEM)
 SMEM_SPEC = pl.BlockSpec(memory_space=pltpu.SMEM)
 HBM_SPEC = pl.BlockSpec(memory_space=pltpu.HBM)
+
+
+def cost(size):
+    return pl.CostEstimate(flops=0, bytes_accessed=size, transcendentals=0)
 
 
 def params(limit=VMEM_LIMIT):
@@ -86,61 +90,39 @@
     lax.fori_loop(begin, end, body, 0)
 
 
-def load_kernel(
-    stages, region, freq_count, src, dst, owner, slot, panels, place, areas, tiles,
-    plan, held_tiles, total, basis, spread, held, sems,
-):
-    tile_count = tiles.shape[0]
-    edges = [tile_count * i // COPIES for i in range(COPIES + 1)]
-    copies = []
-    for i in range(COPIES):
-        span = pl.ds(edges[i], edges[i + 1] - edges[i])
-        copies.append(pltpu.make_async_copy(tiles.at[span], held_tiles.at[span], sems.at[i]))
-    for copy in copies:
-        copy.start()
-    block_count = areas.shape[0]
+def early_kernel(tiles, token):
+    token[...] = jnp.zeros_like(token)
+
+
+def plan_kernel(stages, region, freq_count, table, src, dst, owner, slot, token, plan, total, spread):
+    block_count = owner.shape[0]
     width = plan.shape[0] // 4
+    row_count = lax.axis_size("row")
     me = lax.axis_index("row")
 
     def place_tile(t, counts):
         source = src[t]
-        hop = (source // block_count) ^ me
-        target, here, row = jnp.int32(0), [], jnp.int32(0)
-        for stage, hops in enumerate(stages):
-            inside = hop == hops[0]
-            for index, other in enumerate(hops[1:], 1):
-                inside = inside | (hop == other)
-                row = jnp.where(hop == other, index, row)
-            target = jnp.where(inside, stage * region + counts[stage], target)
-            here.append(inside)
+        found = table[(source // block_count) ^ me]
+        target = jnp.int32(0)
+        for stage in range(len(stages)):
+            target = jnp.where(found // row_count == stage, stage * region + counts[stage], target)
         plan[target] = t
-        plan[width + target] = row * block_count + source % block_count
+        plan[width + target] = found % row_count * block_count + source % block_count
         plan[2 * width + target] = dst[t]
-        return tuple(count + inside.astype(jnp.int32) for count, inside in zip(counts, here))
-
-    counts = (jnp.int32(0),) * len(stages)
-    ready = []
-    for i in range(COPIES):
-        counts = lax.fori_loop(edges[i], edges[i + 1], place_tile, counts)
-        ready.append(counts[0] // UNROLL)
-    ready[-1] = (counts[0] + UNROLL - 1) // UNROLL
-    for stage, hops in enumerate(stages):
+        return tuple(
+            count + (found // row_count == stage).astype(jnp.int32)
+            for stage, count in enumerate(counts)
+        )
+
+    counts = lax.fori_loop(0, src.shape[0], place_tile, (jnp.int32(0),) * len(stages))
+    for stage, held in enumerate(stages):
         plan[3 * width + stage] = counts[stage]
-        loaded = plan[stage * region]
         for lane in range(UNROLL):
             position = stage * region + counts[stage] + lane
-            plan[position] = loaded
-            plan[width + position] = len(hops) * block_count
+            plan[position] = 0
+            plan[width + position] = len(held) * block_count
             plan[2 * width + position] = 0
     total[...] = jnp.zeros_like(total)
-    fill_panels([panels], held)
-    nx, ny, nz, px, py, pz = [place[i] for i in range(6)]
-    weight = areas[...]
-    rows = [nx, ny, nz, py * nz - pz * ny, pz * nx - px * nz, px * ny - py * nx]
-    for index, row in enumerate(rows):
-        basis[index * block_count : (index + 1) * block_count] = weight * row
-    for index in range(len(rows), MOMENTS):
-        basis[index * block_count : (index + 1) * block_count] = weight
     shape = (freq_count, spread.shape[1])
     lanes = lax.broadcasted_iota(jnp.int32, shape, 1)
     same = lanes % freq_count == lax.broadcasted_iota(jnp.int32, shape, 0)
@@ -150,11 +132,17 @@
         spread[block * freq_count : (block + 1) * freq_count] = jnp.where(
             chosen, 1.0, 0.0
         ).astype(BF16)
-    begin = jnp.int32(0)
-    for copy, end in zip(copies, ready):
-        copy.wait()
-        add_groups(0, region, begin, end, plan, held, held_tiles, total)
-        begin = end
+
+
+def basis_kernel(place, areas, basis):
+    block_count = areas.shape[0]
+    nx, ny, nz, px, py, pz = [place[i] for i in range(6)]
+    weight = areas[...]
+    rows = [nx, ny, nz, py * nz - pz * ny, pz * nx - px * nz, px * ny - py * nx]
+    for index, row in enumerate(rows):
+        basis[index * block_count : (index + 1) * block_count] = weight * row
+    for index in range(len(rows), MOMENTS):
+        basis[index * block_count : (index + 1) * block_count] = weight
 
 
 def near_kernel(stage, region, count, plan, *refs):
@@ -237,74 +225,88 @@
     row_count = lax.axis_size("row")
     group_count = lax.axis_size("col")
     particle_count = group_count * PD
-    first, late = row_count // 2, row_count - 2
-    others = [hop for hop in range(2, row_count, 2) if hop not in (first, late)]
-    stages = (
-        [0],
-        [first, *others],
-        [first + 1, *[hop + 1 for hop in others], late, 1],
-        [late + 1],
-    )
-    region = tile_count + UNROLL
-    width = -(-(len(stages) * region) // 128) * 128
     image_shape = (block_count, rows_twice, 2 * node_count)
     basis_shape = (MOMENTS * block_count, node_count)
     spread_shape = (block_count * freq_count, particle_count * freq_count)
     power_shape = (block_count * freq_count, node_count)
     table_shape = (MOMENTS, particle_count * freq_count)
-
-    def held(stage):
-        return pltpu.VMEM((len(stages[stage]) * block_count + 1, rows_twice, node_count), BF16)
-
-    hops = {0: panels}
-    for hop in [first, *others, late, 1]:
-        hops[hop] = exchange(panels, "row", hop)
-
-    plan, held_tiles, total, basis, spread = pl.pallas_call(
-        functools.partial(load_kernel, stages, region, freq_count),
+    region = tile_count + UNROLL
+
+    token = pl.pallas_call(
+        early_kernel,
+        out_shape=pltpu.VMEM((8, 128), F32),
+        in_specs=[HBM_SPEC],
+        out_specs=VMEM_SPEC,
+        compiler_params=params(EARLY_LIMIT),
+        cost_estimate=cost(4 * tiles.size),
+        name="early_stage",
+    )(tiles)
+
+    first, late = row_count // 2, row_count - 2
+    middle = [first, *[hop for hop in range(2, row_count, 2) if hop not in (first, late)]]
+    stages = ([0], [*middle, 1], [*[hop + 1 for hop in middle], late], [late + 1])
+    places = {
+        hop: stage * row_count + index
+        for stage, hops in enumerate(stages)
+        for index, hop in enumerate(hops)
+    }
+    table = jnp.array([places[hop] for hop in range(row_count)], jnp.int32)
+    width = -(-(len(stages) * region) // 128) * 128
+
+    arrived = {0: panels}
+    token, out = lax.optimization_barrier((token, panels))
+    for hop in [*middle, late, 1]:
+        arrived[hop] = exchange(out, "row", hop)
+
+    plan, total, spread = pl.pallas_call(
+        functools.partial(plan_kernel, stages, region, freq_count),
         out_shape=(
             pltpu.SMEM((4 * width,), jnp.int32),
-            pltpu.VMEM(tiles.shape, tiles.dtype),
             pltpu.VMEM(image_shape, F32),
-            pltpu.VMEM(basis_shape, F32),
             pltpu.VMEM(spread_shape, BF16),
         ),
-        in_specs=[SMEM_SPEC] * 4 + [VMEM_SPEC] * 3 + [HBM_SPEC],
-        out_specs=(SMEM_SPEC,) + (VMEM_SPEC,) * 4,
-        scratch_shapes=[held(0), pltpu.SemaphoreType.DMA((COPIES,))],
-        compiler_params=params(LOAD_LIMIT),
-        cost_estimate=pl.CostEstimate(flops=0, bytes_accessed=tiles.size * 2, transcendentals=0),
-        name="load_stage",
-    )(
-        tile_src,
-        tile_dst,
-        block_owner[:, 0],
-        block_slot,
-        panels,
-        jnp.transpose(geometry, (1, 0, 2)),
-        areas,
-        tiles,
-    )
+        in_specs=[SMEM_SPEC] * 5 + [VMEM_SPEC],
+        out_specs=(SMEM_SPEC,) + (VMEM_SPEC,) * 2,
+        compiler_params=params(),
+        cost_estimate=cost(4 * tiles.size),
+        name="plan_stage",
+    )(table, tile_src, tile_dst, block_owner[:, 0], block_slot, token)
 
     def near(stage, total):
-        sources = [hops[hop] for hop in stages[stage]]
+        sources = [arrived[hop] for hop in stages[stage]]
+        scratch = pltpu.VMEM((len(sources) * block_count + 1, rows_twice, node_count), BF16)
         return pl.pallas_call(
             functools.partial(near_kernel, stage, region, len(sources)),
             out_shape=pltpu.VMEM(image_shape, F32),
             in_specs=[SMEM_SPEC] + [VMEM_SPEC] * (len(sources) + 2),
             out_specs=VMEM_SPEC,
-            scratch_shapes=[held(stage)],
+            scratch_shapes=[scratch],
             input_output_aliases={len(sources) + 2: 0},
             compiler_params=params(),
+            cost_estimate=cost(SMALL),
             name="near_stage",
-        )(plan, *sources, held_tiles, total)
-
-    for hop in [first, *others]:
-        hops[hop], total = lax.optimization_barrier((hops[hop], total))
-        hops[hop + 1] = exchange(hops[hop], "row", 1)
+        )(plan, *sources, tiles, total)
+
+    def forward(hop, total):
+        arrived[hop], total = lax.optimization_barrier((arrived[hop], total))
+        arrived[hop + 1] = exchange(arrived[hop], "row", 1)
+        return total
+
+    total = near(0, total)
+    for hop in middle:
+        total = forward(hop, total)
     total = near(1, total)
-    hops[late], total = lax.optimization_barrier((hops[late], total))
-    hops[late + 1] = exchange(hops[late], "row", 1)
+    weights, total = lax.optimization_barrier((areas, total))
+    basis = pl.pallas_call(
+        basis_kernel,
+        out_shape=pltpu.VMEM(basis_shape, F32),
+        in_specs=[VMEM_SPEC] * 2,
+        out_specs=VMEM_SPEC,
+        compiler_params=params(),
+        cost_estimate=cost(SMALL),
+        name="basis_stage",
+    )(jnp.transpose(geometry, (1, 0, 2)), weights)
+    total = forward(late, total)
     total = near(2, total)
 
     total, field, table, powers, crosses = pl.pallas_call(
@@ -318,15 +320,16 @@
         ),
         in_specs=[SMEM_SPEC] + [VMEM_SPEC] * 6,
         out_specs=(VMEM_SPEC,) * 5,
-        scratch_shapes=[held(3)],
+        scratch_shapes=[pltpu.VMEM((block_count + 1, rows_twice, node_count), BF16)],
         input_output_aliases={4: 0},
         compiler_params=params(),
+        cost_estimate=cost(SMALL),
         name="field_stage",
-    )(plan, hops[late + 1], panels, held_tiles, total, basis, spread)
+    )(plan, arrived[late + 1], panels, tiles, total, basis, spread)
 
     tables = [table]
-    for hop in range(1, group_count):
-        tables.append(exchange(table, "col", hop))
+    for distance in range(1, group_count):
+        tables.append(exchange(table, "col", distance))
 
     gradient = pl.pallas_call(
         functools.partial(gradient_kernel, len(tables)),
@@ -334,6 +337,7 @@
         in_specs=[VMEM_SPEC] * (len(tables) + 4),
         out_specs=VMEM_SPEC,
         compiler_params=params(),
+        cost_estimate=cost(SMALL),
         name="gradient_stage",
     )(*tables, basis, spread, powers, crosses)
     return (field, gradient)

time: 26.3 us -> 26 us (0.989)
  the two profiles are of different devices: /device:TPU:20 before, /device:TPU:0 now
where the time goes in v5:
time: 26 us; the launch traced here: 26.1 us
  starting transfers between devices  9.82 us (38%)
  Pallas kernels  7.71 us (30%)
  waiting for transfers between devices  6.12 us (24%)
  local copies, waits for them, and re-layouts  1.64 us (6%)
  between operations  0.8 us (3%)
    ppermute x10, starting transfers between devices, exchange(): return lax.ppermute(values, axis, pairs)  9.82 us
    ppermute x10, waiting for transfers between devices, exchange(): return lax.ppermute(values, axis, pairs)  6.12 us
    pallas_call x3, Pallas kernels, near(): pl.pallas_call(functools.partial(near_kernel, stage, region, len(sources)...  3.52 us
    pallas_call x1, Pallas kernels, shards(): pl.pallas_call(functools.partial(plan_kernel, stages, region, freq_count)...  2.24 us
    unnamed x21, local copies, waits for them, and re-layouts  1.64 us
    pallas_call x1, Pallas kernels, shards(): pl.pallas_call(functools.partial(field_kernel, 3, region, 1), out_shape=(...  0.99 us
    pallas_call x1, Pallas kernels, shards(): pl.pallas_call(functools.partial(gradient_kernel, len(tables)), out_shape...  0.94 us
  transfers between devices with their start and end apart: 10, of which 5 were waited for; matrix products, arithmetic and copies ran while one was open for 3% of the time, Pallas kernels for 22%

profile of v5, /device:TPU:0, one launch (start us, length us, event | category | flops | bytes accessed | tf_op | source)
XLA Modules:
  0.0 26.1 jit_solution(16486328742533370898)
XLA Ops:
  0.6 0.0 copy-start.9
  0.6 0.0 copy-start
  0.7 0.0 copy-start.8
  0.7 4.1 %collective-permute-start.1 = (bf16[8,32,256]{2,1,0:T(8,128)(2,1)}, bf16[8,32,256]{2,1,0:T(8,128)(2,1)S(1)}, u32[]{:S(2)}, u32[]{:S(2)}) collective-permute-start(bf16[8,32,256]{2,1,0:T(8,128)(2,1)} %refs_1_.3), channel_id=1, source_target_pairs={{0,16},{4,20},{8,24},{12,28},{16,0},{20,4},{24,8},{28,12},{1,17},{... | collective-permute-start | bytes 393224 | tf_op jit(solution)/shard_map/ppermute | solution.py:218
  4.8 1.6 %collective-permute-start.2 = (bf16[8,32,256]{2,1,0:T(8,128)(2,1)}, bf16[8,32,256]{2,1,0:T(8,128)(2,1)S(1)}, u32[]{:S(2)}, u32[]{:S(2)}) collective-permute-start(bf16[8,32,256]{2,1,0:T(8,128)(2,1)} %refs_1_.3), channel_id=1, source_target_pairs={{0,8},{4,12},{8,0},{12,4},{16,24},{20,28},{24,16},{28,20},{1,9},{5... | collective-permute-start | bytes 393224 | tf_op jit(solution)/shard_map/ppermute | solution.py:218
  6.4 0.0 collective-permute-start.3
  6.4 0.0 collective-permute-start
  6.4 2.2 %plan_stage.1 = (s32[1024]{0:T(1024)S(4)}, f32[8,32,512]{2,1,0:T(8,128)S(1)}, bf16[128,256]{1,0:T(8,128)(2,1)S(1)}) custom-call(s32[8]{0:T(128)S(1)} %copy-done.9, s32[48]{0:T(128)S(1)} %copy-done.5, s32[48]{0:T(128)S(1)} %copy-done.6, s32[8]{0:T(128)S(1)} %bitcast.3, s32[8]{0:T(128)S(1)} %copy-done.8, f32[8,128]{1,0:T(8,128)S(1)} %early_stage.1.token), custom_call_target="tpu_custom_call" | custom-call | bytes 25165824 | tf_op jit(solution)/shard_map/plan_stage/pallas_call | solution.py:261
  8.7 0.0 copy-start.1
  8.7 0.9 %copy-done.1 = bf16[8,32,256]{2,1,0:T(8,128)(2,1)S(1)} copy-done((bf16[8,32,256]{2,1,0:T(8,128)(2,1)S(1)}, bf16[8,32,256]{2,1,0:T(8,128)(2,1)}, u32[]{:S(2)}) %copy-start.1) | copy-done | bytes 131096
  9.6 0.6 %near_stage.3.refs_4_ = f32[8,32,512]{2,1,0:T(8,128)S(1)} custom-call(s32[1024]{0:T(1024)S(4)} %get-tuple-element.20.plan, bf16[8,32,256]{2,1,0:T(8,128)(2,1)S(1)} %copy-done.1, bf16[48,256,512]{2,1,0:T(8,128)(2,1)S(1)} %copy-done, f32[8,32,512]{2,1,0:T(8,128)S(1)} %get-tuple-element.22.refs_2_), custom_call_target="tpu_custom_call", output_to_operand_aliasing={{}: (3, {})} | custom-call | bytes 65536 | tf_op jit(solution)/shard_map/near_stage/pallas_call | solution.py:278
  10.2 2.5 %collective-permute-done.1.refs_0_ = bf16[8,32,256]{2,1,0:T(8,128)(2,1)S(1)} collective-permute-done((bf16[8,32,256]{2,1,0:T(8,128)(2,1)}, bf16[8,32,256]{2,1,0:T(8,128)(2,1)S(1)}, u32[]{:S(2)}, u32[]{:S(2)}) %collective-permute-start.1) | collective-permute-done | bytes 131104 | tf_op jit(solution)/shard_map/ppermute | solution.py:218
  12.7 0.0 collective-permute-done.2.refs_1_
  12.7 0.0 collective-permute-start.6
  12.7 0.5 %collective-permute-start.5 = (bf16[8,32,256]{2,1,0:T(8,128)(2,1)S(1)}, bf16[8,32,256]{2,1,0:T(8,128)(2,1)S(1)}, u32[]{:S(2)}, u32[]{:S(2)}) collective-permute-start(bf16[8,32,256]{2,1,0:T(8,128)(2,1)S(1)} %collective-permute-done.1.refs_0_), channel_id=1, source_target_pairs={{0,4},{4,0},{8,12},{12,8},{16,20},{20,16},{24,28},{28,24},{1,5},{5... | collective-permute-start | bytes 393224 | tf_op jit(solution)/shard_map/ppermute | solution.py:218
  13.3 0.0 collective-permute-done.3.refs_2_
  13.3 1.5 %near_stage.4.refs_4_ = f32[8,32,512]{2,1,0:T(8,128)S(1)} custom-call(s32[1024]{0:T(1024)S(4)} %get-tuple-element.20.plan, bf16[8,32,256]{2,1,0:T(8,128)(2,1)S(1)} %collective-permute-done.1.refs_0_, bf16[8,32,256]{2,1,0:T(8,128)(2,1)S(1)} %collective-permute-done.2.refs_1_, ...), custom_call_target="tpu_custom_call", output_to_operand_aliasing={{}: (5, {})} | custom-call | bytes 65536 | tf_op jit(solution)/shard_map/near_stage/pallas_call | solution.py:278
  14.7 0.6 %collective-permute-done.refs_2_ = bf16[8,32,256]{2,1,0:T(8,128)(2,1)S(1)} collective-permute-done((bf16[8,32,256]{2,1,0:T(8,128)(2,1)}, bf16[8,32,256]{2,1,0:T(8,128)(2,1)S(1)}, u32[]{:S(2)}, u32[]{:S(2)}) %collective-permute-start) | collective-permute-done | bytes 131104 | tf_op jit(solution)/shard_map/ppermute | solution.py:218
  15.3 0.0 collective-permute-start.4
  15.4 0.0 collective-permute-done.6.refs_1_
  15.4 0.0 collective-permute-done.5.refs_0_
  15.4 1.5 %near_stage.5.refs_3_ = f32[8,32,512]{2,1,0:T(8,128)S(1)} custom-call(s32[1024]{0:T(1024)S(4)} %get-tuple-element.20.plan, bf16[8,32,256]{2,1,0:T(8,128)(2,1)S(1)} %collective-permute-done.5.refs_0_, bf16[8,32,256]{2,1,0:T(8,128)(2,1)S(1)} %collective-permute-done.6.refs_1_, ...), custom_call_target="tpu_custom_call", output_to_operand_aliasing={{}: (5, {})} | custom-call | bytes 65536 | tf_op jit(solution)/shard_map/near_stage/pallas_call | solution.py:278
  16.9 0.0 collective-permute-done.4.refs_0_
  16.9 1.0 %field_stage.1 = (f32[8,32,512]{2,1,0:T(8,128)S(1)}, f32[8,32,256]{2,1,0:T(8,128)S(1)}, f32[8,256]{1,0:T(8,128)S(1)}, f32[128,256]{1,0:T(8,128)S(1)}, f32[128,256]{1,0:T(8,128)S(1)}) custom-call(s32[1024]{0:T(1024)S(4)} %get-tuple-element.20.plan, bf16[8,32,256]{2,1,0:T(8,128)(2,1)S(1)} %collective-permute-done.4.refs_0_, ...), custom_call_target="tpu_custom_call", output_to_operand_aliasing={{0}: (4, {})} | custom-call | bytes 65536 | tf_op jit(solution)/shard_map/field_stage/pallas_call | solution.py:312
  17.9 2.6 %collective-permute-start.9 = (f32[8,256]{1,0:T(8,128)S(1)}, f32[8,256]{1,0:T(8,128)S(1)}, u32[]{:S(2)}, u32[]{:S(2)}) collective-permute-start(f32[8,256]{1,0:T(8,128)S(1)} %get-tuple-element.33.refs_0_), channel_id=1, source_target_pairs={{0,3},{1,2},{2,1},{3,0},{4,7},{5,6},{6,5},{7,4},{8,11},{9,10},{10,... | collective-permute-start | bytes 24584 | tf_op jit(solution)/shard_map/ppermute | solution.py:218
  20.4 1.1 %collective-permute-start.8 = (f32[8,256]{1,0:T(8,128)S(1)}, f32[8,256]{1,0:T(8,128)S(1)}, u32[]{:S(2)}, u32[]{:S(2)}) collective-permute-start(f32[8,256]{1,0:T(8,128)S(1)} %get-tuple-element.33.refs_0_), channel_id=1, source_target_pairs={{0,2},{1,3},{2,0},{3,1},{4,6},{5,7},{6,4},{7,5},{8,10},{9,11},{10,... | collective-permute-start | bytes 24584 | tf_op jit(solution)/shard_map/ppermute | solution.py:218
  21.5 0.0 collective-permute-start.7
  21.5 0.7 %copy.19 = f32[8,32,256]{2,1,0:T(8,128)} copy(f32[8,32,256]{2,1,0:T(8,128)S(1)} %get-tuple-element.36) | data formatting | bytes 524288
  22.2 0.2 collective-permute-done.9.refs_3_
  22.4 1.7 %collective-permute-done.8.refs_2_ = f32[8,256]{1,0:T(8,128)S(1)} collective-permute-done((f32[8,256]{1,0:T(8,128)S(1)}, f32[8,256]{1,0:T(8,128)S(1)}, u32[]{:S(2)}, u32[]{:S(2)}) %collective-permute-start.8) | collective-permute-done | bytes 8224 | tf_op jit(solution)/shard_map/ppermute | solution.py:218
  24.1 1.1 %collective-permute-done.7.refs_1_ = f32[8,256]{1,0:T(8,128)S(1)} collective-permute-done((f32[8,256]{1,0:T(8,128)S(1)}, f32[8,256]{1,0:T(8,128)S(1)}, u32[]{:S(2)}, u32[]{:S(2)}) %collective-permute-start.7) | collective-permute-done | bytes 8224 | tf_op jit(solution)/shard_map/ppermute | solution.py:218
  25.2 0.9 %gradient_stage.1 = f32[8,256]{1,0:T(8,128)} custom-call(f32[8,256]{1,0:T(8,128)S(1)} %get-tuple-element.33.refs_0_, f32[8,256]{1,0:T(8,128)S(1)} %collective-permute-done.7.refs_1_, f32[8,256]{1,0:T(8,128)S(1)} %collective-permute-done.8.refs_2_, f32[8,256]{1,0:T(8,128)S(1)} %collective-permute-done.9.refs_3_, f32[64,256]{1,0:T(8,128)S(1)} %basis_stage.1.refs_4_, ...), custom_call_target="tpu_custom_call" | custom-call | bytes 65536 | tf_op jit(solution)/shard_map/gradient_stage/pallas_call | solution.py:334
  (17 shorter events, 0.0 us)
Async XLA Ops:
  0.6 5.8 %copy-start.9 = (s32[8]{0:T(128)S(1)}, s32[8]{0:T(128)}, u32[]{:S(2)}) copy-start(s32[8]{0:T(128)} %constant.2.clone.table) | copy-start | bytes 100
  0.6 8.0 %copy-start = (bf16[48,256,512]{2,1,0:T(8,128)(2,1)S(1)}, bf16[48,256,512]{2,1,0:T(8,128)(2,1)}, u32[]{:S(2)}) copy-start(bf16[48,256,512]{2,1,0:T(8,128)(2,1)} %refs_2_.1) | copy-start | bytes 37748740
  0.7 5.7 %copy-start.8 = (s32[8]{0:T(128)S(1)}, s32[8]{0:T(128)}, u32[]{:S(2)}) copy-start(s32[8]{0:T(128)} %slot.1) | copy-start | bytes 100
  0.7 5.7 %copy-start.7 = (s32[8,1]{0,1:T(1,128)S(1)}, s32[8,1]{0,1:T(1,128)}, u32[]{:S(2)}) copy-start(s32[8,1]{0,1:T(1,128)} %param.15) | copy-start | bytes 100
  0.7 5.7 %copy-start.5 = (s32[48]{0:T(128)S(1)}, s32[48]{0:T(128)}, u32[]{:S(2)}) copy-start(s32[48]{0:T(128)} %src.1) | copy-start | bytes 580
  0.7 5.7 %copy-start.6 = (s32[48]{0:T(128)S(1)}, s32[48]{0:T(128)}, u32[]{:S(2)}) copy-start(s32[48]{0:T(128)} %dst.1) | copy-start | bytes 580
  0.7 12.0 %collective-permute-start.1 = (bf16[8,32,256]{2,1,0:T(8,128)(2,1)}, bf16[8,32,256]{2,1,0:T(8,128)(2,1)S(1)}, u32[]{:S(2)}, u32[]{:S(2)}) collective-permute-start(bf16[8,32,256]{2,1,0:T(8,128)(2,1)} %refs_1_.3), channel_id=1, source_target_pairs={{0,16},{4,20},{8,24},{12,28},{16,0},{20,4},{24,8},{28,12},{1,17},{... | collective-permute-start | bytes 393224 | tf_op jit(solution)/shard_map/ppermute | solution.py:218
  4.8 7.9 %collective-permute-start.2 = (bf16[8,32,256]{2,1,0:T(8,128)(2,1)}, bf16[8,32,256]{2,1,0:T(8,128)(2,1)S(1)}, u32[]{:S(2)}, u32[]{:S(2)}) collective-permute-start(bf16[8,32,256]{2,1,0:T(8,128)(2,1)} %refs_1_.3), channel_id=1, source_target_pairs={{0,8},{4,12},{8,0},{12,4},{16,24},{20,28},{24,16},{28,20},{1,9},{5... | collective-permute-start | bytes 393224 | tf_op jit(solution)/shard_map/ppermute | solution.py:218
  6.4 6.9 %collective-permute-start.3 = (bf16[8,32,256]{2,1,0:T(8,128)(2,1)}, bf16[8,32,256]{2,1,0:T(8,128)(2,1)S(1)}, u32[]{:S(2)}, u32[]{:S(2)}) collective-permute-start(bf16[8,32,256]{2,1,0:T(8,128)(2,1)} %refs_1_.3), channel_id=1, source_target_pairs={{0,4},{4,0},{8,12},{12,8},{16,20},{20,16},{24,28},{28,24},{1,5},{5... | collective-permute-start | bytes 393224 | tf_op jit(solution)/shard_map/ppermute | solution.py:218
  6.4 9.0 %collective-permute-start = (bf16[8,32,256]{2,1,0:T(8,128)(2,1)}, bf16[8,32,256]{2,1,0:T(8,128)(2,1)S(1)}, u32[]{:S(2)}, u32[]{:S(2)}) collective-permute-start(bf16[8,32,256]{2,1,0:T(8,128)(2,1)} %refs_1_.3), channel_id=1, source_target_pairs={{0,24},{4,28},{8,16},{12,20},{16,8},{20,12},{24,0},{28,4},{1,25},{... | collective-permute-start | bytes 393224 | tf_op jit(solution)/shard_map/ppermute | solution.py:218
  8.7 0.9 %copy-start.1 = (bf16[8,32,256]{2,1,0:T(8,128)(2,1)S(1)}, bf16[8,32,256]{2,1,0:T(8,128)(2,1)}, u32[]{:S(2)}) copy-start(bf16[8,32,256]{2,1,0:T(8,128)(2,1)} %refs_1_.3) | copy-start | bytes 393220
  9.6 5.8 %copy-start.3 = (f32[8,6,256]{2,0,1:T(8,128)S(1)}, f32[8,6,256]{2,0,1:T(8,128)}, u32[]{:S(2)}) copy-start(f32[8,6,256]{2,0,1:T(8,128)} %param.13) | copy-start | bytes 147460
  9.6 5.8 %copy-start.4 = (f32[8,256]{1,0:T(8,128)S(1)}, f32[8,256]{1,0:T(8,128)}, u32[]{:S(2)}) copy-start(f32[8,256]{1,0:T(8,128)} %areas) | copy-start | bytes 24580
  10.2 6.7 %copy-start.2 = (bf16[8,32,256]{2,1,0:T(8,128)(2,1)S(1)}, bf16[8,32,256]{2,1,0:T(8,128)(2,1)}, u32[]{:S(2)}) copy-start(bf16[8,32,256]{2,1,0:T(8,128)(2,1)} %refs_1_.3) | copy-start | bytes 393220
  12.7 2.6 %collective-permute-start.6 = (bf16[8,32,256]{2,1,0:T(8,128)(2,1)S(1)}, bf16[8,32,256]{2,1,0:T(8,128)(2,1)S(1)}, u32[]{:S(2)}, u32[]{:S(2)}) collective-permute-start(bf16[8,32,256]{2,1,0:T(8,128)(2,1)S(1)} %collective-permute-done.2.refs_1_), channel_id=1, source_target_pairs={{0,4},{4,0},{8,12},{12,8},{16,20},{20,16},{24,28},{28,24},{1,5},{5... | collective-permute-start | bytes 393224 | tf_op jit(solution)/shard_map/ppermute | solution.py:218
  12.7 2.6 %collective-permute-start.5 = (bf16[8,32,256]{2,1,0:T(8,128)(2,1)S(1)}, bf16[8,32,256]{2,1,0:T(8,128)(2,1)S(1)}, u32[]{:S(2)}, u32[]{:S(2)}) collective-permute-start(bf16[8,32,256]{2,1,0:T(8,128)(2,1)S(1)} %collective-permute-done.1.refs_0_), channel_id=1, source_target_pairs={{0,4},{4,0},{8,12},{12,8},{16,20},{20,16},{24,28},{28,24},{1,5},{5... | collective-permute-start | bytes 393224 | tf_op jit(solution)/shard_map/ppermute | solution.py:218
  15.3 1.5 %collective-permute-start.4 = (bf16[8,32,256]{2,1,0:T(8,128)(2,1)S(1)}, bf16[8,32,256]{2,1,0:T(8,128)(2,1)S(1)}, u32[]{:S(2)}, u32[]{:S(2)}) collective-permute-start(bf16[8,32,256]{2,1,0:T(8,128)(2,1)S(1)} %collective-permute-done.refs_2_), channel_id=1, source_target_pairs={{0,4},{4,0},{8,12},{12,8},{16,20},{20,16},{24,28},{28,24},{1,5},{5... | collective-permute-start | bytes 393224 | tf_op jit(solution)/shard_map/ppermute | solution.py:218
  17.9 4.6 %collective-permute-start.9 = (f32[8,256]{1,0:T(8,128)S(1)}, f32[8,256]{1,0:T(8,128)S(1)}, u32[]{:S(2)}, u32[]{:S(2)}) collective-permute-start(f32[8,256]{1,0:T(8,128)S(1)} %get-tuple-element.33.refs_0_), channel_id=1, source_target_pairs={{0,3},{1,2},{2,1},{3,0},{4,7},{5,6},{6,5},{7,4},{8,11},{9,10},{10,... | collective-permute-start | bytes 24584 | tf_op jit(solution)/shard_map/ppermute | solution.py:218
  20.4 3.7 %collective-permute-start.8 = (f32[8,256]{1,0:T(8,128)S(1)}, f32[8,256]{1,0:T(8,128)S(1)}, u32[]{:S(2)}, u32[]{:S(2)}) collective-permute-start(f32[8,256]{1,0:T(8,128)S(1)} %get-tuple-element.33.refs_0_), channel_id=1, source_target_pairs={{0,2},{1,3},{2,0},{3,1},{4,6},{5,7},{6,4},{7,5},{8,10},{9,11},{10,... | collective-permute-start | bytes 24584 | tf_op jit(solution)/shard_map/ppermute | solution.py:218
  21.5 3.7 %collective-permute-start.7 = (f32[8,256]{1,0:T(8,128)S(1)}, f32[8,256]{1,0:T(8,128)S(1)}, u32[]{:S(2)}, u32[]{:S(2)}) collective-permute-start(f32[8,256]{1,0:T(8,128)S(1)} %get-tuple-element.33.refs_0_), channel_id=1, source_target_pairs={{0,1},{1,0},{2,3},{3,2},{4,5},{5,4},{6,7},{7,6},{8,9},{9,8},{10,11... | collective-permute-start | bytes 24584 | tf_op jit(solution)/shard_map/ppermute | solution.py:218

commit v6 on v5

--- a/solution.py
+++ b/solution.py
@@ -9,7 +9,7 @@
 
 PD = 4
 EPSILON = 1e-05
-UNROLL = 4
+UNROLL = 8
 MOMENTS = 8
 SMALL = 1 << 16
 F32 = jnp.float32
@@ -68,26 +68,30 @@
 
 
 def add_stage(stage, region, plan, held, tiles, total):
-    count = plan[3 * (plan.shape[0] // 4) + stage]
-    add_groups(stage, region, 0, (count + UNROLL - 1) // UNROLL, plan, held, tiles, total)
-
-
-def add_groups(stage, region, begin, end, plan, held, tiles, total):
     width = plan.shape[0] // 4
-    start = stage * region
-
-    def body(step, carry):
-        base = start + step * UNROLL
+    count = plan[3 * width + stage]
+    whole = count // UNROLL
+
+    def add_group(base, size):
         images = [
             dot(held[plan[width + base + lane]], tiles[plan[base + lane]])
-            for lane in range(UNROLL)
+            for lane in range(size)
         ]
-        for lane in range(UNROLL):
+        for lane in range(size):
             target = plan[2 * width + base + lane]
             total[target] += images[lane]
+
+    def body(step, carry):
+        add_group(stage * region + step * UNROLL, UNROLL)
         return carry
 
-    lax.fori_loop(begin, end, body, 0)
+    lax.fori_loop(0, whole, body, 0)
+    left = count - whole * UNROLL
+    for size in range(2, UNROLL + 1, 2):
+
+        @pl.when((left > size - 2) & (left <= size))
+        def _(size=size):
+            add_group(stage * region + whole * UNROLL, size)
 
 
 def early_kernel(tiles, token):

time: 26 us -> 25.6 us (0.985); the launches traced: 26.1 us -> 25.2 us
  Pallas kernels: 7.71 us -> 6.73 us
    pallas_call x3, Pallas kernels: 3.52 us -> 2.63 us  [near(): pl.pallas_call(functools.partial(near_kernel, stage, region, len(sources)...]
  transfers between devices with their start and end apart: 10 -> 10, of which waited for: 5 -> 5; matrix products, arithmetic and copies ran while one was open for 3% -> 3% of each run, Pallas kernels for 22% -> 19%
where the time goes in v6:
time: 25.6 us; the launch traced here: 25.2 us
  starting transfers between devices  9.69 us (38%)
  Pallas kernels  6.73 us (26%)
  waiting for transfers between devices  6.31 us (25%)
  local copies, waits for them, and re-layouts  1.64 us (6%)
  between operations  0.79 us (3%)
    ppermute x10, starting transfers between devices, exchange(): return lax.ppermute(values, axis, pairs)  9.69 us
    ppermute x10, waiting for transfers between devices, exchange(): return lax.ppermute(values, axis, pairs)  6.31 us
    pallas_call x3, Pallas kernels, near(): pl.pallas_call(functools.partial(near_kernel, stage, region, len(sources)...  2.63 us
    pallas_call x1, Pallas kernels, shards(): pl.pallas_call(functools.partial(plan_kernel, stages, region, freq_count)...  2.26 us
    unnamed x21, local copies, waits for them, and re-layouts  1.64 us
    pallas_call x1, Pallas kernels, shards(): pl.pallas_call(functools.partial(gradient_kernel, len(tables)), out_shape...  0.94 us
    pallas_call x1, Pallas kernels, shards(): pl.pallas_call(functools.partial(field_kernel, 3, region, 1), out_shape=(...  0.88 us
  transfers between devices with their start and end apart: 10, of which 5 were waited for; matrix products, arithmetic and copies ran while one was open for 3% of the time, Pallas kernels for 19%

profile of v6, /device:TPU:0, one launch (start us, length us, event | category | flops | bytes accessed | tf_op | source)
XLA Modules:
  0.0 25.2 jit_solution(743048522691055654)
XLA Ops:
  0.6 0.0 copy-start.9
  0.7 4.1 %collective-permute-start.1 = (bf16[8,32,256]{2,1,0:T(8,128)(2,1)}, bf16[8,32,256]{2,1,0:T(8,128)(2,1)S(1)}, u32[]{:S(2)}, u32[]{:S(2)}) collective-permute-start(bf16[8,32,256]{2,1,0:T(8,128)(2,1)} %refs_1_.3), channel_id=1, source_target_pairs={{0,16},{4,20},{8,24},{12,28},{16,0},{20,4},{24,8},{28,12},{1,17},{... | collective-permute-start | bytes 393224 | tf_op jit(solution)/shard_map/ppermute | solution.py:222
  4.8 1.6 %collective-permute-start.2 = (bf16[8,32,256]{2,1,0:T(8,128)(2,1)}, bf16[8,32,256]{2,1,0:T(8,128)(2,1)S(1)}, u32[]{:S(2)}, u32[]{:S(2)}) collective-permute-start(bf16[8,32,256]{2,1,0:T(8,128)(2,1)} %refs_1_.3), channel_id=1, source_target_pairs={{0,8},{4,12},{8,0},{12,4},{16,24},{20,28},{24,16},{28,20},{1,9},{5... | collective-permute-start | bytes 393224 | tf_op jit(solution)/shard_map/ppermute | solution.py:222
  6.4 0.0 collective-permute-start.3
  6.4 0.0 collective-permute-start
  6.4 2.3 %plan_stage.1 = (s32[1024]{0:T(1024)S(4)}, f32[8,32,512]{2,1,0:T(8,128)S(1)}, bf16[128,256]{1,0:T(8,128)(2,1)S(1)}) custom-call(s32[8]{0:T(128)S(1)} %copy-done.9, s32[48]{0:T(128)S(1)} %copy-done.5, s32[48]{0:T(128)S(1)} %copy-done.6, s32[8]{0:T(128)S(1)} %bitcast.3, s32[8]{0:T(128)S(1)} %copy-done.8, f32[8,128]{1,0:T(8,128)S(1)} %early_stage.1.token), custom_call_target="tpu_custom_call" | custom-call | bytes 25165824 | tf_op jit(solution)/shard_map/plan_stage/pallas_call | solution.py:265
  8.7 0.0 copy-done
  8.7 0.0 copy-start.1
  8.7 0.9 %copy-done.1 = bf16[8,32,256]{2,1,0:T(8,128)(2,1)S(1)} copy-done((bf16[8,32,256]{2,1,0:T(8,128)(2,1)S(1)}, bf16[8,32,256]{2,1,0:T(8,128)(2,1)}, u32[]{:S(2)}) %copy-start.1) | copy-done | bytes 131096
  9.6 0.4 %near_stage.3.refs_4_ = f32[8,32,512]{2,1,0:T(8,128)S(1)} custom-call(s32[1024]{0:T(1024)S(4)} %get-tuple-element.20.plan, bf16[8,32,256]{2,1,0:T(8,128)(2,1)S(1)} %copy-done.1, bf16[48,256,512]{2,1,0:T(8,128)(2,1)S(1)} %copy-done, f32[8,32,512]{2,1,0:T(8,128)S(1)} %get-tuple-element.22.refs_2_), custom_call_target="tpu_custom_call", output_to_operand_aliasing={{}: (3, {})} | custom-call | bytes 65536 | tf_op jit(solution)/shard_map/near_stage/pallas_call | solution.py:282
  10.0 2.7 %collective-permute-done.1.refs_0_ = bf16[8,32,256]{2,1,0:T(8,128)(2,1)S(1)} collective-permute-done((bf16[8,32,256]{2,1,0:T(8,128)(2,1)}, bf16[8,32,256]{2,1,0:T(8,128)(2,1)S(1)}, u32[]{:S(2)}, u32[]{:S(2)}) %collective-permute-start.1) | collective-permute-done | bytes 131104 | tf_op jit(solution)/shard_map/ppermute | solution.py:222
  12.7 0.0 collective-permute-done.2.refs_1_
  12.7 0.0 collective-permute-start.6
  12.7 0.5 %collective-permute-start.5 = (bf16[8,32,256]{2,1,0:T(8,128)(2,1)S(1)}, bf16[8,32,256]{2,1,0:T(8,128)(2,1)S(1)}, u32[]{:S(2)}, u32[]{:S(2)}) collective-permute-start(bf16[8,32,256]{2,1,0:T(8,128)(2,1)S(1)} %collective-permute-done.1.refs_0_), channel_id=1, source_target_pairs={{0,4},{4,0},{8,12},{12,8},{16,20},{20,16},{24,28},{28,24},{1,5},{5... | collective-permute-start | bytes 393224 | tf_op jit(solution)/shard_map/ppermute | solution.py:222
  13.3 0.0 collective-permute-done.3.refs_2_
  13.3 1.0 %near_stage.4.refs_4_ = f32[8,32,512]{2,1,0:T(8,128)S(1)} custom-call(s32[1024]{0:T(1024)S(4)} %get-tuple-element.20.plan, bf16[8,32,256]{2,1,0:T(8,128)(2,1)S(1)} %collective-permute-done.1.refs_0_, bf16[8,32,256]{2,1,0:T(8,128)(2,1)S(1)} %collective-permute-done.2.refs_1_, ...), custom_call_target="tpu_custom_call", output_to_operand_aliasing={{}: (5, {})} | custom-call | bytes 65536 | tf_op jit(solution)/shard_map/near_stage/pallas_call | solution.py:282
  14.2 1.1 %collective-permute-done.refs_2_ = bf16[8,32,256]{2,1,0:T(8,128)(2,1)S(1)} collective-permute-done((bf16[8,32,256]{2,1,0:T(8,128)(2,1)}, bf16[8,32,256]{2,1,0:T(8,128)(2,1)S(1)}, u32[]{:S(2)}, u32[]{:S(2)}) %collective-permute-start) | collective-permute-done | bytes 131104 | tf_op jit(solution)/shard_map/ppermute | solution.py:222
  15.3 0.0 collective-permute-start.4
  15.4 0.0 copy-done.4
  15.4 0.0 collective-permute-done.6.refs_1_
  15.4 0.0 collective-permute-done.5.refs_0_
  15.4 1.3 %near_stage.5.refs_3_ = f32[8,32,512]{2,1,0:T(8,128)S(1)} custom-call(s32[1024]{0:T(1024)S(4)} %get-tuple-element.20.plan, bf16[8,32,256]{2,1,0:T(8,128)(2,1)S(1)} %collective-permute-done.5.refs_0_, bf16[8,32,256]{2,1,0:T(8,128)(2,1)S(1)} %collective-permute-done.6.refs_1_, ...), custom_call_target="tpu_custom_call", output_to_operand_aliasing={{}: (5, {})} | custom-call | bytes 65536 | tf_op jit(solution)/shard_map/near_stage/pallas_call | solution.py:282
  16.7 0.0 collective-permute-done.4.refs_0_
  16.7 0.9 %field_stage.1 = (f32[8,32,512]{2,1,0:T(8,128)S(1)}, f32[8,32,256]{2,1,0:T(8,128)S(1)}, f32[8,256]{1,0:T(8,128)S(1)}, f32[128,256]{1,0:T(8,128)S(1)}, f32[128,256]{1,0:T(8,128)S(1)}) custom-call(s32[1024]{0:T(1024)S(4)} %get-tuple-element.20.plan, bf16[8,32,256]{2,1,0:T(8,128)(2,1)S(1)} %collective-permute-done.4.refs_0_, ...), custom_call_target="tpu_custom_call", output_to_operand_aliasing={{0}: (4, {})} | custom-call | bytes 65536 | tf_op jit(solution)/shard_map/field_stage/pallas_call | solution.py:316
  17.6 2.7 %collective-permute-start.9 = (f32[8,256]{1,0:T(8,128)S(1)}, f32[8,256]{1,0:T(8,128)S(1)}, u32[]{:S(2)}, u32[]{:S(2)}) collective-permute-start(f32[8,256]{1,0:T(8,128)S(1)} %get-tuple-element.33.refs_0_), channel_id=1, source_target_pairs={{0,3},{1,2},{2,1},{3,0},{4,7},{5,6},{6,5},{7,4},{8,11},{9,10},{10,... | collective-permute-start | bytes 24584 | tf_op jit(solution)/shard_map/ppermute | solution.py:222
  20.2 0.3 %collective-permute-start.8 = (f32[8,256]{1,0:T(8,128)S(1)}, f32[8,256]{1,0:T(8,128)S(1)}, u32[]{:S(2)}, u32[]{:S(2)}) collective-permute-start(f32[8,256]{1,0:T(8,128)S(1)} %get-tuple-element.33.refs_0_), channel_id=1, source_target_pairs={{0,2},{1,3},{2,0},{3,1},{4,6},{5,7},{6,4},{7,5},{8,10},{9,11},{10,... | collective-permute-start | bytes 24584 | tf_op jit(solution)/shard_map/ppermute | solution.py:222
  20.6 0.5 %collective-permute-start.7 = (f32[8,256]{1,0:T(8,128)S(1)}, f32[8,256]{1,0:T(8,128)S(1)}, u32[]{:S(2)}, u32[]{:S(2)}) collective-permute-start(f32[8,256]{1,0:T(8,128)S(1)} %get-tuple-element.33.refs_0_), channel_id=1, source_target_pairs={{0,1},{1,0},{2,3},{3,2},{4,5},{5,4},{6,7},{7,6},{8,9},{9,8},{10,11... | collective-permute-start | bytes 24584 | tf_op jit(solution)/shard_map/ppermute | solution.py:222
  21.1 0.7 %copy.19 = f32[8,32,256]{2,1,0:T(8,128)} copy(f32[8,32,256]{2,1,0:T(8,128)S(1)} %get-tuple-element.36) | data formatting | bytes 524288
  21.8 0.4 %collective-permute-done.9.refs_3_ = f32[8,256]{1,0:T(8,128)S(1)} collective-permute-done((f32[8,256]{1,0:T(8,128)S(1)}, f32[8,256]{1,0:T(8,128)S(1)}, u32[]{:S(2)}, u32[]{:S(2)}) %collective-permute-start.9) | collective-permute-done | bytes 8224 | tf_op jit(solution)/shard_map/ppermute | solution.py:222
  22.1 1.7 %collective-permute-done.8.refs_2_ = f32[8,256]{1,0:T(8,128)S(1)} collective-permute-done((f32[8,256]{1,0:T(8,128)S(1)}, f32[8,256]{1,0:T(8,128)S(1)}, u32[]{:S(2)}, u32[]{:S(2)}) %collective-permute-start.8) | collective-permute-done | bytes 8224 | tf_op jit(solution)/shard_map/ppermute | solution.py:222
  23.9 0.3 %collective-permute-done.7.refs_1_ = f32[8,256]{1,0:T(8,128)S(1)} collective-permute-done((f32[8,256]{1,0:T(8,128)S(1)}, f32[8,256]{1,0:T(8,128)S(1)}, u32[]{:S(2)}, u32[]{:S(2)}) %collective-permute-start.7) | collective-permute-done | bytes 8224 | tf_op jit(solution)/shard_map/ppermute | solution.py:222
  24.2 0.9 %gradient_stage.1 = f32[8,256]{1,0:T(8,128)} custom-call(f32[8,256]{1,0:T(8,128)S(1)} %get-tuple-element.33.refs_0_, f32[8,256]{1,0:T(8,128)S(1)} %collective-permute-done.7.refs_1_, f32[8,256]{1,0:T(8,128)S(1)} %collective-permute-done.8.refs_2_, f32[8,256]{1,0:T(8,128)S(1)} %collective-permute-done.9.refs_3_, f32[64,256]{1,0:T(8,128)S(1)} %basis_stage.1.refs_4_, ...), custom_call_target="tpu_custom_call" | custom-call | bytes 65536 | tf_op jit(solution)/shard_map/gradient_stage/pallas_call | solution.py:338
  (17 shorter events, 0.0 us)
Async XLA Ops:
  0.6 5.8 %copy-start.9 = (s32[8]{0:T(128)S(1)}, s32[8]{0:T(128)}, u32[]{:S(2)}) copy-start(s32[8]{0:T(128)} %constant.2.clone.table) | copy-start | bytes 100
  0.6 8.1 %copy-start = (bf16[48,256,512]{2,1,0:T(8,128)(2,1)S(1)}, bf16[48,256,512]{2,1,0:T(8,128)(2,1)}, u32[]{:S(2)}) copy-start(bf16[48,256,512]{2,1,0:T(8,128)(2,1)} %refs_2_.1) | copy-start | bytes 37748740
  0.7 5.7 %copy-start.8 = (s32[8]{0:T(128)S(1)}, s32[8]{0:T(128)}, u32[]{:S(2)}) copy-start(s32[8]{0:T(128)} %slot.1) | copy-start | bytes 100
  0.7 5.7 %copy-start.7 = (s32[8,1]{0,1:T(1,128)S(1)}, s32[8,1]{0,1:T(1,128)}, u32[]{:S(2)}) copy-start(s32[8,1]{0,1:T(1,128)} %param.15) | copy-start | bytes 100
  0.7 5.7 %copy-start.5 = (s32[48]{0:T(128)S(1)}, s32[48]{0:T(128)}, u32[]{:S(2)}) copy-start(s32[48]{0:T(128)} %src.1) | copy-start | bytes 580
  0.7 5.7 %copy-start.6 = (s32[48]{0:T(128)S(1)}, s32[48]{0:T(128)}, u32[]{:S(2)}) copy-start(s32[48]{0:T(128)} %dst.1) | copy-start | bytes 580
  0.7 12.0 %collective-permute-start.1 = (bf16[8,32,256]{2,1,0:T(8,128)(2,1)}, bf16[8,32,256]{2,1,0:T(8,128)(2,1)S(1)}, u32[]{:S(2)}, u32[]{:S(2)}) collective-permute-start(bf16[8,32,256]{2,1,0:T(8,128)(2,1)} %refs_1_.3), channel_id=1, source_target_pairs={{0,16},{4,20},{8,24},{12,28},{16,0},{20,4},{24,8},{28,12},{1,17},{... | collective-permute-start | bytes 393224 | tf_op jit(solution)/shard_map/ppermute | solution.py:222
  4.8 7.9 %collective-permute-start.2 = (bf16[8,32,256]{2,1,0:T(8,128)(2,1)}, bf16[8,32,256]{2,1,0:T(8,128)(2,1)S(1)}, u32[]{:S(2)}, u32[]{:S(2)}) collective-permute-start(bf16[8,32,256]{2,1,0:T(8,128)(2,1)} %refs_1_.3), channel_id=1, source_target_pairs={{0,8},{4,12},{8,0},{12,4},{16,24},{20,28},{24,16},{28,20},{1,9},{5... | collective-permute-start | bytes 393224 | tf_op jit(solution)/shard_map/ppermute | solution.py:222
  6.4 6.9 %collective-permute-start.3 = (bf16[8,32,256]{2,1,0:T(8,128)(2,1)}, bf16[8,32,256]{2,1,0:T(8,128)(2,1)S(1)}, u32[]{:S(2)}, u32[]{:S(2)}) collective-permute-start(bf16[8,32,256]{2,1,0:T(8,128)(2,1)} %refs_1_.3), channel_id=1, source_target_pairs={{0,4},{4,0},{8,12},{12,8},{16,20},{20,16},{24,28},{28,24},{1,5},{5... | collective-permute-start | bytes 393224 | tf_op jit(solution)/shard_map/ppermute | solution.py:222
  6.4 9.0 %collective-permute-start = (bf16[8,32,256]{2,1,0:T(8,128)(2,1)}, bf16[8,32,256]{2,1,0:T(8,128)(2,1)S(1)}, u32[]{:S(2)}, u32[]{:S(2)}) collective-permute-start(bf16[8,32,256]{2,1,0:T(8,128)(2,1)} %refs_1_.3), channel_id=1, source_target_pairs={{0,24},{4,28},{8,16},{12,20},{16,8},{20,12},{24,0},{28,4},{1,25},{... | collective-permute-start | bytes 393224 | tf_op jit(solution)/shard_map/ppermute | solution.py:222
  8.7 0.9 %copy-start.1 = (bf16[8,32,256]{2,1,0:T(8,128)(2,1)S(1)}, bf16[8,32,256]{2,1,0:T(8,128)(2,1)}, u32[]{:S(2)}) copy-start(bf16[8,32,256]{2,1,0:T(8,128)(2,1)} %refs_1_.3) | copy-start | bytes 393220
  9.6 5.7 %copy-start.3 = (f32[8,6,256]{2,0,1:T(8,128)S(1)}, f32[8,6,256]{2,0,1:T(8,128)}, u32[]{:S(2)}) copy-start(f32[8,6,256]{2,0,1:T(8,128)} %param.13) | copy-start | bytes 147460
  9.6 5.7 %copy-start.4 = (f32[8,256]{1,0:T(8,128)S(1)}, f32[8,256]{1,0:T(8,128)}, u32[]{:S(2)}) copy-start(f32[8,256]{1,0:T(8,128)} %areas) | copy-start | bytes 24580
  10.0 6.7 %copy-start.2 = (bf16[8,32,256]{2,1,0:T(8,128)(2,1)S(1)}, bf16[8,32,256]{2,1,0:T(8,128)(2,1)}, u32[]{:S(2)}) copy-start(bf16[8,32,256]{2,1,0:T(8,128)(2,1)} %refs_1_.3) | copy-start | bytes 393220
  12.7 2.6 %collective-permute-start.6 = (bf16[8,32,256]{2,1,0:T(8,128)(2,1)S(1)}, bf16[8,32,256]{2,1,0:T(8,128)(2,1)S(1)}, u32[]{:S(2)}, u32[]{:S(2)}) collective-permute-start(bf16[8,32,256]{2,1,0:T(8,128)(2,1)S(1)} %collective-permute-done.2.refs_1_), channel_id=1, source_target_pairs={{0,4},{4,0},{8,12},{12,8},{16,20},{20,16},{24,28},{28,24},{1,5},{5... | collective-permute-start | bytes 393224 | tf_op jit(solution)/shard_map/ppermute | solution.py:222
  12.7 2.6 %collective-permute-start.5 = (bf16[8,32,256]{2,1,0:T(8,128)(2,1)S(1)}, bf16[8,32,256]{2,1,0:T(8,128)(2,1)S(1)}, u32[]{:S(2)}, u32[]{:S(2)}) collective-permute-start(bf16[8,32,256]{2,1,0:T(8,128)(2,1)S(1)} %collective-permute-done.1.refs_0_), channel_id=1, source_target_pairs={{0,4},{4,0},{8,12},{12,8},{16,20},{20,16},{24,28},{28,24},{1,5},{5... | collective-permute-start | bytes 393224 | tf_op jit(solution)/shard_map/ppermute | solution.py:222
  15.3 1.3 %collective-permute-start.4 = (bf16[8,32,256]{2,1,0:T(8,128)(2,1)S(1)}, bf16[8,32,256]{2,1,0:T(8,128)(2,1)S(1)}, u32[]{:S(2)}, u32[]{:S(2)}) collective-permute-start(bf16[8,32,256]{2,1,0:T(8,128)(2,1)S(1)} %collective-permute-done.refs_2_), channel_id=1, source_target_pairs={{0,4},{4,0},{8,12},{12,8},{16,20},{20,16},{24,28},{28,24},{1,5},{5... | collective-permute-start | bytes 393224 | tf_op jit(solution)/shard_map/ppermute | solution.py:222
  17.6 4.6 %collective-permute-start.9 = (f32[8,256]{1,0:T(8,128)S(1)}, f32[8,256]{1,0:T(8,128)S(1)}, u32[]{:S(2)}, u32[]{:S(2)}) collective-permute-start(f32[8,256]{1,0:T(8,128)S(1)} %get-tuple-element.33.refs_0_), channel_id=1, source_target_pairs={{0,3},{1,2},{2,1},{3,0},{4,7},{5,6},{6,5},{7,4},{8,11},{9,10},{10,... | collective-permute-start | bytes 24584 | tf_op jit(solution)/shard_map/ppermute | solution.py:222
  20.2 3.7 %collective-permute-start.8 = (f32[8,256]{1,0:T(8,128)S(1)}, f32[8,256]{1,0:T(8,128)S(1)}, u32[]{:S(2)}, u32[]{:S(2)}) collective-permute-start(f32[8,256]{1,0:T(8,128)S(1)} %get-tuple-element.33.refs_0_), channel_id=1, source_target_pairs={{0,2},{1,3},{2,0},{3,1},{4,6},{5,7},{6,4},{7,5},{8,10},{9,11},{10,... | collective-permute-start | bytes 24584 | tf_op jit(solution)/shard_map/ppermute | solution.py:222
  20.6 3.7 %collective-permute-start.7 = (f32[8,256]{1,0:T(8,128)S(1)}, f32[8,256]{1,0:T(8,128)S(1)}, u32[]{:S(2)}, u32[]{:S(2)}) collective-permute-start(f32[8,256]{1,0:T(8,128)S(1)} %get-tuple-element.33.refs_0_), channel_id=1, source_target_pairs={{0,1},{1,0},{2,3},{3,2},{4,5},{5,4},{6,7},{7,6},{8,9},{9,8},{10,11... | collective-permute-start | bytes 24584 | tf_op jit(solution)/shard_map/ppermute | solution.py:222

commit v7 on v6

--- a/solution.py
+++ b/solution.py
@@ -12,6 +12,7 @@
 UNROLL = 8
 MOMENTS = 8
 SMALL = 1 << 16
+STAGE_SHIFT = 16
 F32 = jnp.float32
 BF16 = jnp.bfloat16
 VMEM_LIMIT = 8 << 20
@@ -46,11 +47,11 @@
 
 
 def dot_near_exact(left, right, transposed=False):
+    rows = left.shape[0]
     left_high, left_low = parts_of(left, 2)
     right_high, right_low = parts_of(right, 2)
-    return dot(left_high, right_high, transposed) + (
-        dot(left_high, right_low, transposed) + dot(left_low, right_high, transposed)
-    )
+    both = dot(jnp.concatenate([left_high, left_low], axis=0), right_high, transposed)
+    return both[:rows] + (both[rows:] + dot(left_high, right_low, transposed))
 
 
 def block_mask(block_count, freq_count):
@@ -101,24 +102,23 @@
 def plan_kernel(stages, region, freq_count, table, src, dst, owner, slot, token, plan, total, spread):
     block_count = owner.shape[0]
     width = plan.shape[0] // 4
-    row_count = lax.axis_size("row")
     me = lax.axis_index("row")
 
     def place_tile(t, counts):
         source = src[t]
-        found = table[(source // block_count) ^ me]
+        found = table[lax.div(source, block_count) ^ me]
+        stage_here = lax.shift_right_logical(found, STAGE_SHIFT)
         target = jnp.int32(0)
         for stage in range(len(stages)):
-            target = jnp.where(found // row_count == stage, stage * region + counts[stage], target)
+            target = jnp.where(stage_here == stage, stage * region + counts[stage], target)
         plan[target] = t
-        plan[width + target] = found % row_count * block_count + source % block_count
+        plan[width + target] = (found & (2**STAGE_SHIFT - 1)) + lax.rem(source, block_count)
         plan[2 * width + target] = dst[t]
         return tuple(
-            count + (found // row_count == stage).astype(jnp.int32)
-            for stage, count in enumerate(counts)
+            count + (stage_here == stage).astype(jnp.int32) for stage, count in enumerate(counts)
         )
 
-    counts = lax.fori_loop(0, src.shape[0], place_tile, (jnp.int32(0),) * len(stages))
+    counts = lax.fori_loop(0, src.shape[0], place_tile, (jnp.int32(0),) * len(stages), unroll=8)
     for stage, held in enumerate(stages):
         plan[3 * width + stage] = counts[stage]
         for lane in range(UNROLL):
@@ -250,7 +250,7 @@
     middle = [first, *[hop for hop in range(2, row_count, 2) if hop not in (first, late)]]
     stages = ([0], [*middle, 1], [*[hop + 1 for hop in middle], late], [late + 1])
     places = {
-        hop: stage * row_count + index
+        hop: (stage << STAGE_SHIFT) + index * block_count
         for stage, hops in enumerate(stages)
         for index, hop in enumerate(hops)
     }

time: 25.6 us -> 25.5 us (level)
  Pallas kernels: 6.73 us -> 5.77 us
  waiting for transfers between devices: 6.31 us -> 7.22 us
    pallas_call x1, Pallas kernels: 2.26 us -> 1.32 us  [shards(): pl.pallas_call(functools.partial(plan_kernel, stages, region, freq_count)...]
    ppermute x10, waiting for transfers between devices: 6.31 us -> 7.22 us  [exchange(): return lax.ppermute(values, axis, pairs)]
  transfers between devices with their start and end apart: 10 -> 10, of which waited for: 5 -> 5; matrix products, arithmetic and copies ran while one was open for 3% -> 3% of each run, Pallas kernels for 19% -> 16%
where the time goes in v7:
time: 25.5 us; the launch traced here: 25.1 us
  starting transfers between devices  9.69 us (38%)
  waiting for transfers between devices  7.22 us (28%)
  Pallas kernels  5.77 us (23%)
  local copies, waits for them, and re-layouts  1.64 us (6%)
  between operations  0.8 us (3%)
    ppermute x10, starting transfers between devices, exchange(): return lax.ppermute(values, axis, pairs)  9.69 us
    ppermute x10, waiting for transfers between devices, exchange(): return lax.ppermute(values, axis, pairs)  7.22 us
    pallas_call x3, Pallas kernels, near(): pl.pallas_call(functools.partial(near_kernel, stage, region, len(sources)...  2.73 us
    unnamed x21, local copies, waits for them, and re-layouts  1.64 us
    pallas_call x1, Pallas kernels, shards(): pl.pallas_call(functools.partial(plan_kernel, stages, region, freq_count)...  1.32 us
    pallas_call x1, Pallas kernels, shards(): pl.pallas_call(functools.partial(gradient_kernel, len(tables)), out_shape...  0.94 us
    pallas_call x1, Pallas kernels, shards(): pl.pallas_call(functools.partial(field_kernel, 3, region, 1), out_shape=(...  0.78 us
  transfers between devices with their start and end apart: 10, of which 5 were waited for; matrix products, arithmetic and copies ran while one was open for 3% of the time, Pallas kernels for 16%

profile of v7, /device:TPU:0, one launch (start us, length us, event | category | flops | bytes accessed | tf_op | source)
XLA Modules:
  0.0 25.1 jit_solution(9067790008593740629)
XLA Ops:
  0.6 0.0 copy-start.9
  0.7 4.1 %collective-permute-start.1 = (bf16[8,32,256]{2,1,0:T(8,128)(2,1)}, bf16[8,32,256]{2,1,0:T(8,128)(2,1)S(1)}, u32[]{:S(2)}, u32[]{:S(2)}) collective-permute-start(bf16[8,32,256]{2,1,0:T(8,128)(2,1)} %refs_1_.3), channel_id=1, source_target_pairs={{0,16},{4,20},{8,24},{12,28},{16,0},{20,4},{24,8},{28,12},{1,17},{... | collective-permute-start | bytes 393224 | tf_op jit(solution)/shard_map/ppermute | solution.py:222
  4.8 1.6 %collective-permute-start.2 = (bf16[8,32,256]{2,1,0:T(8,128)(2,1)}, bf16[8,32,256]{2,1,0:T(8,128)(2,1)S(1)}, u32[]{:S(2)}, u32[]{:S(2)}) collective-permute-start(bf16[8,32,256]{2,1,0:T(8,128)(2,1)} %refs_1_.3), channel_id=1, source_target_pairs={{0,8},{4,12},{8,0},{12,4},{16,24},{20,28},{24,16},{28,20},{1,9},{5... | collective-permute-start | bytes 393224 | tf_op jit(solution)/shard_map/ppermute | solution.py:222
  6.4 0.0 collective-permute-start.3
  6.4 0.0 collective-permute-start
  6.4 1.3 %plan_stage.1 = (s32[1024]{0:T(1024)S(4)}, f32[8,32,512]{2,1,0:T(8,128)S(1)}, bf16[128,256]{1,0:T(8,128)(2,1)S(1)}) custom-call(s32[8]{0:T(128)S(1)} %copy-done.9, s32[48]{0:T(128)S(1)} %copy-done.5, s32[48]{0:T(128)S(1)} %copy-done.6, s32[8]{0:T(128)S(1)} %bitcast.3, s32[8]{0:T(128)S(1)} %copy-done.8, f32[8,128]{1,0:T(8,128)S(1)} %early_stage.1.token), custom_call_target="tpu_custom_call" | custom-call | bytes 25165824 | tf_op jit(solution)/shard_map/plan_stage/pallas_call | solution.py:265
  7.8 0.0 copy-start.1
  7.8 0.9 %copy-done.1 = bf16[8,32,256]{2,1,0:T(8,128)(2,1)S(1)} copy-done((bf16[8,32,256]{2,1,0:T(8,128)(2,1)S(1)}, bf16[8,32,256]{2,1,0:T(8,128)(2,1)}, u32[]{:S(2)}) %copy-start.1) | copy-done | bytes 131096
  8.7 0.4 %near_stage.3.refs_4_ = f32[8,32,512]{2,1,0:T(8,128)S(1)} custom-call(s32[1024]{0:T(1024)S(4)} %get-tuple-element.20.plan, bf16[8,32,256]{2,1,0:T(8,128)(2,1)S(1)} %copy-done.1, bf16[48,256,512]{2,1,0:T(8,128)(2,1)S(1)} %copy-done, f32[8,32,512]{2,1,0:T(8,128)S(1)} %get-tuple-element.22.refs_2_), custom_call_target="tpu_custom_call", output_to_operand_aliasing={{}: (3, {})} | custom-call | bytes 65536 | tf_op jit(solution)/shard_map/near_stage/pallas_call | solution.py:282
  9.1 3.7 %collective-permute-done.1.refs_0_ = bf16[8,32,256]{2,1,0:T(8,128)(2,1)S(1)} collective-permute-done((bf16[8,32,256]{2,1,0:T(8,128)(2,1)}, bf16[8,32,256]{2,1,0:T(8,128)(2,1)S(1)}, u32[]{:S(2)}, u32[]{:S(2)}) %collective-permute-start.1) | collective-permute-done | bytes 131104 | tf_op jit(solution)/shard_map/ppermute | solution.py:222
  12.7 0.0 collective-permute-done.2.refs_1_
  12.7 0.0 collective-permute-start.6
  12.7 0.5 %collective-permute-start.5 = (bf16[8,32,256]{2,1,0:T(8,128)(2,1)S(1)}, bf16[8,32,256]{2,1,0:T(8,128)(2,1)S(1)}, u32[]{:S(2)}, u32[]{:S(2)}) collective-permute-start(bf16[8,32,256]{2,1,0:T(8,128)(2,1)S(1)} %collective-permute-done.1.refs_0_), channel_id=1, source_target_pairs={{0,4},{4,0},{8,12},{12,8},{16,20},{20,16},{24,28},{28,24},{1,5},{5... | collective-permute-start | bytes 393224 | tf_op jit(solution)/shard_map/ppermute | solution.py:222
  13.3 0.0 collective-permute-done.3.refs_2_
  13.3 1.0 %near_stage.4.refs_4_ = f32[8,32,512]{2,1,0:T(8,128)S(1)} custom-call(s32[1024]{0:T(1024)S(4)} %get-tuple-element.20.plan, bf16[8,32,256]{2,1,0:T(8,128)(2,1)S(1)} %collective-permute-done.1.refs_0_, bf16[8,32,256]{2,1,0:T(8,128)(2,1)S(1)} %collective-permute-done.2.refs_1_, ...), custom_call_target="tpu_custom_call", output_to_operand_aliasing={{}: (5, {})} | custom-call | bytes 65536 | tf_op jit(solution)/shard_map/near_stage/pallas_call | solution.py:282
  14.2 1.1 %collective-permute-done.refs_2_ = bf16[8,32,256]{2,1,0:T(8,128)(2,1)S(1)} collective-permute-done((bf16[8,32,256]{2,1,0:T(8,128)(2,1)}, bf16[8,32,256]{2,1,0:T(8,128)(2,1)S(1)}, u32[]{:S(2)}, u32[]{:S(2)}) %collective-permute-start) | collective-permute-done | bytes 131104 | tf_op jit(solution)/shard_map/ppermute | solution.py:222
  15.3 0.0 collective-permute-start.4
  15.4 0.0 copy-done.4
  15.4 0.0 collective-permute-done.6.refs_1_
  15.4 0.0 collective-permute-done.5.refs_0_
  15.4 1.4 %near_stage.5.refs_3_ = f32[8,32,512]{2,1,0:T(8,128)S(1)} custom-call(s32[1024]{0:T(1024)S(4)} %get-tuple-element.20.plan, bf16[8,32,256]{2,1,0:T(8,128)(2,1)S(1)} %collective-permute-done.5.refs_0_, bf16[8,32,256]{2,1,0:T(8,128)(2,1)S(1)} %collective-permute-done.6.refs_1_, ...), custom_call_target="tpu_custom_call", output_to_operand_aliasing={{}: (5, {})} | custom-call | bytes 65536 | tf_op jit(solution)/shard_map/near_stage/pallas_call | solution.py:282
  16.7 0.0 collective-permute-done.4.refs_0_
  16.8 0.0 copy-done.2
  16.8 0.8 %field_stage.1 = (f32[8,32,512]{2,1,0:T(8,128)S(1)}, f32[8,32,256]{2,1,0:T(8,128)S(1)}, f32[8,256]{1,0:T(8,128)S(1)}, f32[128,256]{1,0:T(8,128)S(1)}, f32[128,256]{1,0:T(8,128)S(1)}) custom-call(s32[1024]{0:T(1024)S(4)} %get-tuple-element.20.plan, bf16[8,32,256]{2,1,0:T(8,128)(2,1)S(1)} %collective-permute-done.4.refs_0_, ...), custom_call_target="tpu_custom_call", output_to_operand_aliasing={{0}: (4, {})} | custom-call | bytes 65536 | tf_op jit(solution)/shard_map/field_stage/pallas_call | solution.py:316
  17.5 2.6 %collective-permute-start.9 = (f32[8,256]{1,0:T(8,128)S(1)}, f32[8,256]{1,0:T(8,128)S(1)}, u32[]{:S(2)}, u32[]{:S(2)}) collective-permute-start(f32[8,256]{1,0:T(8,128)S(1)} %get-tuple-element.33.refs_0_), channel_id=1, source_target_pairs={{0,3},{1,2},{2,1},{3,0},{4,7},{5,6},{6,5},{7,4},{8,11},{9,10},{10,... | collective-permute-start | bytes 24584 | tf_op jit(solution)/shard_map/ppermute | solution.py:222
  20.1 0.4 %collective-permute-start.8 = (f32[8,256]{1,0:T(8,128)S(1)}, f32[8,256]{1,0:T(8,128)S(1)}, u32[]{:S(2)}, u32[]{:S(2)}) collective-permute-start(f32[8,256]{1,0:T(8,128)S(1)} %get-tuple-element.33.refs_0_), channel_id=1, source_target_pairs={{0,2},{1,3},{2,0},{3,1},{4,6},{5,7},{6,4},{7,5},{8,10},{9,11},{10,... | collective-permute-start | bytes 24584 | tf_op jit(solution)/shard_map/ppermute | solution.py:222
  20.5 0.5 %collective-permute-start.7 = (f32[8,256]{1,0:T(8,128)S(1)}, f32[8,256]{1,0:T(8,128)S(1)}, u32[]{:S(2)}, u32[]{:S(2)}) collective-permute-start(f32[8,256]{1,0:T(8,128)S(1)} %get-tuple-element.33.refs_0_), channel_id=1, source_target_pairs={{0,1},{1,0},{2,3},{3,2},{4,5},{5,4},{6,7},{7,6},{8,9},{9,8},{10,11... | collective-permute-start | bytes 24584 | tf_op jit(solution)/shard_map/ppermute | solution.py:222
  21.0 0.7 %copy.19 = f32[8,32,256]{2,1,0:T(8,128)} copy(f32[8,32,256]{2,1,0:T(8,128)S(1)} %get-tuple-element.36) | data formatting | bytes 524288
  21.8 0.4 %collective-permute-done.9.refs_3_ = f32[8,256]{1,0:T(8,128)S(1)} collective-permute-done((f32[8,256]{1,0:T(8,128)S(1)}, f32[8,256]{1,0:T(8,128)S(1)}, u32[]{:S(2)}, u32[]{:S(2)}) %collective-permute-start.9) | collective-permute-done | bytes 8224 | tf_op jit(solution)/shard_map/ppermute | solution.py:222
  22.1 1.6 %collective-permute-done.8.refs_2_ = f32[8,256]{1,0:T(8,128)S(1)} collective-permute-done((f32[8,256]{1,0:T(8,128)S(1)}, f32[8,256]{1,0:T(8,128)S(1)}, u32[]{:S(2)}, u32[]{:S(2)}) %collective-permute-start.8) | collective-permute-done | bytes 8224 | tf_op jit(solution)/shard_map/ppermute | solution.py:222
  23.8 0.4 %collective-permute-done.7.refs_1_ = f32[8,256]{1,0:T(8,128)S(1)} collective-permute-done((f32[8,256]{1,0:T(8,128)S(1)}, f32[8,256]{1,0:T(8,128)S(1)}, u32[]{:S(2)}, u32[]{:S(2)}) %collective-permute-start.7) | collective-permute-done | bytes 8224 | tf_op jit(solution)/shard_map/ppermute | solution.py:222
  24.2 0.9 %gradient_stage.1 = f32[8,256]{1,0:T(8,128)} custom-call(f32[8,256]{1,0:T(8,128)S(1)} %get-tuple-element.33.refs_0_, f32[8,256]{1,0:T(8,128)S(1)} %collective-permute-done.7.refs_1_, f32[8,256]{1,0:T(8,128)S(1)} %collective-permute-done.8.refs_2_, f32[8,256]{1,0:T(8,128)S(1)} %collective-permute-done.9.refs_3_, f32[64,256]{1,0:T(8,128)S(1)} %basis_stage.1.refs_4_, ...), custom_call_target="tpu_custom_call" | custom-call | bytes 65536 | tf_op jit(solution)/shard_map/gradient_stage/pallas_call | solution.py:338
  (17 shorter events, 0.0 us)
Async XLA Ops:
  0.6 5.8 %copy-start.9 = (s32[8]{0:T(128)S(1)}, s32[8]{0:T(128)}, u32[]{:S(2)}) copy-start(s32[8]{0:T(128)} %constant.2.clone.table) | copy-start | bytes 100
  0.6 7.1 %copy-start = (bf16[48,256,512]{2,1,0:T(8,128)(2,1)S(1)}, bf16[48,256,512]{2,1,0:T(8,128)(2,1)}, u32[]{:S(2)}) copy-start(bf16[48,256,512]{2,1,0:T(8,128)(2,1)} %refs_2_.1) | copy-start | bytes 37748740
  0.7 5.7 %copy-start.8 = (s32[8]{0:T(128)S(1)}, s32[8]{0:T(128)}, u32[]{:S(2)}) copy-start(s32[8]{0:T(128)} %slot.1) | copy-start | bytes 100
  0.7 5.7 %copy-start.7 = (s32[8,1]{0,1:T(1,128)S(1)}, s32[8,1]{0,1:T(1,128)}, u32[]{:S(2)}) copy-start(s32[8,1]{0,1:T(1,128)} %param.15) | copy-start | bytes 100
  0.7 5.7 %copy-start.5 = (s32[48]{0:T(128)S(1)}, s32[48]{0:T(128)}, u32[]{:S(2)}) copy-start(s32[48]{0:T(128)} %src.1) | copy-start | bytes 580
  0.7 5.7 %copy-start.6 = (s32[48]{0:T(128)S(1)}, s32[48]{0:T(128)}, u32[]{:S(2)}) copy-start(s32[48]{0:T(128)} %dst.1) | copy-start | bytes 580
  0.7 12.0 %collective-permute-start.1 = (bf16[8,32,256]{2,1,0:T(8,128)(2,1)}, bf16[8,32,256]{2,1,0:T(8,128)(2,1)S(1)}, u32[]{:S(2)}, u32[]{:S(2)}) collective-permute-start(bf16[8,32,256]{2,1,0:T(8,128)(2,1)} %refs_1_.3), channel_id=1, source_target_pairs={{0,16},{4,20},{8,24},{12,28},{16,0},{20,4},{24,8},{28,12},{1,17},{... | collective-permute-start | bytes 393224 | tf_op jit(solution)/shard_map/ppermute | solution.py:222
  4.8 7.9 %collective-permute-start.2 = (bf16[8,32,256]{2,1,0:T(8,128)(2,1)}, bf16[8,32,256]{2,1,0:T(8,128)(2,1)S(1)}, u32[]{:S(2)}, u32[]{:S(2)}) collective-permute-start(bf16[8,32,256]{2,1,0:T(8,128)(2,1)} %refs_1_.3), channel_id=1, source_target_pairs={{0,8},{4,12},{8,0},{12,4},{16,24},{20,28},{24,16},{28,20},{1,9},{5... | collective-permute-start | bytes 393224 | tf_op jit(solution)/shard_map/ppermute | solution.py:222
  6.4 6.9 %collective-permute-start.3 = (bf16[8,32,256]{2,1,0:T(8,128)(2,1)}, bf16[8,32,256]{2,1,0:T(8,128)(2,1)S(1)}, u32[]{:S(2)}, u32[]{:S(2)}) collective-permute-start(bf16[8,32,256]{2,1,0:T(8,128)(2,1)} %refs_1_.3), channel_id=1, source_target_pairs={{0,4},{4,0},{8,12},{12,8},{16,20},{20,16},{24,28},{28,24},{1,5},{5... | collective-permute-start | bytes 393224 | tf_op jit(solution)/shard_map/ppermute | solution.py:222
  6.4 9.0 %collective-permute-start = (bf16[8,32,256]{2,1,0:T(8,128)(2,1)}, bf16[8,32,256]{2,1,0:T(8,128)(2,1)S(1)}, u32[]{:S(2)}, u32[]{:S(2)}) collective-permute-start(bf16[8,32,256]{2,1,0:T(8,128)(2,1)} %refs_1_.3), channel_id=1, source_target_pairs={{0,24},{4,28},{8,16},{12,20},{16,8},{20,12},{24,0},{28,4},{1,25},{... | collective-permute-start | bytes 393224 | tf_op jit(solution)/shard_map/ppermute | solution.py:222
  7.8 0.9 %copy-start.1 = (bf16[8,32,256]{2,1,0:T(8,128)(2,1)S(1)}, bf16[8,32,256]{2,1,0:T(8,128)(2,1)}, u32[]{:S(2)}) copy-start(bf16[8,32,256]{2,1,0:T(8,128)(2,1)} %refs_1_.3) | copy-start | bytes 393220
  8.7 6.7 %copy-start.3 = (f32[8,6,256]{2,0,1:T(8,128)S(1)}, f32[8,6,256]{2,0,1:T(8,128)}, u32[]{:S(2)}) copy-start(f32[8,6,256]{2,0,1:T(8,128)} %param.13) | copy-start | bytes 147460
  8.7 6.7 %copy-start.4 = (f32[8,256]{1,0:T(8,128)S(1)}, f32[8,256]{1,0:T(8,128)}, u32[]{:S(2)}) copy-start(f32[8,256]{1,0:T(8,128)} %areas) | copy-start | bytes 24580
  9.1 7.7 %copy-start.2 = (bf16[8,32,256]{2,1,0:T(8,128)(2,1)S(1)}, bf16[8,32,256]{2,1,0:T(8,128)(2,1)}, u32[]{:S(2)}) copy-start(bf16[8,32,256]{2,1,0:T(8,128)(2,1)} %refs_1_.3) | copy-start | bytes 393220
  12.7 2.6 %collective-permute-start.6 = (bf16[8,32,256]{2,1,0:T(8,128)(2,1)S(1)}, bf16[8,32,256]{2,1,0:T(8,128)(2,1)S(1)}, u32[]{:S(2)}, u32[]{:S(2)}) collective-permute-start(bf16[8,32,256]{2,1,0:T(8,128)(2,1)S(1)} %collective-permute-done.2.refs_1_), channel_id=1, source_target_pairs={{0,4},{4,0},{8,12},{12,8},{16,20},{20,16},{24,28},{28,24},{1,5},{5... | collective-permute-start | bytes 393224 | tf_op jit(solution)/shard_map/ppermute | solution.py:222
  12.7 2.6 %collective-permute-start.5 = (bf16[8,32,256]{2,1,0:T(8,128)(2,1)S(1)}, bf16[8,32,256]{2,1,0:T(8,128)(2,1)S(1)}, u32[]{:S(2)}, u32[]{:S(2)}) collective-permute-start(bf16[8,32,256]{2,1,0:T(8,128)(2,1)S(1)} %collective-permute-done.1.refs_0_), channel_id=1, source_target_pairs={{0,4},{4,0},{8,12},{12,8},{16,20},{20,16},{24,28},{28,24},{1,5},{5... | collective-permute-start | bytes 393224 | tf_op jit(solution)/shard_map/ppermute | solution.py:222
  15.3 1.4 %collective-permute-start.4 = (bf16[8,32,256]{2,1,0:T(8,128)(2,1)S(1)}, bf16[8,32,256]{2,1,0:T(8,128)(2,1)S(1)}, u32[]{:S(2)}, u32[]{:S(2)}) collective-permute-start(bf16[8,32,256]{2,1,0:T(8,128)(2,1)S(1)} %collective-permute-done.refs_2_), channel_id=1, source_target_pairs={{0,4},{4,0},{8,12},{12,8},{16,20},{20,16},{24,28},{28,24},{1,5},{5... | collective-permute-start | bytes 393224 | tf_op jit(solution)/shard_map/ppermute | solution.py:222
  17.5 4.6 %collective-permute-start.9 = (f32[8,256]{1,0:T(8,128)S(1)}, f32[8,256]{1,0:T(8,128)S(1)}, u32[]{:S(2)}, u32[]{:S(2)}) collective-permute-start(f32[8,256]{1,0:T(8,128)S(1)} %get-tuple-element.33.refs_0_), channel_id=1, source_target_pairs={{0,3},{1,2},{2,1},{3,0},{4,7},{5,6},{6,5},{7,4},{8,11},{9,10},{10,... | collective-permute-start | bytes 24584 | tf_op jit(solution)/shard_map/ppermute | solution.py:222
  20.1 3.7 %collective-permute-start.8 = (f32[8,256]{1,0:T(8,128)S(1)}, f32[8,256]{1,0:T(8,128)S(1)}, u32[]{:S(2)}, u32[]{:S(2)}) collective-permute-start(f32[8,256]{1,0:T(8,128)S(1)} %get-tuple-element.33.refs_0_), channel_id=1, source_target_pairs={{0,2},{1,3},{2,0},{3,1},{4,6},{5,7},{6,4},{7,5},{8,10},{9,11},{10,... | collective-permute-start | bytes 24584 | tf_op jit(solution)/shard_map/ppermute | solution.py:222
  20.5 3.7 %collective-permute-start.7 = (f32[8,256]{1,0:T(8,128)S(1)}, f32[8,256]{1,0:T(8,128)S(1)}, u32[]{:S(2)}, u32[]{:S(2)}) collective-permute-start(f32[8,256]{1,0:T(8,128)S(1)} %get-tuple-element.33.refs_0_), channel_id=1, source_target_pairs={{0,1},{1,0},{2,3},{3,2},{4,5},{5,4},{6,7},{7,6},{8,9},{9,8},{10,11... | collective-permute-start | bytes 24584 | tf_op jit(solution)/shard_map/ppermute | solution.py:222

commit v8 on v7

--- a/solution.py
+++ b/solution.py
@@ -65,7 +65,6 @@
     depth = sources[0].shape[0]
     for index, source in enumerate(sources):
         held[index * depth : (index + 1) * depth] = source[...]
-    held[len(sources) * depth] = jnp.zeros(held.shape[1:], held.dtype)
 
 
 def add_stage(stage, region, plan, held, tiles, total):
@@ -99,7 +98,9 @@
     token[...] = jnp.zeros_like(token)
 
 
-def plan_kernel(stages, region, freq_count, table, src, dst, owner, slot, token, plan, total, spread):
+def plan_kernel(
+    stages, region, freq_count, table, src, dst, owner, slot, token, plan, total, spread, collect
+):
     block_count = owner.shape[0]
     width = plan.shape[0] // 4
     me = lax.axis_index("row")
@@ -119,13 +120,13 @@
         )
 
     counts = lax.fori_loop(0, src.shape[0], place_tile, (jnp.int32(0),) * len(stages), unroll=8)
-    for stage, held in enumerate(stages):
+    for stage in range(len(stages)):
         plan[3 * width + stage] = counts[stage]
         for lane in range(UNROLL):
             position = stage * region + counts[stage] + lane
             plan[position] = 0
-            plan[width + position] = len(held) * block_count
-            plan[2 * width + position] = 0
+            plan[width + position] = 0
+            plan[2 * width + position] = block_count
     total[...] = jnp.zeros_like(total)
     shape = (freq_count, spread.shape[1])
     lanes = lax.broadcasted_iota(jnp.int32, shape, 1)
@@ -136,6 +137,13 @@
         spread[block * freq_count : (block + 1) * freq_count] = jnp.where(
             chosen, 1.0, 0.0
         ).astype(BF16)
+    rows = lax.broadcasted_iota(jnp.int32, collect.shape, 0)
+    lanes = lax.broadcasted_iota(jnp.int32, collect.shape, 1)
+    wanted = lanes % freq_count
+    for block in range(block_count):
+        particle = owner[block] * PD + slot[block]
+        wanted = wanted + jnp.where(lanes // freq_count == block, particle * freq_count, 0)
+    collect[...] = jnp.where(rows == wanted, 1.0, 0.0).astype(BF16)
 
 
 def basis_kernel(place, areas, basis):
@@ -151,19 +159,19 @@
 
 def near_kernel(stage, region, count, plan, *refs):
     sources = refs[:count]
-    tiles, start, total, held = refs[count:]
-    fill_panels(sources, held)
-    add_stage(stage, region, plan, held, tiles, total)
-
-
-def field_kernel(stage, region, count, plan, *refs):
-    sources = refs[:count]
-    panels, tiles, start, basis, spread = refs[count : count + 5]
-    total, field, table, powers, crosses, held = refs[count + 5 :]
+    tiles, start, total, *held = refs[count:]
+    if held:
+        fill_panels(sources, held[0])
+    add_stage(stage, region, plan, held[0] if held else sources[0], tiles, total)
+
+
+def field_kernel(
+    stage, region, plan, source, panels, tiles, start, basis, spread,
+    total, field, table, powers, crosses,
+):
     block_count, rows_twice, node_count = panels.shape
     freq_count = rows_twice // 2
-    fill_panels(sources, held)
-    add_stage(stage, region, plan, held, tiles, total)
+    add_stage(stage, region, plan, source, tiles, total)
     for block in range(block_count):
         image = total[block]
         incident = panels[block].astype(F32)
@@ -195,13 +203,13 @@
 
 def gradient_kernel(count, *refs):
     tables = refs[:count]
-    basis, spread, powers, crosses, gradient = refs[count:]
+    basis, collect, powers, crosses, gradient = refs[count:]
     block_count = gradient.shape[0]
     freq_count = powers.shape[0] // block_count
     summed = tables[0][...]
     for table in tables[1:]:
         summed = summed + table[...]
-    joined = dot(jnp.concatenate(parts_of(summed, 3), axis=0), spread[...], True)
+    joined = dot(jnp.concatenate(parts_of(summed, 3), axis=0), collect[...])
     totals = joined[:MOMENTS] + (joined[MOMENTS : 2 * MOMENTS] + joined[2 * MOMENTS :])
     mask = block_mask(block_count, freq_count)
     squares = jnp.sum(totals * totals, axis=0, keepdims=True)
@@ -229,7 +237,7 @@
     row_count = lax.axis_size("row")
     group_count = lax.axis_size("col")
     particle_count = group_count * PD
-    image_shape = (block_count, rows_twice, 2 * node_count)
+    image_shape = (block_count + 1, rows_twice, 2 * node_count)
     basis_shape = (MOMENTS * block_count, node_count)
     spread_shape = (block_count * freq_count, particle_count * freq_count)
     power_shape = (block_count * freq_count, node_count)
@@ -262,15 +270,16 @@
     for hop in [*middle, late, 1]:
         arrived[hop] = exchange(out, "row", hop)
 
-    plan, total, spread = pl.pallas_call(
+    plan, total, spread, collect = pl.pallas_call(
         functools.partial(plan_kernel, stages, region, freq_count),
         out_shape=(
             pltpu.SMEM((4 * width,), jnp.int32),
             pltpu.VMEM(image_shape, F32),
             pltpu.VMEM(spread_shape, BF16),
+            pltpu.VMEM(spread_shape[::-1], BF16),
         ),
         in_specs=[SMEM_SPEC] * 5 + [VMEM_SPEC],
-        out_specs=(SMEM_SPEC,) + (VMEM_SPEC,) * 2,
+        out_specs=(SMEM_SPEC,) + (VMEM_SPEC,) * 3,
         compiler_params=params(),
         cost_estimate=cost(4 * tiles.size),
         name="plan_stage",
@@ -278,13 +287,13 @@
 
     def near(stage, total):
         sources = [arrived[hop] for hop in stages[stage]]
-        scratch = pltpu.VMEM((len(sources) * block_count + 1, rows_twice, node_count), BF16)
+        stacked = pltpu.VMEM((len(sources) * block_count, rows_twice, node_count), BF16)
         return pl.pallas_call(
             functools.partial(near_kernel, stage, region, len(sources)),
             out_shape=pltpu.VMEM(image_shape, F32),
             in_specs=[SMEM_SPEC] + [VMEM_SPEC] * (len(sources) + 2),
             out_specs=VMEM_SPEC,
-            scratch_shapes=[scratch],
+            scratch_shapes=[stacked] if len(sources) > 1 else [],
             input_output_aliases={len(sources) + 2: 0},
             compiler_params=params(),
             cost_estimate=cost(SMALL),
@@ -314,7 +323,7 @@
     total = near(2, total)
 
     total, field, table, powers, crosses = pl.pallas_call(
-        functools.partial(field_kernel, 3, region, 1),
+        functools.partial(field_kernel, 3, region),
         out_shape=(
             pltpu.VMEM(image_shape, F32),
             pltpu.VMEM(panels.shape, F32),
@@ -324,7 +333,6 @@
         ),
         in_specs=[SMEM_SPEC] + [VMEM_SPEC] * 6,
         out_specs=(VMEM_SPEC,) * 5,
-        scratch_shapes=[pltpu.VMEM((block_count + 1, rows_twice, node_count), BF16)],
         input_output_aliases={4: 0},
         compiler_params=params(),
         cost_estimate=cost(SMALL),
@@ -343,7 +351,7 @@
         compiler_params=params(),
         cost_estimate=cost(SMALL),
         name="gradient_stage",
-    )(*tables, basis, spread, powers, crosses)
+    )(*tables, basis, collect, powers, crosses)
     return (field, gradient)
 
 

time: 25.5 us -> 25.6 us (level)
  the two profiles are of different devices: /device:TPU:0 before, /device:TPU:16 now
where the time goes in v8:
time: 25.6 us; the launch traced here: 25.2 us
  waiting for transfers between devices  9.51 us (37%)
  starting transfers between devices  7.59 us (30%)
  Pallas kernels  5.66 us (22%)
  local copies, waits for them, and re-layouts  1.64 us (6%)
  between operations  0.77 us (3%)
    ppermute x10, waiting for transfers between devices, exchange(): return lax.ppermute(values, axis, pairs)  9.51 us
    ppermute x10, starting transfers between devices, exchange(): return lax.ppermute(values, axis, pairs)  7.59 us
    pallas_call x3, Pallas kernels, near(): pl.pallas_call(functools.partial(near_kernel, stage, region, len(sources)...  2.6 us
    unnamed x21, local copies, waits for them, and re-layouts  1.64 us
    pallas_call x1, Pallas kernels, shards(): pl.pallas_call(functools.partial(plan_kernel, stages, region, freq_count)...  1.31 us
    pallas_call x1, Pallas kernels, shards(): pl.pallas_call(functools.partial(gradient_kernel, len(tables)), out_shape...  0.91 us
    pallas_call x1, Pallas kernels, shards(): pl.pallas_call(functools.partial(field_kernel, 3, region), out_shape=(plt...  0.84 us
  transfers between devices with their start and end apart: 10, of which 7 were waited for; matrix products, arithmetic and copies ran while one was open for 3% of the time, Pallas kernels for 16%

profile of v8, /device:TPU:16, one launch (start us, length us, event | category | flops | bytes accessed | tf_op | source)
XLA Modules:
  0.0 25.2 jit_solution(16921018303714132122)
XLA Ops:
  0.6 0.0 copy-start.9
  0.7 0.1 collective-permute-start.1
  0.8 1.9 %collective-permute-start.2 = (bf16[8,32,256]{2,1,0:T(8,128)(2,1)}, bf16[8,32,256]{2,1,0:T(8,128)(2,1)S(1)}, u32[]{:S(2)}, u32[]{:S(2)}) collective-permute-start(bf16[8,32,256]{2,1,0:T(8,128)(2,1)} %panels.1), channel_id=1, source_target_pairs={{0,8},{4,12},{8,0},{12,4},{16,24},{20,28},{24,16},{28,20},{1,9},{5... | collective-permute-start | bytes 393224 | tf_op jit(solution)/shard_map/ppermute | solution.py:230
  2.7 0.0 collective-permute-start.3
  2.7 1.6 %collective-permute-start = (bf16[8,32,256]{2,1,0:T(8,128)(2,1)}, bf16[8,32,256]{2,1,0:T(8,128)(2,1)S(1)}, u32[]{:S(2)}, u32[]{:S(2)}) collective-permute-start(bf16[8,32,256]{2,1,0:T(8,128)(2,1)} %panels.1), channel_id=1, source_target_pairs={{0,24},{4,28},{8,16},{12,20},{16,8},{20,12},{24,0},{28,4},{1,25},{... | collective-permute-start | bytes 393224 | tf_op jit(solution)/shard_map/ppermute | solution.py:230
  4.3 0.0 copy-done.8
  4.3 1.3 %plan_stage.1 = (s32[1024]{0:T(1024)S(4)}, f32[9,32,512]{2,1,0:T(8,128)S(1)}, bf16[128,256]{1,0:T(8,128)(2,1)S(1)}, bf16[256,128]{1,0:T(8,128)(2,1)S(1)}) custom-call(s32[8]{0:T(128)S(1)} %copy-done.9, s32[48]{0:T(128)S(1)} %copy-done.5, s32[48]{0:T(128)S(1)} %copy-done.6, s32[8]{0:T(128)S(1)} %bitcast.3, s32[8]{0:T(128)S(1)} %copy-done.8, ...), custom_call_target="tpu_custom_call" | custom-call | bytes 25165824 | tf_op jit(solution)/shard_map/plan_stage/pallas_call | solution.py:273
  5.6 0.0 copy-done
  5.6 0.0 copy-start.1
  5.6 0.9 %copy-done.1 = bf16[8,32,256]{2,1,0:T(8,128)(2,1)S(1)} copy-done((bf16[8,32,256]{2,1,0:T(8,128)(2,1)S(1)}, bf16[8,32,256]{2,1,0:T(8,128)(2,1)}, u32[]{:S(2)}) %copy-start.1) | copy-done | bytes 131096
  6.5 0.5 %near_stage.3.refs_4_ = f32[9,32,512]{2,1,0:T(8,128)S(1)} custom-call(s32[1024]{0:T(1024)S(4)} %get-tuple-element.21.plan, bf16[8,32,256]{2,1,0:T(8,128)(2,1)S(1)} %copy-done.1, bf16[48,256,512]{2,1,0:T(8,128)(2,1)S(1)} %copy-done, f32[9,32,512]{2,1,0:T(8,128)S(1)} %get-tuple-element.23.refs_2_), custom_call_target="tpu_custom_call", output_to_operand_aliasing={{}: (3, {})} | custom-call | bytes 65536 | tf_op jit(solution)/shard_map/near_stage/pallas_call | solution.py:291
  7.0 1.3 %collective-permute-done.1.refs_0_ = bf16[8,32,256]{2,1,0:T(8,128)(2,1)S(1)} collective-permute-done((bf16[8,32,256]{2,1,0:T(8,128)(2,1)}, bf16[8,32,256]{2,1,0:T(8,128)(2,1)S(1)}, u32[]{:S(2)}, u32[]{:S(2)}) %collective-permute-start.1) | collective-permute-done | bytes 131104 | tf_op jit(solution)/shard_map/ppermute | solution.py:230
  8.3 1.6 %collective-permute-done.2.refs_1_ = bf16[8,32,256]{2,1,0:T(8,128)(2,1)S(1)} collective-permute-done((bf16[8,32,256]{2,1,0:T(8,128)(2,1)}, bf16[8,32,256]{2,1,0:T(8,128)(2,1)S(1)}, u32[]{:S(2)}, u32[]{:S(2)}) %collective-permute-start.2) | collective-permute-done | bytes 131104 | tf_op jit(solution)/shard_map/ppermute | solution.py:230
  9.8 0.0 collective-permute-start.6
  9.8 0.5 %collective-permute-start.5 = (bf16[8,32,256]{2,1,0:T(8,128)(2,1)S(1)}, bf16[8,32,256]{2,1,0:T(8,128)(2,1)S(1)}, u32[]{:S(2)}, u32[]{:S(2)}) collective-permute-start(bf16[8,32,256]{2,1,0:T(8,128)(2,1)S(1)} %collective-permute-done.1.refs_0_), channel_id=1, source_target_pairs={{0,4},{4,0},{8,12},{12,8},{16,20},{20,16},{24,28},{28,24},{1,5},{5... | collective-permute-start | bytes 393224 | tf_op jit(solution)/shard_map/ppermute | solution.py:230
  10.3 0.0 collective-permute-done.3.refs_2_
  10.3 1.3 %near_stage.4.refs_4_ = f32[9,32,512]{2,1,0:T(8,128)S(1)} custom-call(s32[1024]{0:T(1024)S(4)} %get-tuple-element.21.plan, bf16[8,32,256]{2,1,0:T(8,128)(2,1)S(1)} %collective-permute-done.1.refs_0_, bf16[8,32,256]{2,1,0:T(8,128)(2,1)S(1)} %collective-permute-done.2.refs_1_, ...), custom_call_target="tpu_custom_call", output_to_operand_aliasing={{}: (5, {})} | custom-call | bytes 65536 | tf_op jit(solution)/shard_map/near_stage/pallas_call | solution.py:291
  11.7 3.9 %collective-permute-done.refs_2_ = bf16[8,32,256]{2,1,0:T(8,128)(2,1)S(1)} collective-permute-done((bf16[8,32,256]{2,1,0:T(8,128)(2,1)}, bf16[8,32,256]{2,1,0:T(8,128)(2,1)S(1)}, u32[]{:S(2)}, u32[]{:S(2)}) %collective-permute-start) | collective-permute-done | bytes 131104 | tf_op jit(solution)/shard_map/ppermute | solution.py:230
  15.5 0.0 collective-permute-start.4
  15.6 0.0 collective-permute-done.6.refs_1_
  15.6 0.0 collective-permute-done.5.refs_0_
  15.6 0.8 %near_stage.5.start = f32[9,32,512]{2,1,0:T(8,128)S(1)} custom-call(s32[1024]{0:T(1024)S(4)} %get-tuple-element.21.plan, bf16[8,32,256]{2,1,0:T(8,128)(2,1)S(1)} %collective-permute-done.5.refs_0_, bf16[8,32,256]{2,1,0:T(8,128)(2,1)S(1)} %collective-permute-done.6.refs_1_, ...), custom_call_target="tpu_custom_call", output_to_operand_aliasing={{}: (5, {})} | custom-call | bytes 65536 | tf_op jit(solution)/shard_map/near_stage/pallas_call | solution.py:291
  16.4 0.5 %collective-permute-done.4.source = bf16[8,32,256]{2,1,0:T(8,128)(2,1)S(1)} collective-permute-done((bf16[8,32,256]{2,1,0:T(8,128)(2,1)S(1)}, bf16[8,32,256]{2,1,0:T(8,128)(2,1)S(1)}, u32[]{:S(2)}, u32[]{:S(2)}) %collective-permute-start.4) | collective-permute-done | bytes 131104 | tf_op jit(solution)/shard_map/ppermute | solution.py:230
  16.9 0.8 %field_stage.1 = (f32[9,32,512]{2,1,0:T(8,128)S(1)}, f32[8,32,256]{2,1,0:T(8,128)S(1)}, f32[8,256]{1,0:T(8,128)S(1)}, f32[128,256]{1,0:T(8,128)S(1)}, f32[128,256]{1,0:T(8,128)S(1)}) custom-call(s32[1024]{0:T(1024)S(4)} %get-tuple-element.21.plan, bf16[8,32,256]{2,1,0:T(8,128)(2,1)S(1)} %collective-permute-done.4.source, ...), custom_call_target="tpu_custom_call", output_to_operand_aliasing={{0}: (4, {})} | custom-call | bytes 65536 | tf_op jit(solution)/shard_map/field_stage/pallas_call | solution.py:325
  17.7 2.5 %collective-permute-start.9 = (f32[8,256]{1,0:T(8,128)S(1)}, f32[8,256]{1,0:T(8,128)S(1)}, u32[]{:S(2)}, u32[]{:S(2)}) collective-permute-start(f32[8,256]{1,0:T(8,128)S(1)} %get-tuple-element.34.refs_0_), channel_id=1, source_target_pairs={{0,3},{1,2},{2,1},{3,0},{4,7},{5,6},{6,5},{7,4},{8,11},{9,10},{10,... | collective-permute-start | bytes 24584 | tf_op jit(solution)/shard_map/ppermute | solution.py:230
  20.2 0.4 %collective-permute-start.8 = (f32[8,256]{1,0:T(8,128)S(1)}, f32[8,256]{1,0:T(8,128)S(1)}, u32[]{:S(2)}, u32[]{:S(2)}) collective-permute-start(f32[8,256]{1,0:T(8,128)S(1)} %get-tuple-element.34.refs_0_), channel_id=1, source_target_pairs={{0,2},{1,3},{2,0},{3,1},{4,6},{5,7},{6,4},{7,5},{8,10},{9,11},{10,... | collective-permute-start | bytes 24584 | tf_op jit(solution)/shard_map/ppermute | solution.py:230
  20.6 0.6 %collective-permute-start.7 = (f32[8,256]{1,0:T(8,128)S(1)}, f32[8,256]{1,0:T(8,128)S(1)}, u32[]{:S(2)}, u32[]{:S(2)}) collective-permute-start(f32[8,256]{1,0:T(8,128)S(1)} %get-tuple-element.34.refs_0_), channel_id=1, source_target_pairs={{0,1},{1,0},{2,3},{3,2},{4,5},{5,4},{6,7},{7,6},{8,9},{9,8},{10,11... | collective-permute-start | bytes 24584 | tf_op jit(solution)/shard_map/ppermute | solution.py:230
  21.2 0.7 %copy.19 = f32[8,32,256]{2,1,0:T(8,128)} copy(f32[8,32,256]{2,1,0:T(8,128)S(1)} %get-tuple-element.38) | data formatting | bytes 524288
  21.9 0.3 %collective-permute-done.9.refs_3_ = f32[8,256]{1,0:T(8,128)S(1)} collective-permute-done((f32[8,256]{1,0:T(8,128)S(1)}, f32[8,256]{1,0:T(8,128)S(1)}, u32[]{:S(2)}, u32[]{:S(2)}) %collective-permute-start.9) | collective-permute-done | bytes 8224 | tf_op jit(solution)/shard_map/ppermute | solution.py:230
  22.3 1.6 %collective-permute-done.8.refs_2_ = f32[8,256]{1,0:T(8,128)S(1)} collective-permute-done((f32[8,256]{1,0:T(8,128)S(1)}, f32[8,256]{1,0:T(8,128)S(1)}, u32[]{:S(2)}, u32[]{:S(2)}) %collective-permute-start.8) | collective-permute-done | bytes 8224 | tf_op jit(solution)/shard_map/ppermute | solution.py:230
  23.9 0.4 %collective-permute-done.7.refs_1_ = f32[8,256]{1,0:T(8,128)S(1)} collective-permute-done((f32[8,256]{1,0:T(8,128)S(1)}, f32[8,256]{1,0:T(8,128)S(1)}, u32[]{:S(2)}, u32[]{:S(2)}) %collective-permute-start.7) | collective-permute-done | bytes 8224 | tf_op jit(solution)/shard_map/ppermute | solution.py:230
  24.3 0.9 %gradient_stage.1 = f32[8,256]{1,0:T(8,128)} custom-call(f32[8,256]{1,0:T(8,128)S(1)} %get-tuple-element.34.refs_0_, f32[8,256]{1,0:T(8,128)S(1)} %collective-permute-done.7.refs_1_, f32[8,256]{1,0:T(8,128)S(1)} %collective-permute-done.8.refs_2_, f32[8,256]{1,0:T(8,128)S(1)} %collective-permute-done.9.refs_3_, f32[64,256]{1,0:T(8,128)S(1)} %basis_stage.1.basis.refs_4_, ...), custom_call_target="tpu_custom_call" | custom-call | bytes 65536 | tf_op jit(solution)/shard_map/gradient_stage/pallas_call | solution.py:346
  (17 shorter events, 0.0 us)
Async XLA Ops:
  0.6 3.6 %copy-start.9 = (s32[8]{0:T(128)S(1)}, s32[8]{0:T(128)}, u32[]{:S(2)}) copy-start(s32[8]{0:T(128)} %constant.2.clone.table) | copy-start | bytes 100
  0.6 5.0 %copy-start = (bf16[48,256,512]{2,1,0:T(8,128)(2,1)S(1)}, bf16[48,256,512]{2,1,0:T(8,128)(2,1)}, u32[]{:S(2)}) copy-start(bf16[48,256,512]{2,1,0:T(8,128)(2,1)} %tiles.3) | copy-start | bytes 37748740
  0.7 3.6 %copy-start.8 = (s32[8]{0:T(128)S(1)}, s32[8]{0:T(128)}, u32[]{:S(2)}) copy-start(s32[8]{0:T(128)} %slot.1) | copy-start | bytes 100
  0.7 3.6 %copy-start.7 = (s32[8,1]{0,1:T(1,128)S(1)}, s32[8,1]{0,1:T(1,128)}, u32[]{:S(2)}) copy-start(s32[8,1]{0,1:T(1,128)} %param.15) | copy-start | bytes 100
  0.7 3.6 %copy-start.5 = (s32[48]{0:T(128)S(1)}, s32[48]{0:T(128)}, u32[]{:S(2)}) copy-start(s32[48]{0:T(128)} %src.1) | copy-start | bytes 580
  0.7 3.6 %copy-start.6 = (s32[48]{0:T(128)S(1)}, s32[48]{0:T(128)}, u32[]{:S(2)}) copy-start(s32[48]{0:T(128)} %dst.1) | copy-start | bytes 580
  0.7 7.6 %collective-permute-start.1 = (bf16[8,32,256]{2,1,0:T(8,128)(2,1)}, bf16[8,32,256]{2,1,0:T(8,128)(2,1)S(1)}, u32[]{:S(2)}, u32[]{:S(2)}) collective-permute-start(bf16[8,32,256]{2,1,0:T(8,128)(2,1)} %panels.1), channel_id=1, source_target_pairs={{0,16},{4,20},{8,24},{12,28},{16,0},{20,4},{24,8},{28,12},{1,17},{... | collective-permute-start | bytes 393224 | tf_op jit(solution)/shard_map/ppermute | solution.py:230
  0.8 9.0 %collective-permute-start.2 = (bf16[8,32,256]{2,1,0:T(8,128)(2,1)}, bf16[8,32,256]{2,1,0:T(8,128)(2,1)S(1)}, u32[]{:S(2)}, u32[]{:S(2)}) collective-permute-start(bf16[8,32,256]{2,1,0:T(8,128)(2,1)} %panels.1), channel_id=1, source_target_pairs={{0,8},{4,12},{8,0},{12,4},{16,24},{20,28},{24,16},{28,20},{1,9},{5... | collective-permute-start | bytes 393224 | tf_op jit(solution)/shard_map/ppermute | solution.py:230
  2.7 7.7 %collective-permute-start.3 = (bf16[8,32,256]{2,1,0:T(8,128)(2,1)}, bf16[8,32,256]{2,1,0:T(8,128)(2,1)S(1)}, u32[]{:S(2)}, u32[]{:S(2)}) collective-permute-start(bf16[8,32,256]{2,1,0:T(8,128)(2,1)} %panels.1), channel_id=1, source_target_pairs={{0,4},{4,0},{8,12},{12,8},{16,20},{20,16},{24,28},{28,24},{1,5},{5... | collective-permute-start | bytes 393224 | tf_op jit(solution)/shard_map/ppermute | solution.py:230
  2.7 12.9 %collective-permute-start = (bf16[8,32,256]{2,1,0:T(8,128)(2,1)}, bf16[8,32,256]{2,1,0:T(8,128)(2,1)S(1)}, u32[]{:S(2)}, u32[]{:S(2)}) collective-permute-start(bf16[8,32,256]{2,1,0:T(8,128)(2,1)} %panels.1), channel_id=1, source_target_pairs={{0,24},{4,28},{8,16},{12,20},{16,8},{20,12},{24,0},{28,4},{1,25},{... | collective-permute-start | bytes 393224 | tf_op jit(solution)/shard_map/ppermute | solution.py:230
  5.6 0.9 %copy-start.1 = (bf16[8,32,256]{2,1,0:T(8,128)(2,1)S(1)}, bf16[8,32,256]{2,1,0:T(8,128)(2,1)}, u32[]{:S(2)}) copy-start(bf16[8,32,256]{2,1,0:T(8,128)(2,1)} %panels.1) | copy-start | bytes 393220
  6.5 9.0 %copy-start.3 = (f32[8,6,256]{2,0,1:T(8,128)S(1)}, f32[8,6,256]{2,0,1:T(8,128)}, u32[]{:S(2)}) copy-start(f32[8,6,256]{2,0,1:T(8,128)} %param.13) | copy-start | bytes 147460
  6.5 9.0 %copy-start.4 = (f32[8,256]{1,0:T(8,128)S(1)}, f32[8,256]{1,0:T(8,128)}, u32[]{:S(2)}) copy-start(f32[8,256]{1,0:T(8,128)} %areas) | copy-start | bytes 24580
  7.0 9.9 %copy-start.2 = (bf16[8,32,256]{2,1,0:T(8,128)(2,1)S(1)}, bf16[8,32,256]{2,1,0:T(8,128)(2,1)}, u32[]{:S(2)}) copy-start(bf16[8,32,256]{2,1,0:T(8,128)(2,1)} %panels.1) | copy-start | bytes 393220
  9.8 5.8 %collective-permute-start.6 = (bf16[8,32,256]{2,1,0:T(8,128)(2,1)S(1)}, bf16[8,32,256]{2,1,0:T(8,128)(2,1)S(1)}, u32[]{:S(2)}, u32[]{:S(2)}) collective-permute-start(bf16[8,32,256]{2,1,0:T(8,128)(2,1)S(1)} %collective-permute-done.2.refs_1_), channel_id=1, source_target_pairs={{0,4},{4,0},{8,12},{12,8},{16,20},{20,16},{24,28},{28,24},{1,5},{5... | collective-permute-start | bytes 393224 | tf_op jit(solution)/shard_map/ppermute | solution.py:230
  9.8 5.8 %collective-permute-start.5 = (bf16[8,32,256]{2,1,0:T(8,128)(2,1)S(1)}, bf16[8,32,256]{2,1,0:T(8,128)(2,1)S(1)}, u32[]{:S(2)}, u32[]{:S(2)}) collective-permute-start(bf16[8,32,256]{2,1,0:T(8,128)(2,1)S(1)} %collective-permute-done.1.refs_0_), channel_id=1, source_target_pairs={{0,4},{4,0},{8,12},{12,8},{16,20},{20,16},{24,28},{28,24},{1,5},{5... | collective-permute-start | bytes 393224 | tf_op jit(solution)/shard_map/ppermute | solution.py:230
  15.5 1.3 %collective-permute-start.4 = (bf16[8,32,256]{2,1,0:T(8,128)(2,1)S(1)}, bf16[8,32,256]{2,1,0:T(8,128)(2,1)S(1)}, u32[]{:S(2)}, u32[]{:S(2)}) collective-permute-start(bf16[8,32,256]{2,1,0:T(8,128)(2,1)S(1)} %collective-permute-done.refs_2_), channel_id=1, source_target_pairs={{0,4},{4,0},{8,12},{12,8},{16,20},{20,16},{24,28},{28,24},{1,5},{5... | collective-permute-start | bytes 393224 | tf_op jit(solution)/shard_map/ppermute | solution.py:230
  17.7 4.6 %collective-permute-start.9 = (f32[8,256]{1,0:T(8,128)S(1)}, f32[8,256]{1,0:T(8,128)S(1)}, u32[]{:S(2)}, u32[]{:S(2)}) collective-permute-start(f32[8,256]{1,0:T(8,128)S(1)} %get-tuple-element.34.refs_0_), channel_id=1, source_target_pairs={{0,3},{1,2},{2,1},{3,0},{4,7},{5,6},{6,5},{7,4},{8,11},{9,10},{10,... | collective-permute-start | bytes 24584 | tf_op jit(solution)/shard_map/ppermute | solution.py:230
  20.2 3.7 %collective-permute-start.8 = (f32[8,256]{1,0:T(8,128)S(1)}, f32[8,256]{1,0:T(8,128)S(1)}, u32[]{:S(2)}, u32[]{:S(2)}) collective-permute-start(f32[8,256]{1,0:T(8,128)S(1)} %get-tuple-element.34.refs_0_), channel_id=1, source_target_pairs={{0,2},{1,3},{2,0},{3,1},{4,6},{5,7},{6,4},{7,5},{8,10},{9,11},{10,... | collective-permute-start | bytes 24584 | tf_op jit(solution)/shard_map/ppermute | solution.py:230
  20.6 3.7 %collective-permute-start.7 = (f32[8,256]{1,0:T(8,128)S(1)}, f32[8,256]{1,0:T(8,128)S(1)}, u32[]{:S(2)}, u32[]{:S(2)}) collective-permute-start(f32[8,256]{1,0:T(8,128)S(1)} %get-tuple-element.34.refs_0_), channel_id=1, source_target_pairs={{0,1},{1,0},{2,3},{3,2},{4,5},{5,4},{6,7},{7,6},{8,9},{9,8},{10,11... | collective-permute-start | bytes 24584 | tf_op jit(solution)/shard_map/ppermute | solution.py:230

commit v9 on v8

--- a/solution.py
+++ b/solution.py
@@ -160,6 +160,7 @@
 def near_kernel(stage, region, count, plan, *refs):
     sources = refs[:count]
     tiles, start, total, *held = refs[count:]
+    total[...] = start[...]
     if held:
         fill_panels(sources, held[0])
     add_stage(stage, region, plan, held[0] if held else sources[0], tiles, total)
@@ -167,10 +168,11 @@
 
 def field_kernel(
     stage, region, plan, source, panels, tiles, start, basis, spread,
-    total, field, table, powers, crosses,
+    field, table, powers, crosses, total,
 ):
     block_count, rows_twice, node_count = panels.shape
     freq_count = rows_twice // 2
+    total[...] = start[...]
     add_stage(stage, region, plan, source, tiles, total)
     for block in range(block_count):
         image = total[block]
@@ -294,7 +296,6 @@
             in_specs=[SMEM_SPEC] + [VMEM_SPEC] * (len(sources) + 2),
             out_specs=VMEM_SPEC,
             scratch_shapes=[stacked] if len(sources) > 1 else [],
-            input_output_aliases={len(sources) + 2: 0},
             compiler_params=params(),
             cost_estimate=cost(SMALL),
             name="near_stage",
@@ -322,25 +323,24 @@
     total = forward(late, total)
     total = near(2, total)
 
-    total, field, table, powers, crosses = pl.pallas_call(
+    field, table, powers, crosses = pl.pallas_call(
         functools.partial(field_kernel, 3, region),
         out_shape=(
-            pltpu.VMEM(image_shape, F32),
             pltpu.VMEM(panels.shape, F32),
             pltpu.VMEM(table_shape, F32),
             pltpu.VMEM(power_shape, F32),
             pltpu.VMEM(power_shape, F32),
         ),
         in_specs=[SMEM_SPEC] + [VMEM_SPEC] * 6,
-        out_specs=(VMEM_SPEC,) * 5,
-        input_output_aliases={4: 0},
+        out_specs=(VMEM_SPEC,) * 4,
+        scratch_shapes=[pltpu.VMEM(image_shape, F32)],
         compiler_params=params(),
         cost_estimate=cost(SMALL),
         name="field_stage",
     )(plan, arrived[late + 1], panels, tiles, total, basis, spread)
 
     tables = [table]
-    for distance in range(1, group_count):
+    for distance in range(group_count - 1, 0, -1):
         tables.append(exchange(table, "col", distance))
 
     gradient = pl.pallas_call(

time: 25.6 us -> 25.6 us (level)
  the two profiles are of different devices: /device:TPU:16 before, /device:TPU:0 now
where the time goes in v9:
time: 25.6 us; the launch traced here: 25.1 us
  starting transfers between devices  9.69 us (38%)
  waiting for transfers between devices  7.06 us (28%)
  Pallas kernels  5.95 us (23%)
  local copies, waits for them, and re-layouts  1.64 us (6%)
  between operations  0.8 us (3%)
    ppermute x10, starting transfers between devices, exchange(): return lax.ppermute(values, axis, pairs)  9.69 us
    ppermute x10, waiting for transfers between devices, exchange(): return lax.ppermute(values, axis, pairs)  7.06 us
    pallas_call x3, Pallas kernels, near(): pl.pallas_call(functools.partial(near_kernel, stage, region, len(sources)...  2.64 us
    unnamed x21, local copies, waits for them, and re-layouts  1.64 us
    pallas_call x1, Pallas kernels, shards(): pl.pallas_call(functools.partial(plan_kernel, stages, region, freq_count)...  1.31 us
    pallas_call x1, Pallas kernels, shards(): pl.pallas_call(functools.partial(field_kernel, 3, region), out_shape=(plt...  1.08 us
    pallas_call x1, Pallas kernels, shards(): pl.pallas_call(functools.partial(gradient_kernel, len(tables)), out_shape...  0.91 us
  transfers between devices with their start and end apart: 10, of which 5 were waited for; matrix products, arithmetic and copies ran while one was open for 3% of the time, Pallas kernels for 16%

profile of v9, /device:TPU:0, one launch (start us, length us, event | category | flops | bytes accessed | tf_op | source)
XLA Modules:
  0.0 25.1 jit_solution(12489984735764984513)
XLA Ops:
  0.6 0.0 copy-start.9
  0.6 0.0 copy-start
  0.7 0.0 copy-start.7
  0.7 4.1 %collective-permute-start.1 = (bf16[8,32,256]{2,1,0:T(8,128)(2,1)}, bf16[8,32,256]{2,1,0:T(8,128)(2,1)S(1)}, u32[]{:S(2)}, u32[]{:S(2)}) collective-permute-start(bf16[8,32,256]{2,1,0:T(8,128)(2,1)} %panels.1), channel_id=1, source_target_pairs={{0,16},{4,20},{8,24},{12,28},{16,0},{20,4},{24,8},{28,12},{1,17},{... | collective-permute-start | bytes 393224 | tf_op jit(solution)/shard_map/ppermute | solution.py:232
  4.8 1.6 %collective-permute-start.2 = (bf16[8,32,256]{2,1,0:T(8,128)(2,1)}, bf16[8,32,256]{2,1,0:T(8,128)(2,1)S(1)}, u32[]{:S(2)}, u32[]{:S(2)}) collective-permute-start(bf16[8,32,256]{2,1,0:T(8,128)(2,1)} %panels.1), channel_id=1, source_target_pairs={{0,8},{4,12},{8,0},{12,4},{16,24},{20,28},{24,16},{28,20},{1,9},{5... | collective-permute-start | bytes 393224 | tf_op jit(solution)/shard_map/ppermute | solution.py:232
  6.4 0.0 collective-permute-start.3
  6.4 0.0 collective-permute-start
  6.4 1.3 %plan_stage.1 = (s32[1024]{0:T(1024)S(4)}, f32[9,32,512]{2,1,0:T(8,128)S(1)}, bf16[128,256]{1,0:T(8,128)(2,1)S(1)}, bf16[256,128]{1,0:T(8,128)(2,1)S(1)}) custom-call(s32[8]{0:T(128)S(1)} %copy-done.9, s32[48]{0:T(128)S(1)} %copy-done.5, s32[48]{0:T(128)S(1)} %copy-done.6, s32[8]{0:T(128)S(1)} %bitcast.3, s32[8]{0:T(128)S(1)} %copy-done.8, ...), custom_call_target="tpu_custom_call" | custom-call | bytes 25165824 | tf_op jit(solution)/shard_map/plan_stage/pallas_call | solution.py:275
  7.8 0.0 copy-start.1
  7.8 0.9 %copy-done.1 = bf16[8,32,256]{2,1,0:T(8,128)(2,1)S(1)} copy-done((bf16[8,32,256]{2,1,0:T(8,128)(2,1)S(1)}, bf16[8,32,256]{2,1,0:T(8,128)(2,1)}, u32[]{:S(2)}) %copy-start.1) | copy-done | bytes 131096
  8.7 0.4 %near_stage.3.refs_4_ = f32[9,32,512]{2,1,0:T(8,128)S(1)} custom-call(s32[1024]{0:T(1024)S(4)} %get-tuple-element.21.plan, bf16[8,32,256]{2,1,0:T(8,128)(2,1)S(1)} %copy-done.1, bf16[48,256,512]{2,1,0:T(8,128)(2,1)S(1)} %copy-done, f32[9,32,512]{2,1,0:T(8,128)S(1)} %get-tuple-element.23.refs_2_), custom_call_target="tpu_custom_call" | custom-call | bytes 65536 | tf_op jit(solution)/shard_map/near_stage/pallas_call | solution.py:293
  9.1 3.6 %collective-permute-done.1.refs_0_ = bf16[8,32,256]{2,1,0:T(8,128)(2,1)S(1)} collective-permute-done((bf16[8,32,256]{2,1,0:T(8,128)(2,1)}, bf16[8,32,256]{2,1,0:T(8,128)(2,1)S(1)}, u32[]{:S(2)}, u32[]{:S(2)}) %collective-permute-start.1) | collective-permute-done | bytes 131104 | tf_op jit(solution)/shard_map/ppermute | solution.py:232
  12.7 0.0 collective-permute-done.2.refs_1_
  12.7 0.0 collective-permute-start.6
  12.7 0.5 %collective-permute-start.5 = (bf16[8,32,256]{2,1,0:T(8,128)(2,1)S(1)}, bf16[8,32,256]{2,1,0:T(8,128)(2,1)S(1)}, u32[]{:S(2)}, u32[]{:S(2)}) collective-permute-start(bf16[8,32,256]{2,1,0:T(8,128)(2,1)S(1)} %collective-permute-done.1.refs_0_), channel_id=1, source_target_pairs={{0,4},{4,0},{8,12},{12,8},{16,20},{20,16},{24,28},{28,24},{1,5},{5... | collective-permute-start | bytes 393224 | tf_op jit(solution)/shard_map/ppermute | solution.py:232
  13.3 0.0 collective-permute-done.3.refs_2_
  13.3 0.9 %near_stage.4.refs_4_ = f32[9,32,512]{2,1,0:T(8,128)S(1)} custom-call(s32[1024]{0:T(1024)S(4)} %get-tuple-element.21.plan, bf16[8,32,256]{2,1,0:T(8,128)(2,1)S(1)} %collective-permute-done.1.refs_0_, bf16[8,32,256]{2,1,0:T(8,128)(2,1)S(1)} %collective-permute-done.2.refs_1_, bf16[8,32,256]{2,1,0:T(8,128)(2,1)S(1)} %collective-permute-done.3.refs_2_, ...), custom_call_target="tpu_custom_call" | custom-call | bytes 65536 | tf_op jit(solution)/shard_map/near_stage/pallas_call | solution.py:293
  14.2 1.2 %collective-permute-done.refs_2_ = bf16[8,32,256]{2,1,0:T(8,128)(2,1)S(1)} collective-permute-done((bf16[8,32,256]{2,1,0:T(8,128)(2,1)}, bf16[8,32,256]{2,1,0:T(8,128)(2,1)S(1)}, u32[]{:S(2)}, u32[]{:S(2)}) %collective-permute-start) | collective-permute-done | bytes 131104 | tf_op jit(solution)/shard_map/ppermute | solution.py:232
  15.3 0.0 collective-permute-start.4
  15.4 0.0 collective-permute-done.6.refs_1_
  15.4 0.0 collective-permute-done.5.refs_0_
  15.4 1.3 %near_stage.5.start = f32[9,32,512]{2,1,0:T(8,128)S(1)} custom-call(s32[1024]{0:T(1024)S(4)} %get-tuple-element.21.plan, bf16[8,32,256]{2,1,0:T(8,128)(2,1)S(1)} %collective-permute-done.5.refs_0_, bf16[8,32,256]{2,1,0:T(8,128)(2,1)S(1)} %collective-permute-done.6.refs_1_, bf16[8,32,256]{2,1,0:T(8,128)(2,1)S(1)} %collective-permute-done.refs_2_, ...), custom_call_target="tpu_custom_call" | custom-call | bytes 65536 | tf_op jit(solution)/shard_map/near_stage/pallas_call | solution.py:293
  16.7 0.0 collective-permute-done.4.source
  16.7 1.1 %field_stage.1 = (f32[8,32,256]{2,1,0:T(8,128)S(1)}, f32[8,256]{1,0:T(8,128)S(1)}, f32[128,256]{1,0:T(8,128)S(1)}, f32[128,256]{1,0:T(8,128)S(1)}) custom-call(s32[1024]{0:T(1024)S(4)} %get-tuple-element.21.plan, bf16[8,32,256]{2,1,0:T(8,128)(2,1)S(1)} %collective-permute-done.4.source, bf16[8,32,256]{2,1,0:T(8,128)(2,1)S(1)} %copy-done.2, ...), custom_call_target="tpu_custom_call" | custom-call | bytes 65536 | tf_op jit(solution)/shard_map/field_stage/pallas_call | solution.py:326
  17.8 2.4 %collective-permute-start.7 = (f32[8,256]{1,0:T(8,128)S(1)}, f32[8,256]{1,0:T(8,128)S(1)}, u32[]{:S(2)}, u32[]{:S(2)}) collective-permute-start(f32[8,256]{1,0:T(8,128)S(1)} %get-tuple-element.34.refs_0_), channel_id=1, source_target_pairs={{0,3},{1,2},{2,1},{3,0},{4,7},{5,6},{6,5},{7,4},{8,11},{9,10},{10,... | collective-permute-start | bytes 24584 | tf_op jit(solution)/shard_map/ppermute | solution.py:232
  20.2 0.4 %collective-permute-start.8 = (f32[8,256]{1,0:T(8,128)S(1)}, f32[8,256]{1,0:T(8,128)S(1)}, u32[]{:S(2)}, u32[]{:S(2)}) collective-permute-start(f32[8,256]{1,0:T(8,128)S(1)} %get-tuple-element.34.refs_0_), channel_id=1, source_target_pairs={{0,2},{1,3},{2,0},{3,1},{4,6},{5,7},{6,4},{7,5},{8,10},{9,11},{10,... | collective-permute-start | bytes 24584 | tf_op jit(solution)/shard_map/ppermute | solution.py:232
  20.6 0.7 %collective-permute-start.9 = (f32[8,256]{1,0:T(8,128)S(1)}, f32[8,256]{1,0:T(8,128)S(1)}, u32[]{:S(2)}, u32[]{:S(2)}) collective-permute-start(f32[8,256]{1,0:T(8,128)S(1)} %get-tuple-element.34.refs_0_), channel_id=1, source_target_pairs={{0,1},{1,0},{2,3},{3,2},{4,5},{5,4},{6,7},{7,6},{8,9},{9,8},{10,11... | collective-permute-start | bytes 24584 | tf_op jit(solution)/shard_map/ppermute | solution.py:232
  21.3 0.7 %copy.11 = f32[8,32,256]{2,1,0:T(8,128)} copy(f32[8,32,256]{2,1,0:T(8,128)S(1)} %get-tuple-element.38) | data formatting | bytes 524288
  22.0 0.4 %collective-permute-done.7.refs_1_ = f32[8,256]{1,0:T(8,128)S(1)} collective-permute-done((f32[8,256]{1,0:T(8,128)S(1)}, f32[8,256]{1,0:T(8,128)S(1)}, u32[]{:S(2)}, u32[]{:S(2)}) %collective-permute-start.7) | collective-permute-done | bytes 8224 | tf_op jit(solution)/shard_map/ppermute | solution.py:232
  22.4 1.5 %collective-permute-done.8.refs_2_ = f32[8,256]{1,0:T(8,128)S(1)} collective-permute-done((f32[8,256]{1,0:T(8,128)S(1)}, f32[8,256]{1,0:T(8,128)S(1)}, u32[]{:S(2)}, u32[]{:S(2)}) %collective-permute-start.8) | collective-permute-done | bytes 8224 | tf_op jit(solution)/shard_map/ppermute | solution.py:232
  23.8 0.4 %collective-permute-done.9.refs_3_ = f32[8,256]{1,0:T(8,128)S(1)} collective-permute-done((f32[8,256]{1,0:T(8,128)S(1)}, f32[8,256]{1,0:T(8,128)S(1)}, u32[]{:S(2)}, u32[]{:S(2)}) %collective-permute-start.9) | collective-permute-done | bytes 8224 | tf_op jit(solution)/shard_map/ppermute | solution.py:232
  24.2 0.9 %gradient_stage.1 = f32[8,256]{1,0:T(8,128)} custom-call(f32[8,256]{1,0:T(8,128)S(1)} %get-tuple-element.34.refs_0_, f32[8,256]{1,0:T(8,128)S(1)} %collective-permute-done.7.refs_1_, f32[8,256]{1,0:T(8,128)S(1)} %collective-permute-done.8.refs_2_, f32[8,256]{1,0:T(8,128)S(1)} %collective-permute-done.9.refs_3_, f32[64,256]{1,0:T(8,128)S(1)} %basis_stage.1.basis.refs_4_, ...), custom_call_target="tpu_custom_call" | custom-call | bytes 65536 | tf_op jit(solution)/shard_map/gradient_stage/pallas_call | solution.py:346
  (17 shorter events, 0.0 us)
Async XLA Ops:
  0.6 5.8 %copy-start.9 = (s32[8]{0:T(128)S(1)}, s32[8]{0:T(128)}, u32[]{:S(2)}) copy-start(s32[8]{0:T(128)} %constant.2.clone.table) | copy-start | bytes 100
  0.6 7.1 %copy-start = (bf16[48,256,512]{2,1,0:T(8,128)(2,1)S(1)}, bf16[48,256,512]{2,1,0:T(8,128)(2,1)}, u32[]{:S(2)}) copy-start(bf16[48,256,512]{2,1,0:T(8,128)(2,1)} %tiles.3) | copy-start | bytes 37748740
  0.7 5.7 %copy-start.7 = (s32[8,1]{0,1:T(1,128)S(1)}, s32[8,1]{0,1:T(1,128)}, u32[]{:S(2)}) copy-start(s32[8,1]{0,1:T(1,128)} %param.15) | copy-start | bytes 100
  0.7 5.7 %copy-start.6 = (s32[48]{0:T(128)S(1)}, s32[48]{0:T(128)}, u32[]{:S(2)}) copy-start(s32[48]{0:T(128)} %dst.1) | copy-start | bytes 580
  0.7 5.7 %copy-start.5 = (s32[48]{0:T(128)S(1)}, s32[48]{0:T(128)}, u32[]{:S(2)}) copy-start(s32[48]{0:T(128)} %src.1) | copy-start | bytes 580
  0.7 5.7 %copy-start.8 = (s32[8]{0:T(128)S(1)}, s32[8]{0:T(128)}, u32[]{:S(2)}) copy-start(s32[8]{0:T(128)} %slot.1) | copy-start | bytes 100
  0.7 12.0 %collective-permute-start.1 = (bf16[8,32,256]{2,1,0:T(8,128)(2,1)}, bf16[8,32,256]{2,1,0:T(8,128)(2,1)S(1)}, u32[]{:S(2)}, u32[]{:S(2)}) collective-permute-start(bf16[8,32,256]{2,1,0:T(8,128)(2,1)} %panels.1), channel_id=1, source_target_pairs={{0,16},{4,20},{8,24},{12,28},{16,0},{20,4},{24,8},{28,12},{1,17},{... | collective-permute-start | bytes 393224 | tf_op jit(solution)/shard_map/ppermute | solution.py:232
  4.8 7.9 %collective-permute-start.2 = (bf16[8,32,256]{2,1,0:T(8,128)(2,1)}, bf16[8,32,256]{2,1,0:T(8,128)(2,1)S(1)}, u32[]{:S(2)}, u32[]{:S(2)}) collective-permute-start(bf16[8,32,256]{2,1,0:T(8,128)(2,1)} %panels.1), channel_id=1, source_target_pairs={{0,8},{4,12},{8,0},{12,4},{16,24},{20,28},{24,16},{28,20},{1,9},{5... | collective-permute-start | bytes 393224 | tf_op jit(solution)/shard_map/ppermute | solution.py:232
  6.4 6.9 %collective-permute-start.3 = (bf16[8,32,256]{2,1,0:T(8,128)(2,1)}, bf16[8,32,256]{2,1,0:T(8,128)(2,1)S(1)}, u32[]{:S(2)}, u32[]{:S(2)}) collective-permute-start(bf16[8,32,256]{2,1,0:T(8,128)(2,1)} %panels.1), channel_id=1, source_target_pairs={{0,4},{4,0},{8,12},{12,8},{16,20},{20,16},{24,28},{28,24},{1,5},{5... | collective-permute-start | bytes 393224 | tf_op jit(solution)/shard_map/ppermute | solution.py:232
  6.4 9.0 %collective-permute-start = (bf16[8,32,256]{2,1,0:T(8,128)(2,1)}, bf16[8,32,256]{2,1,0:T(8,128)(2,1)S(1)}, u32[]{:S(2)}, u32[]{:S(2)}) collective-permute-start(bf16[8,32,256]{2,1,0:T(8,128)(2,1)} %panels.1), channel_id=1, source_target_pairs={{0,24},{4,28},{8,16},{12,20},{16,8},{20,12},{24,0},{28,4},{1,25},{... | collective-permute-start | bytes 393224 | tf_op jit(solution)/shard_map/ppermute | solution.py:232
  7.8 0.9 %copy-start.1 = (bf16[8,32,256]{2,1,0:T(8,128)(2,1)S(1)}, bf16[8,32,256]{2,1,0:T(8,128)(2,1)}, u32[]{:S(2)}) copy-start(bf16[8,32,256]{2,1,0:T(8,128)(2,1)} %panels.1) | copy-start | bytes 393220
  8.7 6.7 %copy-start.3 = (f32[8,6,256]{2,0,1:T(8,128)S(1)}, f32[8,6,256]{2,0,1:T(8,128)}, u32[]{:S(2)}) copy-start(f32[8,6,256]{2,0,1:T(8,128)} %param.13) | copy-start | bytes 147460
  8.7 6.7 %copy-start.4 = (f32[8,256]{1,0:T(8,128)S(1)}, f32[8,256]{1,0:T(8,128)}, u32[]{:S(2)}) copy-start(f32[8,256]{1,0:T(8,128)} %areas) | copy-start | bytes 24580
  9.1 7.6 %copy-start.2 = (bf16[8,32,256]{2,1,0:T(8,128)(2,1)S(1)}, bf16[8,32,256]{2,1,0:T(8,128)(2,1)}, u32[]{:S(2)}) copy-start(bf16[8,32,256]{2,1,0:T(8,128)(2,1)} %panels.1) | copy-start | bytes 393220
  12.7 2.6 %collective-permute-start.6 = (bf16[8,32,256]{2,1,0:T(8,128)(2,1)S(1)}, bf16[8,32,256]{2,1,0:T(8,128)(2,1)S(1)}, u32[]{:S(2)}, u32[]{:S(2)}) collective-permute-start(bf16[8,32,256]{2,1,0:T(8,128)(2,1)S(1)} %collective-permute-done.2.refs_1_), channel_id=1, source_target_pairs={{0,4},{4,0},{8,12},{12,8},{16,20},{20,16},{24,28},{28,24},{1,5},{5... | collective-permute-start | bytes 393224 | tf_op jit(solution)/shard_map/ppermute | solution.py:232
  12.7 2.6 %collective-permute-start.5 = (bf16[8,32,256]{2,1,0:T(8,128)(2,1)S(1)}, bf16[8,32,256]{2,1,0:T(8,128)(2,1)S(1)}, u32[]{:S(2)}, u32[]{:S(2)}) collective-permute-start(bf16[8,32,256]{2,1,0:T(8,128)(2,1)S(1)} %collective-permute-done.1.refs_0_), channel_id=1, source_target_pairs={{0,4},{4,0},{8,12},{12,8},{16,20},{20,16},{24,28},{28,24},{1,5},{5... | collective-permute-start | bytes 393224 | tf_op jit(solution)/shard_map/ppermute | solution.py:232
  15.3 1.4 %collective-permute-start.4 = (bf16[8,32,256]{2,1,0:T(8,128)(2,1)S(1)}, bf16[8,32,256]{2,1,0:T(8,128)(2,1)S(1)}, u32[]{:S(2)}, u32[]{:S(2)}) collective-permute-start(bf16[8,32,256]{2,1,0:T(8,128)(2,1)S(1)} %collective-permute-done.refs_2_), channel_id=1, source_target_pairs={{0,4},{4,0},{8,12},{12,8},{16,20},{20,16},{24,28},{28,24},{1,5},{5... | collective-permute-start | bytes 393224 | tf_op jit(solution)/shard_map/ppermute | solution.py:232
  17.8 4.6 %collective-permute-start.7 = (f32[8,256]{1,0:T(8,128)S(1)}, f32[8,256]{1,0:T(8,128)S(1)}, u32[]{:S(2)}, u32[]{:S(2)}) collective-permute-start(f32[8,256]{1,0:T(8,128)S(1)} %get-tuple-element.34.refs_0_), channel_id=1, source_target_pairs={{0,3},{1,2},{2,1},{3,0},{4,7},{5,6},{6,5},{7,4},{8,11},{9,10},{10,... | collective-permute-start | bytes 24584 | tf_op jit(solution)/shard_map/ppermute | solution.py:232
  20.2 3.7 %collective-permute-start.8 = (f32[8,256]{1,0:T(8,128)S(1)}, f32[8,256]{1,0:T(8,128)S(1)}, u32[]{:S(2)}, u32[]{:S(2)}) collective-permute-start(f32[8,256]{1,0:T(8,128)S(1)} %get-tuple-element.34.refs_0_), channel_id=1, source_target_pairs={{0,2},{1,3},{2,0},{3,1},{4,6},{5,7},{6,4},{7,5},{8,10},{9,11},{10,... | collective-permute-start | bytes 24584 | tf_op jit(solution)/shard_map/ppermute | solution.py:232
  20.6 3.7 %collective-permute-start.9 = (f32[8,256]{1,0:T(8,128)S(1)}, f32[8,256]{1,0:T(8,128)S(1)}, u32[]{:S(2)}, u32[]{:S(2)}) collective-permute-start(f32[8,256]{1,0:T(8,128)S(1)} %get-tuple-element.34.refs_0_), channel_id=1, source_target_pairs={{0,1},{1,0},{2,3},{3,2},{4,5},{5,4},{6,7},{7,6},{8,9},{9,8},{10,11... | collective-permute-start | bytes 24584 | tf_op jit(solution)/shard_map/ppermute | solution.py:232

commit v10 on v9

--- a/solution.py
+++ b/solution.py
@@ -9,7 +9,7 @@
 
 PD = 4
 EPSILON = 1e-05
-UNROLL = 8
+UNROLL = 16
 MOMENTS = 8
 SMALL = 1 << 16
 STAGE_SHIFT = 16

time: 25.6 us -> 25.5 us (level)
  transfers between devices with their start and end apart: 10 -> 10, of which waited for: 5 -> 6; matrix products, arithmetic and copies ran while one was open for 3% -> 3% of each run, Pallas kernels for 16% -> 16%
where the time goes in v10:
time: 25.5 us; the launch traced here: 25.2 us
  starting transfers between devices  9.69 us (38%)
  waiting for transfers between devices  7.25 us (28%)
  Pallas kernels  5.81 us (23%)
  local copies, waits for them, and re-layouts  1.64 us (6%)
  between operations  0.82 us (3%)
    ppermute x10, starting transfers between devices, exchange(): return lax.ppermute(values, axis, pairs)  9.69 us
    ppermute x10, waiting for transfers between devices, exchange(): return lax.ppermute(values, axis, pairs)  7.25 us
    pallas_call x3, Pallas kernels, near(): pl.pallas_call(functools.partial(near_kernel, stage, region, len(sources)...  2.63 us
    unnamed x21, local copies, waits for them, and re-layouts  1.64 us
    pallas_call x1, Pallas kernels, shards(): pl.pallas_call(functools.partial(plan_kernel, stages, region, freq_count)...  1.36 us
    pallas_call x1, Pallas kernels, shards(): pl.pallas_call(functools.partial(gradient_kernel, len(tables)), out_shape...  0.91 us
    pallas_call x1, Pallas kernels, shards(): pl.pallas_call(functools.partial(field_kernel, 3, region), out_shape=(plt...  0.9 us
  transfers between devices with their start and end apart: 10, of which 6 were waited for; matrix products, arithmetic and copies ran while one was open for 3% of the time, Pallas kernels for 16%

profile of v10, /device:TPU:0, one launch (start us, length us, event | category | flops | bytes accessed | tf_op | source)
XLA Modules:
  0.0 25.2 jit_solution(13925184270441727802)
XLA Ops:
  0.6 0.0 copy-start.9
  0.6 0.0 copy-start
  0.7 4.1 %collective-permute-start.1 = (bf16[8,32,256]{2,1,0:T(8,128)(2,1)}, bf16[8,32,256]{2,1,0:T(8,128)(2,1)S(1)}, u32[]{:S(2)}, u32[]{:S(2)}) collective-permute-start(bf16[8,32,256]{2,1,0:T(8,128)(2,1)} %panels.1), channel_id=1, source_target_pairs={{0,16},{4,20},{8,24},{12,28},{16,0},{20,4},{24,8},{28,12},{1,17},{... | collective-permute-start | bytes 393224 | tf_op jit(solution)/shard_map/ppermute | solution.py:232
  4.8 1.6 %collective-permute-start.2 = (bf16[8,32,256]{2,1,0:T(8,128)(2,1)}, bf16[8,32,256]{2,1,0:T(8,128)(2,1)S(1)}, u32[]{:S(2)}, u32[]{:S(2)}) collective-permute-start(bf16[8,32,256]{2,1,0:T(8,128)(2,1)} %panels.1), channel_id=1, source_target_pairs={{0,8},{4,12},{8,0},{12,4},{16,24},{20,28},{24,16},{28,20},{1,9},{5... | collective-permute-start | bytes 393224 | tf_op jit(solution)/shard_map/ppermute | solution.py:232
  6.4 0.0 collective-permute-start.3
  6.4 0.0 collective-permute-start
  6.4 1.4 %plan_stage.1 = (s32[1024]{0:T(1024)S(4)}, f32[9,32,512]{2,1,0:T(8,128)S(1)}, bf16[128,256]{1,0:T(8,128)(2,1)S(1)}, bf16[256,128]{1,0:T(8,128)(2,1)S(1)}) custom-call(s32[8]{0:T(128)S(1)} %copy-done.9, s32[48]{0:T(128)S(1)} %copy-done.5, s32[48]{0:T(128)S(1)} %copy-done.6, s32[8]{0:T(128)S(1)} %bitcast.3, s32[8]{0:T(128)S(1)} %copy-done.8, ...), custom_call_target="tpu_custom_call" | custom-call | bytes 25165824 | tf_op jit(solution)/shard_map/plan_stage/pallas_call | solution.py:275
  7.8 0.0 copy-start.1
  7.8 0.9 %copy-done.1 = bf16[8,32,256]{2,1,0:T(8,128)(2,1)S(1)} copy-done((bf16[8,32,256]{2,1,0:T(8,128)(2,1)S(1)}, bf16[8,32,256]{2,1,0:T(8,128)(2,1)}, u32[]{:S(2)}) %copy-start.1) | copy-done | bytes 131096
  8.7 0.3 %near_stage.3.refs_4_ = f32[9,32,512]{2,1,0:T(8,128)S(1)} custom-call(s32[1024]{0:T(1024)S(4)} %get-tuple-element.21.plan, bf16[8,32,256]{2,1,0:T(8,128)(2,1)S(1)} %copy-done.1, bf16[48,256,512]{2,1,0:T(8,128)(2,1)S(1)} %copy-done, f32[9,32,512]{2,1,0:T(8,128)S(1)} %get-tuple-element.23.refs_2_), custom_call_target="tpu_custom_call" | custom-call | bytes 65536 | tf_op jit(solution)/shard_map/near_stage/pallas_call | solution.py:293
  9.1 0.0 copy-start.2
  9.1 3.7 %collective-permute-done.1.refs_0_ = bf16[8,32,256]{2,1,0:T(8,128)(2,1)S(1)} collective-permute-done((bf16[8,32,256]{2,1,0:T(8,128)(2,1)}, bf16[8,32,256]{2,1,0:T(8,128)(2,1)S(1)}, u32[]{:S(2)}, u32[]{:S(2)}) %collective-permute-start.1) | collective-permute-done | bytes 131104 | tf_op jit(solution)/shard_map/ppermute | solution.py:232
  12.7 0.0 collective-permute-done.2.refs_1_
  12.7 0.0 collective-permute-start.6
  12.7 0.5 %collective-permute-start.5 = (bf16[8,32,256]{2,1,0:T(8,128)(2,1)S(1)}, bf16[8,32,256]{2,1,0:T(8,128)(2,1)S(1)}, u32[]{:S(2)}, u32[]{:S(2)}) collective-permute-start(bf16[8,32,256]{2,1,0:T(8,128)(2,1)S(1)} %collective-permute-done.1.refs_0_), channel_id=1, source_target_pairs={{0,4},{4,0},{8,12},{12,8},{16,20},{20,16},{24,28},{28,24},{1,5},{5... | collective-permute-start | bytes 393224 | tf_op jit(solution)/shard_map/ppermute | solution.py:232
  13.3 0.0 collective-permute-done.3.refs_2_
  13.3 1.2 %near_stage.4.refs_4_ = f32[9,32,512]{2,1,0:T(8,128)S(1)} custom-call(s32[1024]{0:T(1024)S(4)} %get-tuple-element.21.plan, bf16[8,32,256]{2,1,0:T(8,128)(2,1)S(1)} %collective-permute-done.1.refs_0_, bf16[8,32,256]{2,1,0:T(8,128)(2,1)S(1)} %collective-permute-done.2.refs_1_, bf16[8,32,256]{2,1,0:T(8,128)(2,1)S(1)} %collective-permute-done.3.refs_2_, ...), custom_call_target="tpu_custom_call" | custom-call | bytes 65536 | tf_op jit(solution)/shard_map/near_stage/pallas_call | solution.py:293
  14.5 0.9 %collective-permute-done.refs_2_ = bf16[8,32,256]{2,1,0:T(8,128)(2,1)S(1)} collective-permute-done((bf16[8,32,256]{2,1,0:T(8,128)(2,1)}, bf16[8,32,256]{2,1,0:T(8,128)(2,1)S(1)}, u32[]{:S(2)}, u32[]{:S(2)}) %collective-permute-start) | collective-permute-done | bytes 131104 | tf_op jit(solution)/shard_map/ppermute | solution.py:232
  15.3 0.0 collective-permute-start.4
  15.4 0.0 collective-permute-done.6.refs_1_
  15.4 0.0 collective-permute-done.5.refs_0_
  15.4 1.1 %near_stage.5.start = f32[9,32,512]{2,1,0:T(8,128)S(1)} custom-call(s32[1024]{0:T(1024)S(4)} %get-tuple-element.21.plan, bf16[8,32,256]{2,1,0:T(8,128)(2,1)S(1)} %collective-permute-done.5.refs_0_, bf16[8,32,256]{2,1,0:T(8,128)(2,1)S(1)} %collective-permute-done.6.refs_1_, bf16[8,32,256]{2,1,0:T(8,128)(2,1)S(1)} %collective-permute-done.refs_2_, ...), custom_call_target="tpu_custom_call" | custom-call | bytes 65536 | tf_op jit(solution)/shard_map/near_stage/pallas_call | solution.py:293
  16.5 0.2 collective-permute-done.4.source
  16.7 0.9 %field_stage.1 = (f32[8,32,256]{2,1,0:T(8,128)S(1)}, f32[8,256]{1,0:T(8,128)S(1)}, f32[128,256]{1,0:T(8,128)S(1)}, f32[128,256]{1,0:T(8,128)S(1)}) custom-call(s32[1024]{0:T(1024)S(4)} %get-tuple-element.21.plan, bf16[8,32,256]{2,1,0:T(8,128)(2,1)S(1)} %collective-permute-done.4.source, bf16[8,32,256]{2,1,0:T(8,128)(2,1)S(1)} %copy-done.2, ...), custom_call_target="tpu_custom_call" | custom-call | bytes 65536 | tf_op jit(solution)/shard_map/field_stage/pallas_call | solution.py:326
  17.6 2.4 %collective-permute-start.7 = (f32[8,256]{1,0:T(8,128)S(1)}, f32[8,256]{1,0:T(8,128)S(1)}, u32[]{:S(2)}, u32[]{:S(2)}) collective-permute-start(f32[8,256]{1,0:T(8,128)S(1)} %get-tuple-element.34.refs_0_), channel_id=1, source_target_pairs={{0,3},{1,2},{2,1},{3,0},{4,7},{5,6},{6,5},{7,4},{8,11},{9,10},{10,... | collective-permute-start | bytes 24584 | tf_op jit(solution)/shard_map/ppermute | solution.py:232
  20.0 0.7 %collective-permute-start.8 = (f32[8,256]{1,0:T(8,128)S(1)}, f32[8,256]{1,0:T(8,128)S(1)}, u32[]{:S(2)}, u32[]{:S(2)}) collective-permute-start(f32[8,256]{1,0:T(8,128)S(1)} %get-tuple-element.34.refs_0_), channel_id=1, source_target_pairs={{0,2},{1,3},{2,0},{3,1},{4,6},{5,7},{6,4},{7,5},{8,10},{9,11},{10,... | collective-permute-start | bytes 24584 | tf_op jit(solution)/shard_map/ppermute | solution.py:232
  20.7 0.4 %collective-permute-start.9 = (f32[8,256]{1,0:T(8,128)S(1)}, f32[8,256]{1,0:T(8,128)S(1)}, u32[]{:S(2)}, u32[]{:S(2)}) collective-permute-start(f32[8,256]{1,0:T(8,128)S(1)} %get-tuple-element.34.refs_0_), channel_id=1, source_target_pairs={{0,1},{1,0},{2,3},{3,2},{4,5},{5,4},{6,7},{7,6},{8,9},{9,8},{10,11... | collective-permute-start | bytes 24584 | tf_op jit(solution)/shard_map/ppermute | solution.py:232
  21.1 0.7 %copy.11 = f32[8,32,256]{2,1,0:T(8,128)} copy(f32[8,32,256]{2,1,0:T(8,128)S(1)} %get-tuple-element.38) | data formatting | bytes 524288
  21.8 0.4 %collective-permute-done.7.refs_1_ = f32[8,256]{1,0:T(8,128)S(1)} collective-permute-done((f32[8,256]{1,0:T(8,128)S(1)}, f32[8,256]{1,0:T(8,128)S(1)}, u32[]{:S(2)}, u32[]{:S(2)}) %collective-permute-start.7) | collective-permute-done | bytes 8224 | tf_op jit(solution)/shard_map/ppermute | solution.py:232
  22.2 1.4 %collective-permute-done.8.refs_2_ = f32[8,256]{1,0:T(8,128)S(1)} collective-permute-done((f32[8,256]{1,0:T(8,128)S(1)}, f32[8,256]{1,0:T(8,128)S(1)}, u32[]{:S(2)}, u32[]{:S(2)}) %collective-permute-start.8) | collective-permute-done | bytes 8224 | tf_op jit(solution)/shard_map/ppermute | solution.py:232
  23.6 0.7 %collective-permute-done.9.refs_3_ = f32[8,256]{1,0:T(8,128)S(1)} collective-permute-done((f32[8,256]{1,0:T(8,128)S(1)}, f32[8,256]{1,0:T(8,128)S(1)}, u32[]{:S(2)}, u32[]{:S(2)}) %collective-permute-start.9) | collective-permute-done | bytes 8224 | tf_op jit(solution)/shard_map/ppermute | solution.py:232
  24.3 0.9 %gradient_stage.1 = f32[8,256]{1,0:T(8,128)} custom-call(f32[8,256]{1,0:T(8,128)S(1)} %get-tuple-element.34.refs_0_, f32[8,256]{1,0:T(8,128)S(1)} %collective-permute-done.7.refs_1_, f32[8,256]{1,0:T(8,128)S(1)} %collective-permute-done.8.refs_2_, f32[8,256]{1,0:T(8,128)S(1)} %collective-permute-done.9.refs_3_, f32[64,256]{1,0:T(8,128)S(1)} %basis_stage.1.basis.refs_4_, ...), custom_call_target="tpu_custom_call" | custom-call | bytes 65536 | tf_op jit(solution)/shard_map/gradient_stage/pallas_call | solution.py:346
  (17 shorter events, 0.0 us)
Async XLA Ops:
  0.6 5.8 %copy-start.9 = (s32[8]{0:T(128)S(1)}, s32[8]{0:T(128)}, u32[]{:S(2)}) copy-start(s32[8]{0:T(128)} %constant.2.clone.table) | copy-start | bytes 100
  0.6 7.2 %copy-start = (bf16[48,256,512]{2,1,0:T(8,128)(2,1)S(1)}, bf16[48,256,512]{2,1,0:T(8,128)(2,1)}, u32[]{:S(2)}) copy-start(bf16[48,256,512]{2,1,0:T(8,128)(2,1)} %tiles.3) | copy-start | bytes 37748740
  0.7 5.7 %copy-start.7 = (s32[8,1]{0,1:T(1,128)S(1)}, s32[8,1]{0,1:T(1,128)}, u32[]{:S(2)}) copy-start(s32[8,1]{0,1:T(1,128)} %param.15) | copy-start | bytes 100
  0.7 5.7 %copy-start.6 = (s32[48]{0:T(128)S(1)}, s32[48]{0:T(128)}, u32[]{:S(2)}) copy-start(s32[48]{0:T(128)} %dst.1) | copy-start | bytes 580
  0.7 5.7 %copy-start.5 = (s32[48]{0:T(128)S(1)}, s32[48]{0:T(128)}, u32[]{:S(2)}) copy-start(s32[48]{0:T(128)} %src.1) | copy-start | bytes 580
  0.7 5.7 %copy-start.8 = (s32[8]{0:T(128)S(1)}, s32[8]{0:T(128)}, u32[]{:S(2)}) copy-start(s32[8]{0:T(128)} %slot.1) | copy-start | bytes 100
  0.7 12.0 %collective-permute-start.1 = (bf16[8,32,256]{2,1,0:T(8,128)(2,1)}, bf16[8,32,256]{2,1,0:T(8,128)(2,1)S(1)}, u32[]{:S(2)}, u32[]{:S(2)}) collective-permute-start(bf16[8,32,256]{2,1,0:T(8,128)(2,1)} %panels.1), channel_id=1, source_target_pairs={{0,16},{4,20},{8,24},{12,28},{16,0},{20,4},{24,8},{28,12},{1,17},{... | collective-permute-start | bytes 393224 | tf_op jit(solution)/shard_map/ppermute | solution.py:232
  4.8 7.9 %collective-permute-start.2 = (bf16[8,32,256]{2,1,0:T(8,128)(2,1)}, bf16[8,32,256]{2,1,0:T(8,128)(2,1)S(1)}, u32[]{:S(2)}, u32[]{:S(2)}) collective-permute-start(bf16[8,32,256]{2,1,0:T(8,128)(2,1)} %panels.1), channel_id=1, source_target_pairs={{0,8},{4,12},{8,0},{12,4},{16,24},{20,28},{24,16},{28,20},{1,9},{5... | collective-permute-start | bytes 393224 | tf_op jit(solution)/shard_map/ppermute | solution.py:232
  6.4 6.9 %collective-permute-start.3 = (bf16[8,32,256]{2,1,0:T(8,128)(2,1)}, bf16[8,32,256]{2,1,0:T(8,128)(2,1)S(1)}, u32[]{:S(2)}, u32[]{:S(2)}) collective-permute-start(bf16[8,32,256]{2,1,0:T(8,128)(2,1)} %panels.1), channel_id=1, source_target_pairs={{0,4},{4,0},{8,12},{12,8},{16,20},{20,16},{24,28},{28,24},{1,5},{5... | collective-permute-start | bytes 393224 | tf_op jit(solution)/shard_map/ppermute | solution.py:232
  6.4 9.0 %collective-permute-start = (bf16[8,32,256]{2,1,0:T(8,128)(2,1)}, bf16[8,32,256]{2,1,0:T(8,128)(2,1)S(1)}, u32[]{:S(2)}, u32[]{:S(2)}) collective-permute-start(bf16[8,32,256]{2,1,0:T(8,128)(2,1)} %panels.1), channel_id=1, source_target_pairs={{0,24},{4,28},{8,16},{12,20},{16,8},{20,12},{24,0},{28,4},{1,25},{... | collective-permute-start | bytes 393224 | tf_op jit(solution)/shard_map/ppermute | solution.py:232
  7.8 0.9 %copy-start.1 = (bf16[8,32,256]{2,1,0:T(8,128)(2,1)S(1)}, bf16[8,32,256]{2,1,0:T(8,128)(2,1)}, u32[]{:S(2)}) copy-start(bf16[8,32,256]{2,1,0:T(8,128)(2,1)} %panels.1) | copy-start | bytes 393220
  8.7 6.6 %copy-start.3 = (f32[8,6,256]{2,0,1:T(8,128)S(1)}, f32[8,6,256]{2,0,1:T(8,128)}, u32[]{:S(2)}) copy-start(f32[8,6,256]{2,0,1:T(8,128)} %param.13) | copy-start | bytes 147460
  8.7 6.6 %copy-start.4 = (f32[8,256]{1,0:T(8,128)S(1)}, f32[8,256]{1,0:T(8,128)}, u32[]{:S(2)}) copy-start(f32[8,256]{1,0:T(8,128)} %areas) | copy-start | bytes 24580
  9.1 7.6 %copy-start.2 = (bf16[8,32,256]{2,1,0:T(8,128)(2,1)S(1)}, bf16[8,32,256]{2,1,0:T(8,128)(2,1)}, u32[]{:S(2)}) copy-start(bf16[8,32,256]{2,1,0:T(8,128)(2,1)} %panels.1) | copy-start | bytes 393220
  12.7 2.6 %collective-permute-start.6 = (bf16[8,32,256]{2,1,0:T(8,128)(2,1)S(1)}, bf16[8,32,256]{2,1,0:T(8,128)(2,1)S(1)}, u32[]{:S(2)}, u32[]{:S(2)}) collective-permute-start(bf16[8,32,256]{2,1,0:T(8,128)(2,1)S(1)} %collective-permute-done.2.refs_1_), channel_id=1, source_target_pairs={{0,4},{4,0},{8,12},{12,8},{16,20},{20,16},{24,28},{28,24},{1,5},{5... | collective-permute-start | bytes 393224 | tf_op jit(solution)/shard_map/ppermute | solution.py:232
  12.7 2.6 %collective-permute-start.5 = (bf16[8,32,256]{2,1,0:T(8,128)(2,1)S(1)}, bf16[8,32,256]{2,1,0:T(8,128)(2,1)S(1)}, u32[]{:S(2)}, u32[]{:S(2)}) collective-permute-start(bf16[8,32,256]{2,1,0:T(8,128)(2,1)S(1)} %collective-permute-done.1.refs_0_), channel_id=1, source_target_pairs={{0,4},{4,0},{8,12},{12,8},{16,20},{20,16},{24,28},{28,24},{1,5},{5... | collective-permute-start | bytes 393224 | tf_op jit(solution)/shard_map/ppermute | solution.py:232
  15.3 1.3 %collective-permute-start.4 = (bf16[8,32,256]{2,1,0:T(8,128)(2,1)S(1)}, bf16[8,32,256]{2,1,0:T(8,128)(2,1)S(1)}, u32[]{:S(2)}, u32[]{:S(2)}) collective-permute-start(bf16[8,32,256]{2,1,0:T(8,128)(2,1)S(1)} %collective-permute-done.refs_2_), channel_id=1, source_target_pairs={{0,4},{4,0},{8,12},{12,8},{16,20},{20,16},{24,28},{28,24},{1,5},{5... | collective-permute-start | bytes 393224 | tf_op jit(solution)/shard_map/ppermute | solution.py:232
  17.6 4.6 %collective-permute-start.7 = (f32[8,256]{1,0:T(8,128)S(1)}, f32[8,256]{1,0:T(8,128)S(1)}, u32[]{:S(2)}, u32[]{:S(2)}) collective-permute-start(f32[8,256]{1,0:T(8,128)S(1)} %get-tuple-element.34.refs_0_), channel_id=1, source_target_pairs={{0,3},{1,2},{2,1},{3,0},{4,7},{5,6},{6,5},{7,4},{8,11},{9,10},{10,... | collective-permute-start | bytes 24584 | tf_op jit(solution)/shard_map/ppermute | solution.py:232
  20.0 3.7 %collective-permute-start.8 = (f32[8,256]{1,0:T(8,128)S(1)}, f32[8,256]{1,0:T(8,128)S(1)}, u32[]{:S(2)}, u32[]{:S(2)}) collective-permute-start(f32[8,256]{1,0:T(8,128)S(1)} %get-tuple-element.34.refs_0_), channel_id=1, source_target_pairs={{0,2},{1,3},{2,0},{3,1},{4,6},{5,7},{6,4},{7,5},{8,10},{9,11},{10,... | collective-permute-start | bytes 24584 | tf_op jit(solution)/shard_map/ppermute | solution.py:232
  20.7 3.7 %collective-permute-start.9 = (f32[8,256]{1,0:T(8,128)S(1)}, f32[8,256]{1,0:T(8,128)S(1)}, u32[]{:S(2)}, u32[]{:S(2)}) collective-permute-start(f32[8,256]{1,0:T(8,128)S(1)} %get-tuple-element.34.refs_0_), channel_id=1, source_target_pairs={{0,1},{1,0},{2,3},{3,2},{4,5},{5,4},{6,7},{7,6},{8,9},{9,8},{10,11... | collective-permute-start | bytes 24584 | tf_op jit(solution)/shard_map/ppermute | solution.py:232

commit v11 on v10

--- a/solution.py
+++ b/solution.py
@@ -168,7 +168,7 @@
 
 def field_kernel(
     stage, region, plan, source, panels, tiles, start, basis, spread,
-    field, table, powers, crosses, total,
+    total, table, powers, crosses,
 ):
     block_count, rows_twice, node_count = panels.shape
     freq_count = rows_twice // 2
@@ -184,8 +184,6 @@
         imag = 0.5 * imag_in + (
             image[:freq_count, node_count:] + image[freq_count:, :node_count]
         )
-        field[block, :freq_count] = real
-        field[block, freq_count:] = imag
         span = slice(block * freq_count, (block + 1) * freq_count)
         powers[span] = real * real + imag * imag
         crosses[span] = real_in * real + imag_in * imag
@@ -201,6 +199,20 @@
     moments = jnp.concatenate(pieces, axis=0)
     joined = dot(jnp.concatenate(parts_of(moments, 3), axis=0), spread[...])
     table[...] = joined[:MOMENTS] + (joined[MOMENTS : 2 * MOMENTS] + joined[2 * MOMENTS :])
+
+
+def write_kernel(panels, total, field):
+    block_count, rows_twice, node_count = panels.shape
+    freq_count = rows_twice // 2
+    for block in range(block_count):
+        image = total[block]
+        incident = panels[block].astype(F32)
+        field[block, :freq_count] = 0.5 * incident[:freq_count] + (
+            image[:freq_count, :node_count] - image[freq_count:, node_count:]
+        )
+        field[block, freq_count:] = 0.5 * incident[freq_count:] + (
+            image[:freq_count, node_count:] + image[freq_count:, :node_count]
+        )
 
 
 def gradient_kernel(count, *refs):
@@ -323,21 +335,30 @@
     total = forward(late, total)
     total = near(2, total)
 
-    field, table, powers, crosses = pl.pallas_call(
+    total, table, powers, crosses = pl.pallas_call(
         functools.partial(field_kernel, 3, region),
         out_shape=(
-            pltpu.VMEM(panels.shape, F32),
+            pltpu.VMEM(image_shape, F32),
             pltpu.VMEM(table_shape, F32),
             pltpu.VMEM(power_shape, F32),
             pltpu.VMEM(power_shape, F32),
         ),
         in_specs=[SMEM_SPEC] + [VMEM_SPEC] * 6,
         out_specs=(VMEM_SPEC,) * 4,
-        scratch_shapes=[pltpu.VMEM(image_shape, F32)],
         compiler_params=params(),
         cost_estimate=cost(SMALL),
         name="field_stage",
     )(plan, arrived[late + 1], panels, tiles, total, basis, spread)
+
+    field = pl.pallas_call(
+        write_kernel,
+        out_shape=jax.ShapeDtypeStruct(panels.shape, F32),
+        in_specs=[VMEM_SPEC] * 2,
+        out_specs=VMEM_SPEC,
+        compiler_params=params(),
+        cost_estimate=cost(SMALL),
+        name="write_stage",
+    )(panels, total)
 
     tables = [table]
     for distance in range(group_count - 1, 0, -1):

time: 25.5 us -> 25.4 us (level)
  local copies, waits for them, and re-layouts: 1.64 us -> 0.94 us
  Pallas kernels: 5.81 us -> 6.34 us
    pallas_call x0 -> x1, Pallas kernels: none -> 0.74 us  [shards(): pl.pallas_call(write_kernel, out_shape=jax.ShapeDtypeStruct(panels.shape,...]
    unnamed x21 -> x20, local copies, waits for them, and re-layouts: 1.64 us -> 0.94 us
  transfers between devices with their start and end apart: 10 -> 10, of which waited for: 6 -> 5; matrix products, arithmetic and copies ran while one was open for 3% -> 0% of each run, Pallas kernels for 16% -> 19%
where the time goes in v11:
time: 25.4 us; the launch traced here: 25 us
  starting transfers between devices  9.7 us (38%)
  waiting for transfers between devices  7.22 us (28%)
  Pallas kernels  6.34 us (25%)
  local copies, waits for them, and re-layouts  0.94 us (4%)
  between operations  0.82 us (3%)
    ppermute x10, starting transfers between devices, exchange(): return lax.ppermute(values, axis, pairs)  9.7 us
    ppermute x10, waiting for transfers between devices, exchange(): return lax.ppermute(values, axis, pairs)  7.22 us
    pallas_call x3, Pallas kernels, near(): pl.pallas_call(functools.partial(near_kernel, stage, region, len(sources)...  2.62 us
    pallas_call x1, Pallas kernels, shards(): pl.pallas_call(functools.partial(plan_kernel, stages, region, freq_count)...  1.36 us
    unnamed x20, local copies, waits for them, and re-layouts  0.94 us
    pallas_call x1, Pallas kernels, shards(): pl.pallas_call(functools.partial(gradient_kernel, len(tables)), out_shape...  0.91 us
    pallas_call x1, Pallas kernels, shards(): pl.pallas_call(write_kernel, out_shape=jax.ShapeDtypeStruct(panels.shape,...  0.74 us
    pallas_call x1, Pallas kernels, shards(): pl.pallas_call(functools.partial(field_kernel, 3, region), out_shape=(plt...  0.7 us
  transfers between devices with their start and end apart: 10, of which 5 were waited for; matrix products, arithmetic and copies ran while one was open for 0% of the time, Pallas kernels for 19%

profile of v11, /device:TPU:0, one launch (start us, length us, event | category | flops | bytes accessed | tf_op | source)
XLA Modules:
  0.0 25.0 jit_solution(1962835050226369667)
XLA Ops:
  0.6 0.0 copy-start.9
  0.6 0.0 copy-start
  0.7 4.1 %collective-permute-start.1 = (bf16[8,32,256]{2,1,0:T(8,128)(2,1)}, bf16[8,32,256]{2,1,0:T(8,128)(2,1)S(1)}, u32[]{:S(2)}, u32[]{:S(2)}) collective-permute-start(bf16[8,32,256]{2,1,0:T(8,128)(2,1)} %panels.3), channel_id=1, source_target_pairs={{0,16},{4,20},{8,24},{12,28},{16,0},{20,4},{24,8},{28,12},{1,17},{... | collective-permute-start | bytes 393224 | tf_op jit(solution)/shard_map/ppermute | solution.py:244
  4.8 1.6 %collective-permute-start.2 = (bf16[8,32,256]{2,1,0:T(8,128)(2,1)}, bf16[8,32,256]{2,1,0:T(8,128)(2,1)S(1)}, u32[]{:S(2)}, u32[]{:S(2)}) collective-permute-start(bf16[8,32,256]{2,1,0:T(8,128)(2,1)} %panels.3), channel_id=1, source_target_pairs={{0,8},{4,12},{8,0},{12,4},{16,24},{20,28},{24,16},{28,20},{1,9},{5... | collective-permute-start | bytes 393224 | tf_op jit(solution)/shard_map/ppermute | solution.py:244
  6.4 0.0 collective-permute-start.3
  6.4 0.0 collective-permute-start
  6.4 1.4 %plan_stage.1 = (s32[1024]{0:T(1024)S(4)}, f32[9,32,512]{2,1,0:T(8,128)S(1)}, bf16[128,256]{1,0:T(8,128)(2,1)S(1)}, bf16[256,128]{1,0:T(8,128)(2,1)S(1)}) custom-call(s32[8]{0:T(128)S(1)} %copy-done.9, s32[48]{0:T(128)S(1)} %copy-done.5, s32[48]{0:T(128)S(1)} %copy-done.6, s32[8]{0:T(128)S(1)} %bitcast.3, s32[8]{0:T(128)S(1)} %copy-done.8, ...), custom_call_target="tpu_custom_call" | custom-call | bytes 25165824 | tf_op jit(solution)/shard_map/plan_stage/pallas_call | solution.py:287
  7.8 0.0 copy-start.1
  7.8 0.9 %copy-done.1 = bf16[8,32,256]{2,1,0:T(8,128)(2,1)S(1)} copy-done((bf16[8,32,256]{2,1,0:T(8,128)(2,1)S(1)}, bf16[8,32,256]{2,1,0:T(8,128)(2,1)}, u32[]{:S(2)}) %copy-start.1) | copy-done | bytes 131096
  8.7 0.3 %near_stage.3.refs_4_ = f32[9,32,512]{2,1,0:T(8,128)S(1)} custom-call(s32[1024]{0:T(1024)S(4)} %get-tuple-element.21.plan, bf16[8,32,256]{2,1,0:T(8,128)(2,1)S(1)} %copy-done.1, bf16[48,256,512]{2,1,0:T(8,128)(2,1)S(1)} %copy-done, f32[9,32,512]{2,1,0:T(8,128)S(1)} %get-tuple-element.23.refs_2_), custom_call_target="tpu_custom_call" | custom-call | bytes 65536 | tf_op jit(solution)/shard_map/near_stage/pallas_call | solution.py:305
  9.1 0.0 copy-start.2
  9.1 3.7 %collective-permute-done.1.refs_0_ = bf16[8,32,256]{2,1,0:T(8,128)(2,1)S(1)} collective-permute-done((bf16[8,32,256]{2,1,0:T(8,128)(2,1)}, bf16[8,32,256]{2,1,0:T(8,128)(2,1)S(1)}, u32[]{:S(2)}, u32[]{:S(2)}) %collective-permute-start.1) | collective-permute-done | bytes 131104 | tf_op jit(solution)/shard_map/ppermute | solution.py:244
  12.7 0.0 collective-permute-done.2.refs_1_
  12.7 0.0 collective-permute-start.6
  12.7 0.5 %collective-permute-start.5 = (bf16[8,32,256]{2,1,0:T(8,128)(2,1)S(1)}, bf16[8,32,256]{2,1,0:T(8,128)(2,1)S(1)}, u32[]{:S(2)}, u32[]{:S(2)}) collective-permute-start(bf16[8,32,256]{2,1,0:T(8,128)(2,1)S(1)} %collective-permute-done.1.refs_0_), channel_id=1, source_target_pairs={{0,4},{4,0},{8,12},{12,8},{16,20},{20,16},{24,28},{28,24},{1,5},{5... | collective-permute-start | bytes 393224 | tf_op jit(solution)/shard_map/ppermute | solution.py:244
  13.3 0.0 collective-permute-done.3.refs_2_
  13.3 0.9 %near_stage.4.refs_4_ = f32[9,32,512]{2,1,0:T(8,128)S(1)} custom-call(s32[1024]{0:T(1024)S(4)} %get-tuple-element.21.plan, bf16[8,32,256]{2,1,0:T(8,128)(2,1)S(1)} %collective-permute-done.1.refs_0_, bf16[8,32,256]{2,1,0:T(8,128)(2,1)S(1)} %collective-permute-done.2.refs_1_, bf16[8,32,256]{2,1,0:T(8,128)(2,1)S(1)} %collective-permute-done.3.refs_2_, ...), custom_call_target="tpu_custom_call" | custom-call | bytes 65536 | tf_op jit(solution)/shard_map/near_stage/pallas_call | solution.py:305
  14.2 1.2 %collective-permute-done.refs_2_ = bf16[8,32,256]{2,1,0:T(8,128)(2,1)S(1)} collective-permute-done((bf16[8,32,256]{2,1,0:T(8,128)(2,1)}, bf16[8,32,256]{2,1,0:T(8,128)(2,1)S(1)}, u32[]{:S(2)}, u32[]{:S(2)}) %collective-permute-start) | collective-permute-done | bytes 131104 | tf_op jit(solution)/shard_map/ppermute | solution.py:244
  15.3 0.0 collective-permute-start.4
  15.4 0.0 collective-permute-done.6.refs_1_
  15.4 0.0 collective-permute-done.5.refs_0_
  15.4 1.4 %near_stage.5.start = f32[9,32,512]{2,1,0:T(8,128)S(1)} custom-call(s32[1024]{0:T(1024)S(4)} %get-tuple-element.21.plan, bf16[8,32,256]{2,1,0:T(8,128)(2,1)S(1)} %collective-permute-done.5.refs_0_, bf16[8,32,256]{2,1,0:T(8,128)(2,1)S(1)} %collective-permute-done.6.refs_1_, bf16[8,32,256]{2,1,0:T(8,128)(2,1)S(1)} %collective-permute-done.refs_2_, ...), custom_call_target="tpu_custom_call" | custom-call | bytes 65536 | tf_op jit(solution)/shard_map/near_stage/pallas_call | solution.py:305
  16.8 0.0 collective-permute-done.4.source
  16.8 0.7 %field_stage.1 = (f32[9,32,512]{2,1,0:T(8,128)S(1)}, f32[8,256]{1,0:T(8,128)S(1)}, f32[128,256]{1,0:T(8,128)S(1)}, f32[128,256]{1,0:T(8,128)S(1)}) custom-call(s32[1024]{0:T(1024)S(4)} %get-tuple-element.21.plan, bf16[8,32,256]{2,1,0:T(8,128)(2,1)S(1)} %collective-permute-done.4.source, bf16[8,32,256]{2,1,0:T(8,128)(2,1)S(1)} %copy-done.2, ...), custom_call_target="tpu_custom_call" | custom-call | bytes 65536 | tf_op jit(solution)/shard_map/field_stage/pallas_call | solution.py:338
  17.5 2.7 %collective-permute-start.7 = (f32[8,256]{1,0:T(8,128)S(1)}, f32[8,256]{1,0:T(8,128)S(1)}, u32[]{:S(2)}, u32[]{:S(2)}) collective-permute-start(f32[8,256]{1,0:T(8,128)S(1)} %get-tuple-element.34.refs_0_), channel_id=1, source_target_pairs={{0,3},{1,2},{2,1},{3,0},{4,7},{5,6},{6,5},{7,4},{8,11},{9,10},{10,... | collective-permute-start | bytes 24584 | tf_op jit(solution)/shard_map/ppermute | solution.py:244
  20.2 0.2 collective-permute-start.8
  20.5 0.5 %collective-permute-start.9 = (f32[8,256]{1,0:T(8,128)S(1)}, f32[8,256]{1,0:T(8,128)S(1)}, u32[]{:S(2)}, u32[]{:S(2)}) collective-permute-start(f32[8,256]{1,0:T(8,128)S(1)} %get-tuple-element.34.refs_0_), channel_id=1, source_target_pairs={{0,1},{1,0},{2,3},{3,2},{4,5},{5,4},{6,7},{7,6},{8,9},{9,8},{10,11... | collective-permute-start | bytes 24584 | tf_op jit(solution)/shard_map/ppermute | solution.py:244
  21.0 0.7 %write_stage.1 = f32[8,32,256]{2,1,0:T(8,128)} custom-call(bf16[8,32,256]{2,1,0:T(8,128)(2,1)S(1)} %copy-done.2, f32[9,32,512]{2,1,0:T(8,128)S(1)} %get-tuple-element.33.total), custom_call_target="tpu_custom_call" | custom-call | bytes 65536 | tf_op jit(solution)/shard_map/write_stage/pallas_call | solution.py:353
  21.7 0.3 %collective-permute-done.7.refs_1_ = f32[8,256]{1,0:T(8,128)S(1)} collective-permute-done((f32[8,256]{1,0:T(8,128)S(1)}, f32[8,256]{1,0:T(8,128)S(1)}, u32[]{:S(2)}, u32[]{:S(2)}) %collective-permute-start.7) | collective-permute-done | bytes 8224 | tf_op jit(solution)/shard_map/ppermute | solution.py:244
  22.1 1.8 %collective-permute-done.8.refs_2_ = f32[8,256]{1,0:T(8,128)S(1)} collective-permute-done((f32[8,256]{1,0:T(8,128)S(1)}, f32[8,256]{1,0:T(8,128)S(1)}, u32[]{:S(2)}, u32[]{:S(2)}) %collective-permute-start.8) | collective-permute-done | bytes 8224 | tf_op jit(solution)/shard_map/ppermute | solution.py:244
  23.9 0.2 collective-permute-done.9.refs_3_
  24.1 0.9 %gradient_stage.1 = f32[8,256]{1,0:T(8,128)} custom-call(f32[8,256]{1,0:T(8,128)S(1)} %get-tuple-element.34.refs_0_, f32[8,256]{1,0:T(8,128)S(1)} %collective-permute-done.7.refs_1_, f32[8,256]{1,0:T(8,128)S(1)} %collective-permute-done.8.refs_2_, f32[8,256]{1,0:T(8,128)S(1)} %collective-permute-done.9.refs_3_, f32[64,256]{1,0:T(8,128)S(1)} %basis_stage.1.basis.refs_4_, ...), custom_call_target="tpu_custom_call" | custom-call | bytes 65536 | tf_op jit(solution)/shard_map/gradient_stage/pallas_call | solution.py:367
  (17 shorter events, 0.0 us)
Async XLA Ops:
  0.6 5.8 %copy-start.9 = (s32[8]{0:T(128)S(1)}, s32[8]{0:T(128)}, u32[]{:S(2)}) copy-start(s32[8]{0:T(128)} %constant.2.clone.table) | copy-start | bytes 100
  0.6 7.2 %copy-start = (bf16[48,256,512]{2,1,0:T(8,128)(2,1)S(1)}, bf16[48,256,512]{2,1,0:T(8,128)(2,1)}, u32[]{:S(2)}) copy-start(bf16[48,256,512]{2,1,0:T(8,128)(2,1)} %tiles.3) | copy-start | bytes 37748740
  0.7 5.7 %copy-start.7 = (s32[8,1]{0,1:T(1,128)S(1)}, s32[8,1]{0,1:T(1,128)}, u32[]{:S(2)}) copy-start(s32[8,1]{0,1:T(1,128)} %param.15) | copy-start | bytes 100
  0.7 5.7 %copy-start.6 = (s32[48]{0:T(128)S(1)}, s32[48]{0:T(128)}, u32[]{:S(2)}) copy-start(s32[48]{0:T(128)} %dst.1) | copy-start | bytes 580
  0.7 5.7 %copy-start.5 = (s32[48]{0:T(128)S(1)}, s32[48]{0:T(128)}, u32[]{:S(2)}) copy-start(s32[48]{0:T(128)} %src.1) | copy-start | bytes 580
  0.7 5.7 %copy-start.8 = (s32[8]{0:T(128)S(1)}, s32[8]{0:T(128)}, u32[]{:S(2)}) copy-start(s32[8]{0:T(128)} %slot.1) | copy-start | bytes 100
  0.7 12.0 %collective-permute-start.1 = (bf16[8,32,256]{2,1,0:T(8,128)(2,1)}, bf16[8,32,256]{2,1,0:T(8,128)(2,1)S(1)}, u32[]{:S(2)}, u32[]{:S(2)}) collective-permute-start(bf16[8,32,256]{2,1,0:T(8,128)(2,1)} %panels.3), channel_id=1, source_target_pairs={{0,16},{4,20},{8,24},{12,28},{16,0},{20,4},{24,8},{28,12},{1,17},{... | collective-permute-start | bytes 393224 | tf_op jit(solution)/shard_map/ppermute | solution.py:244
  4.8 7.9 %collective-permute-start.2 = (bf16[8,32,256]{2,1,0:T(8,128)(2,1)}, bf16[8,32,256]{2,1,0:T(8,128)(2,1)S(1)}, u32[]{:S(2)}, u32[]{:S(2)}) collective-permute-start(bf16[8,32,256]{2,1,0:T(8,128)(2,1)} %panels.3), channel_id=1, source_target_pairs={{0,8},{4,12},{8,0},{12,4},{16,24},{20,28},{24,16},{28,20},{1,9},{5... | collective-permute-start | bytes 393224 | tf_op jit(solution)/shard_map/ppermute | solution.py:244
  6.4 6.9 %collective-permute-start.3 = (bf16[8,32,256]{2,1,0:T(8,128)(2,1)}, bf16[8,32,256]{2,1,0:T(8,128)(2,1)S(1)}, u32[]{:S(2)}, u32[]{:S(2)}) collective-permute-start(bf16[8,32,256]{2,1,0:T(8,128)(2,1)} %panels.3), channel_id=1, source_target_pairs={{0,4},{4,0},{8,12},{12,8},{16,20},{20,16},{24,28},{28,24},{1,5},{5... | collective-permute-start | bytes 393224 | tf_op jit(solution)/shard_map/ppermute | solution.py:244
  6.4 9.0 %collective-permute-start = (bf16[8,32,256]{2,1,0:T(8,128)(2,1)}, bf16[8,32,256]{2,1,0:T(8,128)(2,1)S(1)}, u32[]{:S(2)}, u32[]{:S(2)}) collective-permute-start(bf16[8,32,256]{2,1,0:T(8,128)(2,1)} %panels.3), channel_id=1, source_target_pairs={{0,24},{4,28},{8,16},{12,20},{16,8},{20,12},{24,0},{28,4},{1,25},{... | collective-permute-start | bytes 393224 | tf_op jit(solution)/shard_map/ppermute | solution.py:244
  7.8 0.9 %copy-start.1 = (bf16[8,32,256]{2,1,0:T(8,128)(2,1)S(1)}, bf16[8,32,256]{2,1,0:T(8,128)(2,1)}, u32[]{:S(2)}) copy-start(bf16[8,32,256]{2,1,0:T(8,128)(2,1)} %panels.3) | copy-start | bytes 393220
  8.7 6.6 %copy-start.3 = (f32[8,6,256]{2,0,1:T(8,128)S(1)}, f32[8,6,256]{2,0,1:T(8,128)}, u32[]{:S(2)}) copy-start(f32[8,6,256]{2,0,1:T(8,128)} %param.13) | copy-start | bytes 147460
  8.7 6.6 %copy-start.4 = (f32[8,256]{1,0:T(8,128)S(1)}, f32[8,256]{1,0:T(8,128)}, u32[]{:S(2)}) copy-start(f32[8,256]{1,0:T(8,128)} %areas) | copy-start | bytes 24580
  9.1 7.7 %copy-start.2 = (bf16[8,32,256]{2,1,0:T(8,128)(2,1)S(1)}, bf16[8,32,256]{2,1,0:T(8,128)(2,1)}, u32[]{:S(2)}) copy-start(bf16[8,32,256]{2,1,0:T(8,128)(2,1)} %panels.3) | copy-start | bytes 393220
  12.7 2.6 %collective-permute-start.6 = (bf16[8,32,256]{2,1,0:T(8,128)(2,1)S(1)}, bf16[8,32,256]{2,1,0:T(8,128)(2,1)S(1)}, u32[]{:S(2)}, u32[]{:S(2)}) collective-permute-start(bf16[8,32,256]{2,1,0:T(8,128)(2,1)S(1)} %collective-permute-done.2.refs_1_), channel_id=1, source_target_pairs={{0,4},{4,0},{8,12},{12,8},{16,20},{20,16},{24,28},{28,24},{1,5},{5... | collective-permute-start | bytes 393224 | tf_op jit(solution)/shard_map/ppermute | solution.py:244
  12.7 2.6 %collective-permute-start.5 = (bf16[8,32,256]{2,1,0:T(8,128)(2,1)S(1)}, bf16[8,32,256]{2,1,0:T(8,128)(2,1)S(1)}, u32[]{:S(2)}, u32[]{:S(2)}) collective-permute-start(bf16[8,32,256]{2,1,0:T(8,128)(2,1)S(1)} %collective-permute-done.1.refs_0_), channel_id=1, source_target_pairs={{0,4},{4,0},{8,12},{12,8},{16,20},{20,16},{24,28},{28,24},{1,5},{5... | collective-permute-start | bytes 393224 | tf_op jit(solution)/shard_map/ppermute | solution.py:244
  15.3 1.4 %collective-permute-start.4 = (bf16[8,32,256]{2,1,0:T(8,128)(2,1)S(1)}, bf16[8,32,256]{2,1,0:T(8,128)(2,1)S(1)}, u32[]{:S(2)}, u32[]{:S(2)}) collective-permute-start(bf16[8,32,256]{2,1,0:T(8,128)(2,1)S(1)} %collective-permute-done.refs_2_), channel_id=1, source_target_pairs={{0,4},{4,0},{8,12},{12,8},{16,20},{20,16},{24,28},{28,24},{1,5},{5... | collective-permute-start | bytes 393224 | tf_op jit(solution)/shard_map/ppermute | solution.py:244
  17.5 4.6 %collective-permute-start.7 = (f32[8,256]{1,0:T(8,128)S(1)}, f32[8,256]{1,0:T(8,128)S(1)}, u32[]{:S(2)}, u32[]{:S(2)}) collective-permute-start(f32[8,256]{1,0:T(8,128)S(1)} %get-tuple-element.34.refs_0_), channel_id=1, source_target_pairs={{0,3},{1,2},{2,1},{3,0},{4,7},{5,6},{6,5},{7,4},{8,11},{9,10},{10,... | collective-permute-start | bytes 24584 | tf_op jit(solution)/shard_map/ppermute | solution.py:244
  20.2 3.7 %collective-permute-start.8 = (f32[8,256]{1,0:T(8,128)S(1)}, f32[8,256]{1,0:T(8,128)S(1)}, u32[]{:S(2)}, u32[]{:S(2)}) collective-permute-start(f32[8,256]{1,0:T(8,128)S(1)} %get-tuple-element.34.refs_0_), channel_id=1, source_target_pairs={{0,2},{1,3},{2,0},{3,1},{4,6},{5,7},{6,4},{7,5},{8,10},{9,11},{10,... | collective-permute-start | bytes 24584 | tf_op jit(solution)/shard_map/ppermute | solution.py:244
  20.5 3.7 %collective-permute-start.9 = (f32[8,256]{1,0:T(8,128)S(1)}, f32[8,256]{1,0:T(8,128)S(1)}, u32[]{:S(2)}, u32[]{:S(2)}) collective-permute-start(f32[8,256]{1,0:T(8,128)S(1)} %get-tuple-element.34.refs_0_), channel_id=1, source_target_pairs={{0,1},{1,0},{2,3},{3,2},{4,5},{5,4},{6,7},{7,6},{8,9},{9,8},{10,11... | collective-permute-start | bytes 24584 | tf_op jit(solution)/shard_map/ppermute | solution.py:244

commit v12 on v11

--- a/solution.py
+++ b/solution.py
@@ -361,7 +361,8 @@
     )(panels, total)
 
     tables = [table]
-    for distance in range(group_count - 1, 0, -1):
+    distances = list(range(1, group_count))
+    for distance in distances[-1:] + distances[:-1]:
         tables.append(exchange(table, "col", distance))
 
     gradient = pl.pallas_call(

time: 25.4 us -> 25.6 us (level)
  the two profiles are of different devices: /device:TPU:0 before, /device:TPU:16 now
where the time goes in v12:
time: 25.6 us; the launch traced here: 25.2 us
  waiting for transfers between devices  9.39 us (37%)
  starting transfers between devices  7.58 us (30%)
  Pallas kernels  6.54 us (26%)
  local copies, waits for them, and re-layouts  0.94 us (4%)
  between operations  0.8 us (3%)
    ppermute x10, waiting for transfers between devices, exchange(): return lax.ppermute(values, axis, pairs)  9.39 us
    ppermute x10, starting transfers between devices, exchange(): return lax.ppermute(values, axis, pairs)  7.58 us
    pallas_call x3, Pallas kernels, near(): pl.pallas_call(functools.partial(near_kernel, stage, region, len(sources)...  2.63 us
    pallas_call x1, Pallas kernels, shards(): pl.pallas_call(functools.partial(plan_kernel, stages, region, freq_count)...  1.36 us
    unnamed x20, local copies, waits for them, and re-layouts  0.94 us
    pallas_call x1, Pallas kernels, shards(): pl.pallas_call(functools.partial(gradient_kernel, len(tables)), out_shape...  0.91 us
    pallas_call x1, Pallas kernels, shards(): pl.pallas_call(functools.partial(field_kernel, 3, region), out_shape=(plt...  0.89 us
    pallas_call x1, Pallas kernels, shards(): pl.pallas_call(write_kernel, out_shape=jax.ShapeDtypeStruct(panels.shape,...  0.74 us
  transfers between devices with their start and end apart: 10, of which 7 were waited for; matrix products, arithmetic and copies ran while one was open for 0% of the time, Pallas kernels for 19%

profile of v12, /device:TPU:16, one launch (start us, length us, event | category | flops | bytes accessed | tf_op | source)
XLA Modules:
  0.0 25.2 jit_solution(10247814991896576201)
XLA Ops:
  0.6 0.0 copy-start.9
  0.7 0.1 collective-permute-start.1
  0.8 1.9 %collective-permute-start.2 = (bf16[8,32,256]{2,1,0:T(8,128)(2,1)}, bf16[8,32,256]{2,1,0:T(8,128)(2,1)S(1)}, u32[]{:S(2)}, u32[]{:S(2)}) collective-permute-start(bf16[8,32,256]{2,1,0:T(8,128)(2,1)} %panels.3), channel_id=1, source_target_pairs={{0,8},{4,12},{8,0},{12,4},{16,24},{20,28},{24,16},{28,20},{1,9},{5... | collective-permute-start | bytes 393224 | tf_op jit(solution)/shard_map/ppermute | solution.py:244
  2.7 0.0 collective-permute-start.3
  2.7 1.6 %collective-permute-start = (bf16[8,32,256]{2,1,0:T(8,128)(2,1)}, bf16[8,32,256]{2,1,0:T(8,128)(2,1)S(1)}, u32[]{:S(2)}, u32[]{:S(2)}) collective-permute-start(bf16[8,32,256]{2,1,0:T(8,128)(2,1)} %panels.3), channel_id=1, source_target_pairs={{0,24},{4,28},{8,16},{12,20},{16,8},{20,12},{24,0},{28,4},{1,25},{... | collective-permute-start | bytes 393224 | tf_op jit(solution)/shard_map/ppermute | solution.py:244
  4.3 0.0 copy-done.5
  4.3 1.4 %plan_stage.1 = (s32[1024]{0:T(1024)S(4)}, f32[9,32,512]{2,1,0:T(8,128)S(1)}, bf16[128,256]{1,0:T(8,128)(2,1)S(1)}, bf16[256,128]{1,0:T(8,128)(2,1)S(1)}) custom-call(s32[8]{0:T(128)S(1)} %copy-done.9, s32[48]{0:T(128)S(1)} %copy-done.5, s32[48]{0:T(128)S(1)} %copy-done.6, s32[8]{0:T(128)S(1)} %bitcast.3, s32[8]{0:T(128)S(1)} %copy-done.8, ...), custom_call_target="tpu_custom_call" | custom-call | bytes 25165824 | tf_op jit(solution)/shard_map/plan_stage/pallas_call | solution.py:287
  5.7 0.0 copy-start.1
  5.7 0.9 %copy-done.1 = bf16[8,32,256]{2,1,0:T(8,128)(2,1)S(1)} copy-done((bf16[8,32,256]{2,1,0:T(8,128)(2,1)S(1)}, bf16[8,32,256]{2,1,0:T(8,128)(2,1)}, u32[]{:S(2)}) %copy-start.1) | copy-done | bytes 131096
  6.6 0.3 %near_stage.3.refs_4_ = f32[9,32,512]{2,1,0:T(8,128)S(1)} custom-call(s32[1024]{0:T(1024)S(4)} %get-tuple-element.21.plan, bf16[8,32,256]{2,1,0:T(8,128)(2,1)S(1)} %copy-done.1, bf16[48,256,512]{2,1,0:T(8,128)(2,1)S(1)} %copy-done, f32[9,32,512]{2,1,0:T(8,128)S(1)} %get-tuple-element.23.refs_2_), custom_call_target="tpu_custom_call" | custom-call | bytes 65536 | tf_op jit(solution)/shard_map/near_stage/pallas_call | solution.py:305
  6.9 0.0 copy-start.2
  6.9 1.3 %collective-permute-done.1.refs_0_ = bf16[8,32,256]{2,1,0:T(8,128)(2,1)S(1)} collective-permute-done((bf16[8,32,256]{2,1,0:T(8,128)(2,1)}, bf16[8,32,256]{2,1,0:T(8,128)(2,1)S(1)}, u32[]{:S(2)}, u32[]{:S(2)}) %collective-permute-start.1) | collective-permute-done | bytes 131104 | tf_op jit(solution)/shard_map/ppermute | solution.py:244
  8.3 1.6 %collective-permute-done.2.refs_1_ = bf16[8,32,256]{2,1,0:T(8,128)(2,1)S(1)} collective-permute-done((bf16[8,32,256]{2,1,0:T(8,128)(2,1)}, bf16[8,32,256]{2,1,0:T(8,128)(2,1)S(1)}, u32[]{:S(2)}, u32[]{:S(2)}) %collective-permute-start.2) | collective-permute-done | bytes 131104 | tf_op jit(solution)/shard_map/ppermute | solution.py:244
  9.8 0.0 collective-permute-start.6
  9.8 0.5 %collective-permute-start.5 = (bf16[8,32,256]{2,1,0:T(8,128)(2,1)S(1)}, bf16[8,32,256]{2,1,0:T(8,128)(2,1)S(1)}, u32[]{:S(2)}, u32[]{:S(2)}) collective-permute-start(bf16[8,32,256]{2,1,0:T(8,128)(2,1)S(1)} %collective-permute-done.1.refs_0_), channel_id=1, source_target_pairs={{0,4},{4,0},{8,12},{12,8},{16,20},{20,16},{24,28},{28,24},{1,5},{5... | collective-permute-start | bytes 393224 | tf_op jit(solution)/shard_map/ppermute | solution.py:244
  10.3 0.0 collective-permute-done.3.refs_2_
  10.3 1.2 %near_stage.4.refs_4_ = f32[9,32,512]{2,1,0:T(8,128)S(1)} custom-call(s32[1024]{0:T(1024)S(4)} %get-tuple-element.21.plan, bf16[8,32,256]{2,1,0:T(8,128)(2,1)S(1)} %collective-permute-done.1.refs_0_, bf16[8,32,256]{2,1,0:T(8,128)(2,1)S(1)} %collective-permute-done.2.refs_1_, bf16[8,32,256]{2,1,0:T(8,128)(2,1)S(1)} %collective-permute-done.3.refs_2_, ...), custom_call_target="tpu_custom_call" | custom-call | bytes 65536 | tf_op jit(solution)/shard_map/near_stage/pallas_call | solution.py:305
  11.5 4.0 %collective-permute-done.refs_2_ = bf16[8,32,256]{2,1,0:T(8,128)(2,1)S(1)} collective-permute-done((bf16[8,32,256]{2,1,0:T(8,128)(2,1)}, bf16[8,32,256]{2,1,0:T(8,128)(2,1)S(1)}, u32[]{:S(2)}, u32[]{:S(2)}) %collective-permute-start) | collective-permute-done | bytes 131104 | tf_op jit(solution)/shard_map/ppermute | solution.py:244
  15.5 0.0 collective-permute-start.4
  15.6 0.0 collective-permute-done.6.refs_1_
  15.6 0.0 collective-permute-done.5.refs_0_
  15.6 1.1 %near_stage.5.start = f32[9,32,512]{2,1,0:T(8,128)S(1)} custom-call(s32[1024]{0:T(1024)S(4)} %get-tuple-element.21.plan, bf16[8,32,256]{2,1,0:T(8,128)(2,1)S(1)} %collective-permute-done.5.refs_0_, bf16[8,32,256]{2,1,0:T(8,128)(2,1)S(1)} %collective-permute-done.6.refs_1_, bf16[8,32,256]{2,1,0:T(8,128)(2,1)S(1)} %collective-permute-done.refs_2_, ...), custom_call_target="tpu_custom_call" | custom-call | bytes 65536 | tf_op jit(solution)/shard_map/near_stage/pallas_call | solution.py:305
  16.7 0.2 collective-permute-done.4.source
  16.9 0.9 %field_stage.1 = (f32[9,32,512]{2,1,0:T(8,128)S(1)}, f32[8,256]{1,0:T(8,128)S(1)}, f32[128,256]{1,0:T(8,128)S(1)}, f32[128,256]{1,0:T(8,128)S(1)}) custom-call(s32[1024]{0:T(1024)S(4)} %get-tuple-element.21.plan, bf16[8,32,256]{2,1,0:T(8,128)(2,1)S(1)} %collective-permute-done.4.source, bf16[8,32,256]{2,1,0:T(8,128)(2,1)S(1)} %copy-done.2, ...), custom_call_target="tpu_custom_call" | custom-call | bytes 65536 | tf_op jit(solution)/shard_map/field_stage/pallas_call | solution.py:338
  17.8 2.5 %collective-permute-start.7 = (f32[8,256]{1,0:T(8,128)S(1)}, f32[8,256]{1,0:T(8,128)S(1)}, u32[]{:S(2)}, u32[]{:S(2)}) collective-permute-start(f32[8,256]{1,0:T(8,128)S(1)} %get-tuple-element.34.refs_0_), channel_id=1, source_target_pairs={{0,3},{1,2},{2,1},{3,0},{4,7},{5,6},{6,5},{7,4},{8,11},{9,10},{10,... | collective-permute-start | bytes 24584 | tf_op jit(solution)/shard_map/ppermute | solution.py:244
  20.2 0.4 %collective-permute-start.8 = (f32[8,256]{1,0:T(8,128)S(1)}, f32[8,256]{1,0:T(8,128)S(1)}, u32[]{:S(2)}, u32[]{:S(2)}) collective-permute-start(f32[8,256]{1,0:T(8,128)S(1)} %get-tuple-element.34.refs_0_), channel_id=1, source_target_pairs={{0,1},{1,0},{2,3},{3,2},{4,5},{5,4},{6,7},{7,6},{8,9},{9,8},{10,11... | collective-permute-start | bytes 24584 | tf_op jit(solution)/shard_map/ppermute | solution.py:244
  20.7 0.6 %collective-permute-start.9 = (f32[8,256]{1,0:T(8,128)S(1)}, f32[8,256]{1,0:T(8,128)S(1)}, u32[]{:S(2)}, u32[]{:S(2)}) collective-permute-start(f32[8,256]{1,0:T(8,128)S(1)} %get-tuple-element.34.refs_0_), channel_id=1, source_target_pairs={{0,2},{1,3},{2,0},{3,1},{4,6},{5,7},{6,4},{7,5},{8,10},{9,11},{10,... | collective-permute-start | bytes 24584 | tf_op jit(solution)/shard_map/ppermute | solution.py:244
  21.3 0.7 %write_stage.1 = f32[8,32,256]{2,1,0:T(8,128)} custom-call(bf16[8,32,256]{2,1,0:T(8,128)(2,1)S(1)} %copy-done.2, f32[9,32,512]{2,1,0:T(8,128)S(1)} %get-tuple-element.33.total), custom_call_target="tpu_custom_call" | custom-call | bytes 65536 | tf_op jit(solution)/shard_map/write_stage/pallas_call | solution.py:353
  22.0 0.3 %collective-permute-done.7.refs_1_ = f32[8,256]{1,0:T(8,128)S(1)} collective-permute-done((f32[8,256]{1,0:T(8,128)S(1)}, f32[8,256]{1,0:T(8,128)S(1)}, u32[]{:S(2)}, u32[]{:S(2)}) %collective-permute-start.7) | collective-permute-done | bytes 8224 | tf_op jit(solution)/shard_map/ppermute | solution.py:244
  22.3 1.5 %collective-permute-done.8.refs_2_ = f32[8,256]{1,0:T(8,128)S(1)} collective-permute-done((f32[8,256]{1,0:T(8,128)S(1)}, f32[8,256]{1,0:T(8,128)S(1)}, u32[]{:S(2)}, u32[]{:S(2)}) %collective-permute-start.8) | collective-permute-done | bytes 8224 | tf_op jit(solution)/shard_map/ppermute | solution.py:244
  23.9 0.4 %collective-permute-done.9.refs_3_ = f32[8,256]{1,0:T(8,128)S(1)} collective-permute-done((f32[8,256]{1,0:T(8,128)S(1)}, f32[8,256]{1,0:T(8,128)S(1)}, u32[]{:S(2)}, u32[]{:S(2)}) %collective-permute-start.9) | collective-permute-done | bytes 8224 | tf_op jit(solution)/shard_map/ppermute | solution.py:244
  24.3 0.9 %gradient_stage.1 = f32[8,256]{1,0:T(8,128)} custom-call(f32[8,256]{1,0:T(8,128)S(1)} %get-tuple-element.34.refs_0_, f32[8,256]{1,0:T(8,128)S(1)} %collective-permute-done.7.refs_1_, f32[8,256]{1,0:T(8,128)S(1)} %collective-permute-done.8.refs_2_, f32[8,256]{1,0:T(8,128)S(1)} %collective-permute-done.9.refs_3_, f32[64,256]{1,0:T(8,128)S(1)} %basis_stage.1.basis.refs_4_, ...), custom_call_target="tpu_custom_call" | custom-call | bytes 65536 | tf_op jit(solution)/shard_map/gradient_stage/pallas_call | solution.py:368
  (17 shorter events, 0.0 us)
Async XLA Ops:
  0.6 3.6 %copy-start.9 = (s32[8]{0:T(128)S(1)}, s32[8]{0:T(128)}, u32[]{:S(2)}) copy-start(s32[8]{0:T(128)} %constant.2.clone.table) | copy-start | bytes 100
  0.6 5.0 %copy-start = (bf16[48,256,512]{2,1,0:T(8,128)(2,1)S(1)}, bf16[48,256,512]{2,1,0:T(8,128)(2,1)}, u32[]{:S(2)}) copy-start(bf16[48,256,512]{2,1,0:T(8,128)(2,1)} %tiles.3) | copy-start | bytes 37748740
  0.7 3.6 %copy-start.7 = (s32[8,1]{0,1:T(1,128)S(1)}, s32[8,1]{0,1:T(1,128)}, u32[]{:S(2)}) copy-start(s32[8,1]{0,1:T(1,128)} %param.15) | copy-start | bytes 100
  0.7 3.6 %copy-start.6 = (s32[48]{0:T(128)S(1)}, s32[48]{0:T(128)}, u32[]{:S(2)}) copy-start(s32[48]{0:T(128)} %dst.1) | copy-start | bytes 580
  0.7 3.6 %copy-start.5 = (s32[48]{0:T(128)S(1)}, s32[48]{0:T(128)}, u32[]{:S(2)}) copy-start(s32[48]{0:T(128)} %src.1) | copy-start | bytes 580
  0.7 3.6 %copy-start.8 = (s32[8]{0:T(128)S(1)}, s32[8]{0:T(128)}, u32[]{:S(2)}) copy-start(s32[8]{0:T(128)} %slot.1) | copy-start | bytes 100
  0.7 7.6 %collective-permute-start.1 = (bf16[8,32,256]{2,1,0:T(8,128)(2,1)}, bf16[8,32,256]{2,1,0:T(8,128)(2,1)S(1)}, u32[]{:S(2)}, u32[]{:S(2)}) collective-permute-start(bf16[8,32,256]{2,1,0:T(8,128)(2,1)} %panels.3), channel_id=1, source_target_pairs={{0,16},{4,20},{8,24},{12,28},{16,0},{20,4},{24,8},{28,12},{1,17},{... | collective-permute-start | bytes 393224 | tf_op jit(solution)/shard_map/ppermute | solution.py:244
  0.8 9.0 %collective-permute-start.2 = (bf16[8,32,256]{2,1,0:T(8,128)(2,1)}, bf16[8,32,256]{2,1,0:T(8,128)(2,1)S(1)}, u32[]{:S(2)}, u32[]{:S(2)}) collective-permute-start(bf16[8,32,256]{2,1,0:T(8,128)(2,1)} %panels.3), channel_id=1, source_target_pairs={{0,8},{4,12},{8,0},{12,4},{16,24},{20,28},{24,16},{28,20},{1,9},{5... | collective-permute-start | bytes 393224 | tf_op jit(solution)/shard_map/ppermute | solution.py:244
  2.7 7.7 %collective-permute-start.3 = (bf16[8,32,256]{2,1,0:T(8,128)(2,1)}, bf16[8,32,256]{2,1,0:T(8,128)(2,1)S(1)}, u32[]{:S(2)}, u32[]{:S(2)}) collective-permute-start(bf16[8,32,256]{2,1,0:T(8,128)(2,1)} %panels.3), channel_id=1, source_target_pairs={{0,4},{4,0},{8,12},{12,8},{16,20},{20,16},{24,28},{28,24},{1,5},{5... | collective-permute-start | bytes 393224 | tf_op jit(solution)/shard_map/ppermute | solution.py:244
  2.7 12.9 %collective-permute-start = (bf16[8,32,256]{2,1,0:T(8,128)(2,1)}, bf16[8,32,256]{2,1,0:T(8,128)(2,1)S(1)}, u32[]{:S(2)}, u32[]{:S(2)}) collective-permute-start(bf16[8,32,256]{2,1,0:T(8,128)(2,1)} %panels.3), channel_id=1, source_target_pairs={{0,24},{4,28},{8,16},{12,20},{16,8},{20,12},{24,0},{28,4},{1,25},{... | collective-permute-start | bytes 393224 | tf_op jit(solution)/shard_map/ppermute | solution.py:244
  5.7 0.9 %copy-start.1 = (bf16[8,32,256]{2,1,0:T(8,128)(2,1)S(1)}, bf16[8,32,256]{2,1,0:T(8,128)(2,1)}, u32[]{:S(2)}) copy-start(bf16[8,32,256]{2,1,0:T(8,128)(2,1)} %panels.3) | copy-start | bytes 393220
  6.6 9.0 %copy-start.3 = (f32[8,6,256]{2,0,1:T(8,128)S(1)}, f32[8,6,256]{2,0,1:T(8,128)}, u32[]{:S(2)}) copy-start(f32[8,6,256]{2,0,1:T(8,128)} %param.13) | copy-start | bytes 147460
  6.6 9.0 %copy-start.4 = (f32[8,256]{1,0:T(8,128)S(1)}, f32[8,256]{1,0:T(8,128)}, u32[]{:S(2)}) copy-start(f32[8,256]{1,0:T(8,128)} %areas) | copy-start | bytes 24580
  6.9 10.0 %copy-start.2 = (bf16[8,32,256]{2,1,0:T(8,128)(2,1)S(1)}, bf16[8,32,256]{2,1,0:T(8,128)(2,1)}, u32[]{:S(2)}) copy-start(bf16[8,32,256]{2,1,0:T(8,128)(2,1)} %panels.3) | copy-start | bytes 393220
  9.8 5.8 %collective-permute-start.6 = (bf16[8,32,256]{2,1,0:T(8,128)(2,1)S(1)}, bf16[8,32,256]{2,1,0:T(8,128)(2,1)S(1)}, u32[]{:S(2)}, u32[]{:S(2)}) collective-permute-start(bf16[8,32,256]{2,1,0:T(8,128)(2,1)S(1)} %collective-permute-done.2.refs_1_), channel_id=1, source_target_pairs={{0,4},{4,0},{8,12},{12,8},{16,20},{20,16},{24,28},{28,24},{1,5},{5... | collective-permute-start | bytes 393224 | tf_op jit(solution)/shard_map/ppermute | solution.py:244
  9.8 5.8 %collective-permute-start.5 = (bf16[8,32,256]{2,1,0:T(8,128)(2,1)S(1)}, bf16[8,32,256]{2,1,0:T(8,128)(2,1)S(1)}, u32[]{:S(2)}, u32[]{:S(2)}) collective-permute-start(bf16[8,32,256]{2,1,0:T(8,128)(2,1)S(1)} %collective-permute-done.1.refs_0_), channel_id=1, source_target_pairs={{0,4},{4,0},{8,12},{12,8},{16,20},{20,16},{24,28},{28,24},{1,5},{5... | collective-permute-start | bytes 393224 | tf_op jit(solution)/shard_map/ppermute | solution.py:244
  15.5 1.3 %collective-permute-start.4 = (bf16[8,32,256]{2,1,0:T(8,128)(2,1)S(1)}, bf16[8,32,256]{2,1,0:T(8,128)(2,1)S(1)}, u32[]{:S(2)}, u32[]{:S(2)}) collective-permute-start(bf16[8,32,256]{2,1,0:T(8,128)(2,1)S(1)} %collective-permute-done.refs_2_), channel_id=1, source_target_pairs={{0,4},{4,0},{8,12},{12,8},{16,20},{20,16},{24,28},{28,24},{1,5},{5... | collective-permute-start | bytes 393224 | tf_op jit(solution)/shard_map/ppermute | solution.py:244
  17.8 4.6 %collective-permute-start.7 = (f32[8,256]{1,0:T(8,128)S(1)}, f32[8,256]{1,0:T(8,128)S(1)}, u32[]{:S(2)}, u32[]{:S(2)}) collective-permute-start(f32[8,256]{1,0:T(8,128)S(1)} %get-tuple-element.34.refs_0_), channel_id=1, source_target_pairs={{0,3},{1,2},{2,1},{3,0},{4,7},{5,6},{6,5},{7,4},{8,11},{9,10},{10,... | collective-permute-start | bytes 24584 | tf_op jit(solution)/shard_map/ppermute | solution.py:244
  20.2 3.7 %collective-permute-start.8 = (f32[8,256]{1,0:T(8,128)S(1)}, f32[8,256]{1,0:T(8,128)S(1)}, u32[]{:S(2)}, u32[]{:S(2)}) collective-permute-start(f32[8,256]{1,0:T(8,128)S(1)} %get-tuple-element.34.refs_0_), channel_id=1, source_target_pairs={{0,1},{1,0},{2,3},{3,2},{4,5},{5,4},{6,7},{7,6},{8,9},{9,8},{10,11... | collective-permute-start | bytes 24584 | tf_op jit(solution)/shard_map/ppermute | solution.py:244
  20.7 3.7 %collective-permute-start.9 = (f32[8,256]{1,0:T(8,128)S(1)}, f32[8,256]{1,0:T(8,128)S(1)}, u32[]{:S(2)}, u32[]{:S(2)}) collective-permute-start(f32[8,256]{1,0:T(8,128)S(1)} %get-tuple-element.34.refs_0_), channel_id=1, source_target_pairs={{0,2},{1,3},{2,0},{3,1},{4,6},{5,7},{6,4},{7,5},{8,10},{9,11},{10,... | collective-permute-start | bytes 24584 | tf_op jit(solution)/shard_map/ppermute | solution.py:244
